TPU v7x, 32 devices: a whole 2x2x4 slice. The times are simulated.
32 devices in a mesh: groups: 2 (over y), tile: 4 (over z), sect: 4 (over x, core).
Axes of the slice: x: 2, y: 2, z: 4, core: 2. Of those that a mesh axis runs over, the one named last changes fastest.
Arguments:
- labels: int32 [16, 128, 512], P(('groups', 'sect'), None, 'tile'), parts along dimension 0, may hold values from 0 to 15
- classes: int32 [16, 128, 512], P(('groups', 'sect'), None, 'tile'), parts along dimension 0, may hold values from 0 to 7
- positions: int32 [8], P('groups'), parts along dimension 0, may hold values from 0 to 127
- phase_table: float32 [8], replicated, may hold values from -3.140625 to 3.140625
- brightness: float32 [16], replicated, may hold values from 0.2 to 2
- prop_taps: float32 [2, 2, 129], replicated, may hold values from -1 to 1, as said below
- detect_taps: float32 [2, 129], replicated, may hold values from 0 to 1, as said below
Outputs:
- image: float32 [16, 128, 512], P(('groups', 'sect'), None, 'tile'), parts along dimension 0
There are 2 independent parts, one for each index of `groups`. A program takes and returns all parts, laid end to end along the dimension named above; an argument that names none is the same for every part. Nothing has to cross between parts.
Inputs may be any that keep to these rules, and one draw needn't show every extreme that they name: `prop_taps`: the squares of the 2 x 129 entries of each axis's propagation taps sum to 1. `detect_taps`: each axis's detection taps are positive and sum to 1.
All inputs are finite; a program needn't handle non-finite values.
Results may differ from a plain program's by a relative error of at most 0.0001.
Values sent between devices are 32-bit elements; how exact they have to be, the bound alone decides.
No kernel may reach another device: no remote copies, remote signals or barrier semaphores. Data moves between devices by JAX's collectives and lax.ppermute only.
A program may use at most 64 MiB of HBM per device.

v0:
```python
import jax
import jax.numpy as jnp
from jax import lax
from jax.sharding import PartitionSpec as P

SHEET_WIDTH = 6.0
AMPLITUDE = 2.0


def padded_2(x, sides, width):
    for axis, dim in sides:
        count, length = (lax.axis_size(axis), x.shape[dim])
        up = [(i, (i + 1) % count) for i in range(count - 1)]
        down = [(j, i) for i, j in up]
        last = lax.slice_in_dim(x, length - width, length, axis=dim)
        first = lax.slice_in_dim(x, 0, width, axis=dim)
        before = lax.ppermute(last, axis, up)
        after = lax.ppermute(first, axis, down)
        x = jnp.concatenate([before, x, after], axis=dim)
    return x


def toeplitz(tap_rows, size_in, size_out, shift, period):
    count = tap_rows.shape[-1]
    inner = lax.broadcasted_iota(jnp.int32, (size_in, size_out), 0)
    outer = lax.broadcasted_iota(jnp.int32, (size_in, size_out), 1)
    offset = inner - outer + shift
    if period > 0:
        tap_place = lax.broadcasted_iota(jnp.int32, (count, period), 0)
        target = lax.broadcasted_iota(jnp.int32, (count, period), 1)
        folding = (jnp.mod(tap_place, period) == target).astype(tap_rows.dtype)
        table = jnp.einsum("...t,tj->...j", tap_rows, folding, precision=lax.Precision.HIGHEST)
        index = jnp.mod(offset, period)
        return jnp.take(table, index, axis=-1)
    index = jnp.clip(offset, 0, count - 1)
    valid = (offset >= 0) & (offset < count)
    values = jnp.take(tap_rows, index, axis=-1)
    return jnp.where(valid, values, jnp.zeros_like(values))


def complex_block(parts):
    real_part, imag_part = (parts[0], parts[1])
    return jnp.stack([jnp.stack([real_part, imag_part]), jnp.stack([-imag_part, real_part])])


def lookup(indices, table):
    total = jnp.zeros(indices.shape, jnp.float32)
    for entry in range(table.shape[0]):
        total = total + jnp.where(indices == entry, table[entry], 0.0)
    return total


def sheet_plane(position, y_cells, z_cells):
    place = lax.broadcasted_iota(jnp.int32, (y_cells, z_cells), 0).astype(jnp.float32)
    offset = (place - position.astype(jnp.float32)) / SHEET_WIDTH
    real_part = AMPLITUDE * jnp.exp(-offset * offset)
    return jnp.stack([real_part, jnp.zeros_like(real_part)])


def apply_phase(field, cosine, sine):
    real_part = field[..., 0, :, :]
    imag_part = field[..., 1, :, :]
    return jnp.stack(
        [real_part * cosine - imag_part * sine, real_part * sine + imag_part * cosine], axis=-3
    )


def along_y(field, y_band):
    return jnp.einsum(
        "cdio,...ciz->...doz",
        y_band,
        field,
        precision=lax.Precision.HIGHEST,
        preferred_element_type=jnp.float32,
    )


def along_z(field, z_band):
    return jnp.einsum(
        "...cyi,cdio->...dyo",
        field,
        z_band,
        precision=lax.Precision.HIGHEST,
        preferred_element_type=jnp.float32,
    )


def pick_entry(values, index):
    return jnp.sum(jnp.where(lax.iota(jnp.int32, values.shape[0]) == index, values, 0))


def beam_maps(maps, left_x, right_x):
    return jnp.stack(
        [
            lax.dynamic_index_in_dim(maps, left_x, 0, keepdims=False),
            lax.dynamic_index_in_dim(maps, right_x, 0, keepdims=False),
        ]
    )


def deposit(collected, field, weights, left_x, right_x):
    energy = field[:, 0] * field[:, 0] + field[:, 1] * field[:, 1]
    left_row = (
        lax.dynamic_index_in_dim(collected, left_x, 0, keepdims=False) + weights[0] * energy[0]
    )
    collected = lax.dynamic_update_index_in_dim(collected, left_row, left_x, 0)
    right_row = (
        lax.dynamic_index_in_dim(collected, right_x, 0, keepdims=False) + weights[1] * energy[1]
    )
    return lax.dynamic_update_index_in_dim(collected, right_row, right_x, 0)


def phase_maps(cosine, sine):
    return (cosine, sine, cosine, sine, None)


def run_slices(field, collected, maps, weights, x_cells, y_band, z_band, half_taps):
    cosine, sine, cos_wide, sin_wide, wide_band = maps
    last_x = x_cells - 1

    def slice_step(index, inner):
        beam_pair, gathered = inner
        right_x = last_x - index
        beam_pair = apply_phase(
            beam_pair, beam_maps(cosine, index, right_x), beam_maps(sine, index, right_x)
        )
        beam_pair = along_y(beam_pair, y_band)
        padded = padded_2(beam_pair, (("tile", 3),), half_taps)
        beam_pair = along_z(padded, z_band)
        return (beam_pair, deposit(gathered, beam_pair, weights, index, right_x))

    return lax.fori_loop(0, x_cells, slice_step, (field, collected))


def on_device(labels, classes, positions, phase_table, brightness, prop_taps, detect_taps):
    x_cells, y_cells, z_cells = labels.shape
    half_taps = prop_taps.shape[-1] // 2
    sections = lax.axis_size("sect")
    section = lax.axis_index("sect")
    position_count = positions.shape[0]
    y_band = complex_block(toeplitz(prop_taps[0], y_cells, y_cells, half_taps, y_cells))
    z_band = complex_block(toeplitz(prop_taps[1], z_cells + 2 * half_taps, z_cells, 0, 0))

    def is_live(index):
        return ((index >= 0) & (index < position_count)).astype(jnp.float32)

    every_class = lax.all_gather(classes, "sect", axis=0, tiled=True)
    all_x = every_class.shape[0]
    maps = phase_maps(
        lookup(every_class, jnp.cos(phase_table)), lookup(every_class, jnp.sin(phase_table))
    )
    rounds = (position_count + sections - 1) // sections

    def round_step(number, totals):
        index = number * sections + section
        weight = is_live(index)
        weights = jnp.stack([weight, weight])
        start = sheet_plane(pick_entry(positions, index), y_cells, z_cells)
        field = jnp.stack([start, start])
        _, totals = run_slices(field, totals, maps, weights, all_x, y_band, z_band, half_taps)
        return totals

    totals = lax.fori_loop(0, rounds, round_step, jnp.zeros((all_x, y_cells, z_cells), jnp.float32))
    collected = lax.psum_scatter(totals, "sect", scatter_dimension=0, tiled=True)
    excitation = lookup(labels, brightness) * collected
    blur_y = toeplitz(detect_taps[0], y_cells, y_cells, half_taps, y_cells)
    blurred = jnp.einsum(
        "io,xiz->xoz",
        blur_y,
        excitation,
        precision=lax.Precision.HIGHEST,
        preferred_element_type=jnp.float32,
    )
    padded = padded_2(blurred, (("tile", 2),), half_taps)
    blur_z = toeplitz(detect_taps[1], z_cells + 2 * half_taps, z_cells, 0, 0)
    return jnp.einsum(
        "xyi,io->xyo",
        padded,
        blur_z,
        precision=lax.Precision.HIGHEST,
        preferred_element_type=jnp.float32,
    )


def solution(mesh):
    in_specs = (
        P(("groups", "sect"), None, "tile"),
        P(("groups", "sect"), None, "tile"),
        P("groups"),
        P(),
        P(),
        P(),
        P(),
    )
    out_specs = P(("groups", "sect"), None, "tile")
    return jax.shard_map(
        on_device, mesh=mesh, in_specs=in_specs, out_specs=out_specs, check_vma=False
    )
```

profile of v0, /device:TPU:0, one launch (start us, length us, event | category | flops | bytes accessed | tf_op | source)
XLA Modules:
  0.0 620.5 jit_solution(2362041293282826913)
XLA Ops:
  7.7 54.5 %gather_fusion = f32[16384,2]{1,0:T(8,128)} fusion(f32[2,128]{0,1:T(8,128)S(1)} %copy.67, s32[16384]{0:T(1024)S(1)} %fusion.89), kind=kCustom, calls=%fused_computation | custom fusion | bytes 327680 | tf_op jit(solution)/shard_map/jit(_take)/gather | solution.py:34
  62.2 5.2 copy.68
  68.5 108.5 %gather_fusion.1 = f32[32768,2]{1,0:T(8,128)} fusion(f32[2,129]{0,1:T(8,128)S(1)} %bitcast.168, s32[32768]{0:T(1024)S(1)} %fusion.27), kind=kCustom, calls=%fused_computation.1 | custom fusion | bytes 655360 | tf_op jit(solution)/shard_map/jit(_take)/gather | solution.py:37
  176.9 9.7 %copy.71 = f32[256,128,2]{1,0,2:T(8,128)S(1)} copy(f32[256,128,2]{2,1,0:T(8,128)} %bitcast.169) | data formatting | bytes 524288 | tf_op jit(solution)/shard_map/jit(_take)/gather | solution.py:37
  186.8 8.6 %all_gather.3 = s32[8,128,128]{2,1,0:T(8,128)S(1)} all-gather(s32[2,128,128]{2,1,0:T(8,128)S(1)} %copy-done.1), channel_id=1, replica_groups=mesh['groups'=2,'tile'=4,'sect'=4] {'sect'}, dimensions={0}, use_global_device_ids=true | all-gather | bytes 655360 | tf_op jit(solution)/shard_map/all_gather | solution.py:147
  196.1 5.8 select_add_fusion
  202.0 5.6 select_add_fusion.1
  209.6 84.3 %while.25 = (s32[]{:T(128)}, f32[2,2,128,128]{3,2,1,0:T(8,128)S(1)}, f32[8,128,128]{2,1,0:T(8,128)S(1)}, f32[8,128,128]{1,2,0:T(8,128)S(1)}, f32[8,128,128]{1,2,...) while((s32[]{:T(128)}, ...), condition=%wide.region_2.3_spmd, body=%wide.region_1.2_spmd.sunk | while | flops 604733440 | bytes 6291731 | solution.py:132
  211.6 4.6 collective-permute-start.1
  216.2 1.8 collective-permute-done
  222.1 5.0 collective-permute-start.1
  232.7 5.0 collective-permute-start.1
  243.2 5.0 collective-permute-start.1
  249.2 1.5 collective-permute-done.1
  253.8 5.0 collective-permute-start.1
  264.3 5.0 collective-permute-start.1
  274.8 5.0 collective-permute-start.1
  280.8 1.5 collective-permute-done.1
  285.3 5.0 collective-permute-start.1
  291.3 1.5 collective-permute-done.1
  295.0 97.2 %gather_fusion.2 = f32[16384]{0:T(1024)S(1)} fusion(f32[128]{0:T(128)S(1)} %convolution_bitcast_fusion.4, s32[16384]{0:T(1024)S(1)} %fusion.89), kind=kCustom, calls=%fused_computation.2 | custom fusion | bytes 196608 | tf_op jit(solution)/shard_map/jit(_take)/gather | solution.py:34
  393.0 11.4 %convolution_bitcast_fusion.2 = f32[2,128,128]{1,2,0:T(8,128)S(1)} fusion(f32[2,128,128]{2,1,0:T(8,128)} %reduce-scatter.2.cloned.1.call-done, s32[2,128,128]{2,1,0:T(8,128)S(1)} %copy-done.4, f32[16384]{0:T(1024)S(1)} %gather_fusion.2, f32[]{:T(128)} %bitcast.34, f32[]{:T(128)} %bitcast.33, f32[]{:T(128)} %bitcast.32, f32[]{:T(128)} %bitcast.31, ...), kind=kOutput, calls=%fused_computation.37 | convolution fusion | flops 52232192 | bytes 458816 | tf_op jit(solution)/shard_map/io,xiz->xoz/dot_general | solution.py:167
  404.4 4.4 collective-permute-start.2
  410.1 202.2 %gather_fusion.3 = f32[32768]{0:T(1024)S(1)} fusion(f32[129]{0:T(256)S(1)} %bitcast.167, s32[32768]{0:T(1024)S(1)} %fusion.27), kind=kCustom, calls=%fused_computation.3 | custom fusion | bytes 393216 | tf_op jit(solution)/shard_map/jit(_take)/gather | solution.py:37
  (147 shorter events, 46.3 us)
Async XLA Ops:
  6.5 180.2 %copy-start.5 = (f32[8]{0:T(128)S(1)}, f32[8]{0:T(128)}, u32[]{:S(2)}) copy-start(f32[8]{0:T(128)} %param.12) | copy-start | bytes 100
  6.5 180.2 %copy-start.1 = (s32[2,128,128]{2,1,0:T(8,128)S(1)}, s32[2,128,128]{2,1,0:T(8,128)}, u32[]{:S(2)}) copy-start(s32[2,128,128]{2,1,0:T(8,128)} %param.10) | copy-start | bytes 393220
  6.5 386.4 %reduce-scatter.2.cloned.1.call-start = ((), (), s32[]{:S(2)}) async-start(), calls=%async_computation.1 | async-start | bytes 655360 | tf_op jit(solution)/shard_map/reduce_scatter | solution.py:164
  62.2 145.8 %copy-start.6 = (s32[4]{0:T(128)S(1)}, s32[4]{0:T(128)}, u32[]{:S(2)}) copy-start(s32[4]{0:T(128)} %param.11) | copy-start | bytes 52
  210.3 7.6 %collective-permute-start = (f32[2,2,128,64]{2,3,1,0:T(8,128)S(1)}, f32[2,2,128,64]{2,3,1,0:T(8,128)S(1)}, u32[]{:S(2)}, u32[]{:S(2)}) collective-permute-start(f32[2,2,128,64]{2,3,1,0:T(8,128)S(1)} %get-tuple-element.399), channel_id=1, source_target_pairs={{4,0},{8,4},{12,8},{5,1},{9,5},{13,9},{6,2},{10,6},{14,10},{7,3},{... | collective-permute-start | bytes 393224 | tf_op jit(solution)/shard_map/while/body/eval_jaxpr/while/body/eval_jaxpr/ppermute | solution.py:18
  211.6 7.5 %collective-permute-start.1 = (f32[2,2,128,64]{2,3,1,0:T(8,128)S(1)}, f32[2,2,128,64]{2,3,1,0:T(8,128)S(1)}, u32[]{:S(2)}, u32[]{:S(2)}) collective-permute-start(f32[2,2,128,64]{2,3,1,0:T(8,128)S(1)} %get-tuple-element.400), channel_id=1, source_target_pairs={{0,4},{4,8},{8,12},{1,5},{5,9},{9,13},{2,6},{6,10},{10,14},{3,7},{... | collective-permute-start | bytes 393224 | tf_op jit(solution)/shard_map/while/body/eval_jaxpr/while/body/eval_jaxpr/ppermute | solution.py:17
  220.8 7.3 %collective-permute-start = (f32[2,2,128,64]{2,3,1,0:T(8,128)S(1)}, f32[2,2,128,64]{2,3,1,0:T(8,128)S(1)}, u32[]{:S(2)}, u32[]{:S(2)}) collective-permute-start(f32[2,2,128,64]{2,3,1,0:T(8,128)S(1)} %get-tuple-element.399), channel_id=1, source_target_pairs={{4,0},{8,4},{12,8},{5,1},{9,5},{13,9},{6,2},{10,6},{14,10},{7,3},{... | collective-permute-start | bytes 393224 | tf_op jit(solution)/shard_map/while/body/eval_jaxpr/while/body/eval_jaxpr/ppermute | solution.py:18
  222.1 7.5 %collective-permute-start.1 = (f32[2,2,128,64]{2,3,1,0:T(8,128)S(1)}, f32[2,2,128,64]{2,3,1,0:T(8,128)S(1)}, u32[]{:S(2)}, u32[]{:S(2)}) collective-permute-start(f32[2,2,128,64]{2,3,1,0:T(8,128)S(1)} %get-tuple-element.400), channel_id=1, source_target_pairs={{0,4},{4,8},{8,12},{1,5},{5,9},{9,13},{2,6},{6,10},{10,14},{3,7},{... | collective-permute-start | bytes 393224 | tf_op jit(solution)/shard_map/while/body/eval_jaxpr/while/body/eval_jaxpr/ppermute | solution.py:17
  231.4 7.3 %collective-permute-start = (f32[2,2,128,64]{2,3,1,0:T(8,128)S(1)}, f32[2,2,128,64]{2,3,1,0:T(8,128)S(1)}, u32[]{:S(2)}, u32[]{:S(2)}) collective-permute-start(f32[2,2,128,64]{2,3,1,0:T(8,128)S(1)} %get-tuple-element.399), channel_id=1, source_target_pairs={{4,0},{8,4},{12,8},{5,1},{9,5},{13,9},{6,2},{10,6},{14,10},{7,3},{... | collective-permute-start | bytes 393224 | tf_op jit(solution)/shard_map/while/body/eval_jaxpr/while/body/eval_jaxpr/ppermute | solution.py:18
  232.7 7.5 %collective-permute-start.1 = (f32[2,2,128,64]{2,3,1,0:T(8,128)S(1)}, f32[2,2,128,64]{2,3,1,0:T(8,128)S(1)}, u32[]{:S(2)}, u32[]{:S(2)}) collective-permute-start(f32[2,2,128,64]{2,3,1,0:T(8,128)S(1)} %get-tuple-element.400), channel_id=1, source_target_pairs={{0,4},{4,8},{8,12},{1,5},{5,9},{9,13},{2,6},{6,10},{10,14},{3,7},{... | collective-permute-start | bytes 393224 | tf_op jit(solution)/shard_map/while/body/eval_jaxpr/while/body/eval_jaxpr/ppermute | solution.py:17
  241.9 7.3 %collective-permute-start = (f32[2,2,128,64]{2,3,1,0:T(8,128)S(1)}, f32[2,2,128,64]{2,3,1,0:T(8,128)S(1)}, u32[]{:S(2)}, u32[]{:S(2)}) collective-permute-start(f32[2,2,128,64]{2,3,1,0:T(8,128)S(1)} %get-tuple-element.399), channel_id=1, source_target_pairs={{4,0},{8,4},{12,8},{5,1},{9,5},{13,9},{6,2},{10,6},{14,10},{7,3},{... | collective-permute-start | bytes 393224 | tf_op jit(solution)/shard_map/while/body/eval_jaxpr/while/body/eval_jaxpr/ppermute | solution.py:18
  243.2 7.5 %collective-permute-start.1 = (f32[2,2,128,64]{2,3,1,0:T(8,128)S(1)}, f32[2,2,128,64]{2,3,1,0:T(8,128)S(1)}, u32[]{:S(2)}, u32[]{:S(2)}) collective-permute-start(f32[2,2,128,64]{2,3,1,0:T(8,128)S(1)} %get-tuple-element.400), channel_id=1, source_target_pairs={{0,4},{4,8},{8,12},{1,5},{5,9},{9,13},{2,6},{6,10},{10,14},{3,7},{... | collective-permute-start | bytes 393224 | tf_op jit(solution)/shard_map/while/body/eval_jaxpr/while/body/eval_jaxpr/ppermute | solution.py:17
  252.5 7.3 %collective-permute-start = (f32[2,2,128,64]{2,3,1,0:T(8,128)S(1)}, f32[2,2,128,64]{2,3,1,0:T(8,128)S(1)}, u32[]{:S(2)}, u32[]{:S(2)}) collective-permute-start(f32[2,2,128,64]{2,3,1,0:T(8,128)S(1)} %get-tuple-element.399), channel_id=1, source_target_pairs={{4,0},{8,4},{12,8},{5,1},{9,5},{13,9},{6,2},{10,6},{14,10},{7,3},{... | collective-permute-start | bytes 393224 | tf_op jit(solution)/shard_map/while/body/eval_jaxpr/while/body/eval_jaxpr/ppermute | solution.py:18
  253.8 7.5 %collective-permute-start.1 = (f32[2,2,128,64]{2,3,1,0:T(8,128)S(1)}, f32[2,2,128,64]{2,3,1,0:T(8,128)S(1)}, u32[]{:S(2)}, u32[]{:S(2)}) collective-permute-start(f32[2,2,128,64]{2,3,1,0:T(8,128)S(1)} %get-tuple-element.400), channel_id=1, source_target_pairs={{0,4},{4,8},{8,12},{1,5},{5,9},{9,13},{2,6},{6,10},{10,14},{3,7},{... | collective-permute-start | bytes 393224 | tf_op jit(solution)/shard_map/while/body/eval_jaxpr/while/body/eval_jaxpr/ppermute | solution.py:17
  263.0 7.3 %collective-permute-start = (f32[2,2,128,64]{2,3,1,0:T(8,128)S(1)}, f32[2,2,128,64]{2,3,1,0:T(8,128)S(1)}, u32[]{:S(2)}, u32[]{:S(2)}) collective-permute-start(f32[2,2,128,64]{2,3,1,0:T(8,128)S(1)} %get-tuple-element.399), channel_id=1, source_target_pairs={{4,0},{8,4},{12,8},{5,1},{9,5},{13,9},{6,2},{10,6},{14,10},{7,3},{... | collective-permute-start | bytes 393224 | tf_op jit(solution)/shard_map/while/body/eval_jaxpr/while/body/eval_jaxpr/ppermute | solution.py:18
  264.3 7.5 %collective-permute-start.1 = (f32[2,2,128,64]{2,3,1,0:T(8,128)S(1)}, f32[2,2,128,64]{2,3,1,0:T(8,128)S(1)}, u32[]{:S(2)}, u32[]{:S(2)}) collective-permute-start(f32[2,2,128,64]{2,3,1,0:T(8,128)S(1)} %get-tuple-element.400), channel_id=1, source_target_pairs={{0,4},{4,8},{8,12},{1,5},{5,9},{9,13},{2,6},{6,10},{10,14},{3,7},{... | collective-permute-start | bytes 393224 | tf_op jit(solution)/shard_map/while/body/eval_jaxpr/while/body/eval_jaxpr/ppermute | solution.py:17
  273.5 7.3 %collective-permute-start = (f32[2,2,128,64]{2,3,1,0:T(8,128)S(1)}, f32[2,2,128,64]{2,3,1,0:T(8,128)S(1)}, u32[]{:S(2)}, u32[]{:S(2)}) collective-permute-start(f32[2,2,128,64]{2,3,1,0:T(8,128)S(1)} %get-tuple-element.399), channel_id=1, source_target_pairs={{4,0},{8,4},{12,8},{5,1},{9,5},{13,9},{6,2},{10,6},{14,10},{7,3},{... | collective-permute-start | bytes 393224 | tf_op jit(solution)/shard_map/while/body/eval_jaxpr/while/body/eval_jaxpr/ppermute | solution.py:18
  274.8 7.5 %collective-permute-start.1 = (f32[2,2,128,64]{2,3,1,0:T(8,128)S(1)}, f32[2,2,128,64]{2,3,1,0:T(8,128)S(1)}, u32[]{:S(2)}, u32[]{:S(2)}) collective-permute-start(f32[2,2,128,64]{2,3,1,0:T(8,128)S(1)} %get-tuple-element.400), channel_id=1, source_target_pairs={{0,4},{4,8},{8,12},{1,5},{5,9},{9,13},{2,6},{6,10},{10,14},{3,7},{... | collective-permute-start | bytes 393224 | tf_op jit(solution)/shard_map/while/body/eval_jaxpr/while/body/eval_jaxpr/ppermute | solution.py:17
  284.0 7.3 %collective-permute-start = (f32[2,2,128,64]{2,3,1,0:T(8,128)S(1)}, f32[2,2,128,64]{2,3,1,0:T(8,128)S(1)}, u32[]{:S(2)}, u32[]{:S(2)}) collective-permute-start(f32[2,2,128,64]{2,3,1,0:T(8,128)S(1)} %get-tuple-element.399), channel_id=1, source_target_pairs={{4,0},{8,4},{12,8},{5,1},{9,5},{13,9},{6,2},{10,6},{14,10},{7,3},{... | collective-permute-start | bytes 393224 | tf_op jit(solution)/shard_map/while/body/eval_jaxpr/while/body/eval_jaxpr/ppermute | solution.py:18
  285.3 7.5 %collective-permute-start.1 = (f32[2,2,128,64]{2,3,1,0:T(8,128)S(1)}, f32[2,2,128,64]{2,3,1,0:T(8,128)S(1)}, u32[]{:S(2)}, u32[]{:S(2)}) collective-permute-start(f32[2,2,128,64]{2,3,1,0:T(8,128)S(1)} %get-tuple-element.400), channel_id=1, source_target_pairs={{0,4},{4,8},{8,12},{1,5},{5,9},{9,13},{2,6},{6,10},{10,14},{3,7},{... | collective-permute-start | bytes 393224 | tf_op jit(solution)/shard_map/while/body/eval_jaxpr/while/body/eval_jaxpr/ppermute | solution.py:17
  295.0 97.2 %copy-start.2 = (f32[16]{0:T(128)S(1)}, f32[16]{0:T(128)}, u32[]{:S(2)}) copy-start(f32[16]{0:T(128)} %param.13) | copy-start | bytes 196
  295.0 98.0 %copy-start.4 = (s32[2,128,128]{2,1,0:T(8,128)S(1)}, s32[2,128,128]{2,1,0:T(8,128)}, u32[]{:S(2)}) copy-start(s32[2,128,128]{2,1,0:T(8,128)} %param.9) | copy-start | bytes 393220
  404.4 207.9 %collective-permute-start.2 = (f32[2,128,64]{1,2,0:T(8,128)S(1)}, f32[2,128,64]{1,2,0:T(8,128)S(1)}, u32[]{:S(2)}, u32[]{:S(2)}) collective-permute-start(f32[2,128,64]{1,2,0:T(8,128)S(1)} %get-tuple-element.286), channel_id=1, source_target_pairs={{0,4},{4,8},{8,12},{1,5},{5,9},{9,13},{2,6},{6,10},{10,14},{3,7},{... | collective-permute-start | bytes 196616 | tf_op jit(solution)/shard_map/ppermute | solution.py:17
  408.8 203.6 %collective-permute-start.3 = (f32[2,128,64]{1,2,0:T(8,128)S(1)}, f32[2,128,64]{1,2,0:T(8,128)S(1)}, u32[]{:S(2)}, u32[]{:S(2)}) collective-permute-start(f32[2,128,64]{1,2,0:T(8,128)S(1)} %get-tuple-element.287), channel_id=1, source_target_pairs={{4,0},{8,4},{12,8},{5,1},{9,5},{13,9},{6,2},{10,6},{14,10},{7,3},{... | collective-permute-start | bytes 196616 | tf_op jit(solution)/shard_map/ppermute | solution.py:18
  (2 other events, 88.0 us)
Sparse Core Ops, SparseCore 0:
  294.9 24.2 reduce-scatter.1
where the time goes:
time: 622 us; the launch traced here: 620 us
  local copies, waits for them, and re-layouts  482 us (77%)
  starting transfers between devices  55.5 us (9%)
  matrix products  24.9 us (4%)
  waiting for transfers between devices  20.5 us (3%)
  between operations  14.4 us (2%)
  other arithmetic  13.3 us (2%)
  blocking collectives  8.62 us (1%)
    gather x3, local copies, waits for them, and re-layouts, toeplitz(): values = jnp.take(tap_rows, index, axis=-1)  320 us
    gather x3, local copies, waits for them, and re-layouts, toeplitz(): return jnp.take(table, index, axis=-1)  157 us
    ppermute x9, starting transfers between devices, padded_2(): before = lax.ppermute(last, axis, up)  43.8 us
  transfers between devices with their start and end apart: 19, of which 16 were waited for; matrix products, arithmetic and copies ran while one was open for 48% of the time, Pallas kernels for 0%

commit v1 on v0

v1 whole, which is shorter than its diff:
```python
import functools

import jax
import jax.numpy as jnp
from jax import lax
from jax.experimental import pallas as pl
from jax.experimental.pallas import tpu as pltpu
from jax.sharding import PartitionSpec as P

SHEET_WIDTH = 6.0
AMPLITUDE = 2.0
VMEM_BYTES = 48 * 1024 * 1024
SMEM = pltpu.SMEM
VMEM = pltpu.VMEM


class Plan:
    def __init__(self, labels, positions, taps):
        self.planes, self.ny, self.cz = labels.shape
        self.half = taps // 2
        self.taps = taps
        self.tiles = lax.axis_size("tile")
        self.sections = lax.axis_size("sect")
        self.tile = lax.axis_index("tile")
        self.sect = lax.axis_index("sect")
        self.cores = self.sections // 2
        self.core = self.sect % self.cores
        self.side = self.sect // self.cores
        self.own = self.cores * self.planes
        self.all_x = 2 * self.own
        self.sheets = -(-positions // self.cores)
        self.block = 2 * self.half
        self.units = self.cz // self.half
        self.reach = -(-(self.all_x + 1) * self.half // self.cz)
        self.whole = self.tiles <= 2 * self.reach + 1
        self.window = self.tiles if self.whole else 2 * self.reach + 1
        self.rows = self.window * self.cz
        self.extent = self.cz + 2 * self.half

    def span(self, left):
        need = self.units + 2 + 2 * left
        if self.whole:
            width = min(need, self.window * self.units)
            start = jnp.clip(self.tile * self.units - 1 - left, 0, self.window * self.units - width)
        else:
            width = need
            start = jnp.int32(self.reach * self.units - 1 - left)
        return start, width // 2

    def home(self):
        if self.whole:
            return self.tile * self.cz
        return jnp.int32(self.reach * self.cz)


def swap(x, axis, bits):
    count = lax.axis_size(axis)
    return lax.ppermute(x, axis, [(i, i ^ bits) for i in range(count)])


def shift(x, axis, step):
    count = lax.axis_size(axis)
    return lax.ppermute(x, axis, [(i, i + step) for i in range(count) if 0 <= i + step < count])


def tile_pieces(plan, mine):
    one = jnp.int32(1)
    if plan.whole and plan.tiles & (plan.tiles - 1) == 0:
        got = {0: mine}
        if plan.tiles == 4:
            got[3] = swap(mine, "tile", 3)
            got[1] = swap(mine, "tile", 1)
            got[2] = swap(got[3], "tile", 1)
        else:
            for bits in range(1, plan.tiles):
                got[bits] = swap(mine, "tile", bits)
        return [(got[bits], plan.tile ^ bits, one) for bits in sorted(got)]
    if plan.whole:
        count = plan.tiles
        pieces = [(mine, plan.tile, one)]
        for step in range(1, count):
            turned = lax.ppermute(mine, "tile", [(i, (i + step) % count) for i in range(count)])
            pieces.append((turned, (plan.tile - step) % count, one))
        return pieces
    pieces = []
    for step in range(-plan.reach, plan.reach + 1):
        source = plan.tile + step
        valid = ((source >= 0) & (source < plan.tiles)).astype(jnp.int32)
        piece = mine if step == 0 else shift(mine, "tile", -step)
        pieces.append((piece, jnp.int32(step + plan.reach), valid))
    return pieces


def halves(x):
    high = x.astype(jnp.bfloat16)
    return high, (x - high.astype(jnp.float32)).astype(jnp.bfloat16)


def dot(a, b):
    return jnp.dot(a, b, preferred_element_type=jnp.float32)


def three(high, low, matrix_high, matrix_low):
    return dot(high, matrix_high) + dot(low, matrix_high) + dot(high, matrix_low)


def circulant(row, size, half):
    wide = jnp.broadcast_to(row, (size, size))
    return pltpu.roll(wide, (size - half) % size, 1, stride=1, stride_axis=0).T


def band(row, size, wide):
    return pltpu.roll(jnp.broadcast_to(row, (size, wide)), 0, 1, stride=1, stride_axis=0)


def prepare_kernel(ny, half, taps, dtaps, ky, kz, by, bz, line):
    block = 2 * half
    wide = 4 * half
    count = taps.shape[2]

    def padded(row):
        line[...] = jnp.zeros(line.shape, jnp.float32)
        line[0:1, :count] = row
        return line[0:1, :]

    def folded(row):
        spread = padded(row)
        return sum(spread[:, i:i + ny] for i in range(0, spread.shape[1], ny))

    def keep(ref, matrix, place=()):
        ref[(0, *place)], ref[(1, *place)] = halves(matrix)

    cyr = circulant(folded(taps[0, 0:1, :]), ny, half)
    cyi = circulant(folded(taps[0, 1:2, :]), ny, half)
    keep(ky, complex_matrix(cyr, cyi, -cyi))
    czr = band(padded(taps[1, 0:1, :])[:, :wide], block, wide)
    czi = band(padded(taps[1, 1:2, :])[:, :wide], block, wide)
    early = complex_matrix(czr[:, :block], -czi[:, :block], czi[:, :block])
    late = complex_matrix(czr[:, block:], -czi[:, block:], czi[:, block:])
    for number, matrix in enumerate((early, early + late, late)):
        keep(kz, matrix, (number,))
    keep(by, circulant(folded(dtaps[0:1, :]), ny, half))
    keep(bz, band(padded(dtaps[1:2, :])[:, :wide], block, wide))


def complex_matrix(diagonal, upper, lower):
    top = jnp.concatenate([diagonal, upper], axis=1)
    return jnp.concatenate([top, jnp.concatenate([lower, diagonal], axis=1)], axis=0)


def fill_weight(half, before, after, even, bright, labels, near, far, weight):
    def bright_of(x):
        total = jnp.zeros(x.shape, jnp.float32)
        for entry in range(bright.shape[0]):
            total = jnp.where(x == entry, bright[entry], total)
        return total

    for plane in range(labels.shape[0]):
        one, two = near[plane], far[plane]
        left = jnp.where(even, two, one)
        right = jnp.where(even, one, two)
        weight[plane, :half, :] = (bright_of(left) * before).T
        weight[plane, half:half + labels.shape[2], :] = bright_of(labels[plane]).T
        weight[plane, half + labels.shape[2]:, :] = (bright_of(right) * after).T


def beams_kernel(plan, blocks, count, total, scal, positions, table, bright, ky, kz, *refs):
    pieces = refs[:count]
    if total > plan.own:
        earlier, labels, facing, beyond, out, weight, cosine, sine, field, spread = refs[count:]
        before, after = scal[2].astype(jnp.float32), scal[3].astype(jnp.float32)
        fill_weight(plan.half, before, after, scal[4] == 0, bright, labels, facing, beyond, weight)
    else:
        out, cosine, sine, field, spread = refs[count:]
    ny, cz, half, block = plan.ny, plan.cz, plan.half, plan.block
    sheets, own, rows = plan.sheets, plan.own, plan.rows
    side = scal[0]
    home = pl.multiple_of(scal[1], half)
    first = scal.shape[0] - len(blocks)
    width = sheets * ny

    for number, piece in enumerate(pieces):
        where = scal[6 + 3 * number]
        row = pl.multiple_of(scal[7 + 3 * number] * cz, cz)
        valid = scal[8 + 3 * number] > 0
        for plane in range(plan.planes):
            kind = piece[plane].T
            bits = [(kind & 1) != 0, (kind & 2) != 0, (kind & 4) != 0]
            for part, target in ((0, cosine), (1, sine)):
                values = [jnp.where(valid, table[part, entry], 0.0) for entry in range(table.shape[1])]
                for bit in bits:
                    values = [
                        jnp.where(bit, values[i + 1], values[i]) for i in range(0, len(values), 2)
                    ]
                target[where + plane, pl.ds(row, cz), :] = values[0]

    lane = lax.broadcasted_iota(jnp.int32, (1, ny), 1).astype(jnp.float32)
    sheet = []
    for p in range(sheets):
        number = scal[5] * sheets + p
        live = number < positions.shape[0]
        centre = positions[jnp.where(live, number, 0)].astype(jnp.float32)
        offset = (lane - centre) / SHEET_WIDTH
        sheet.append(jnp.where(live, AMPLITUDE, 0.0) * jnp.exp(-offset * offset))
    field[0, half:half + rows, :] = jnp.broadcast_to(jnp.concatenate(sheet, axis=1), (rows, width))
    field[1, half:half + rows, :] = jnp.zeros((rows, width), jnp.float32)
    for ref in (field, spread):
        for d in range(2):
            ref[d, :half, :] = jnp.zeros((half, width), jnp.float32)
            ref[d, half + rows:, :] = jnp.zeros((half, width), jnp.float32)

    def each(number, body):
        if plan.whole:
            for b in range(number):
                body(b)
        else:
            lax.fori_loop(0, number, lambda b, _: body(b), None)

    def advance(slot, left, sources, targets):
        source = scal[first + left + 1] * half
        target = scal[first + left] * half

        def turn(b):
            row = pl.multiple_of(source + b * block, half)
            cos, sin = cosine[slot, pl.ds(row, block), :], sine[slot, pl.ds(row, block), :]
            parts = []
            for p in range(sheets):
                lanes = slice(p * ny, (p + 1) * ny)
                re = field[0, pl.ds(row + half, block), lanes]
                im = field[1, pl.ds(row + half, block), lanes]
                parts.append(jnp.concatenate([re * cos - im * sin, re * sin + im * cos], axis=1))
            high, low = halves(jnp.concatenate(parts, axis=0))
            v = three(high, low, ky[0], ky[1])
            for d in range(2):
                spread[d, pl.ds(row + half, block), :] = jnp.concatenate(
                    [v[p * block:(p + 1) * block, d * ny:(d + 1) * ny] for p in range(sheets)], axis=1
                )

        def product(number, x):
            high, low = halves(x)
            return dot(kz[0, number], high) + dot(kz[1, number], high) + dot(kz[0, number], low)

        def window(row):
            return jnp.concatenate([spread[d, pl.ds(row, block), :] for d in range(2)], axis=0)

        def store(row, w):
            field[0, pl.ds(row + half, block), :] = w[:block]
            field[1, pl.ds(row + half, block), :] = w[block:]

        def pair(b):
            row = pl.multiple_of(target + 2 * b * block, half)
            x = [window(row + i * block) for i in range(3)]
            middle = product(1, x[1])
            store(row, product(0, x[0] - x[1]) + middle)
            store(row + block, product(2, x[2] - x[1]) + middle)

        def single(b):
            row = pl.multiple_of(target + b * block, half)
            store(row, product(0, window(row)) + product(2, window(row + block)))

        each(sources, turn)
        each(targets // 2, pair)
        if targets % 2:
            single(targets - 1)

    def deposit(slot):
        re = field[0, pl.ds(home, plan.extent), :]
        im = field[1, pl.ds(home, plan.extent), :]
        energy = re * re + im * im
        gathered = energy[:, :ny]
        for p in range(1, sheets):
            gathered = gathered + energy[:, p * ny:(p + 1) * ny]
        out[slot] = earlier[slot] + gathered if total > own else gathered

    forward = (side == 0) if total == own else (side != 0)

    def step(k, sources, targets):
        inner = k % own
        slot = jnp.where(forward, inner, own - 1 - inner)
        left = total - 1 - k
        near = k >= total - own
        advance(slot + jnp.where(near, 0, own), left, sources, targets)

        @pl.when(near)
        def _():
            deposit(slot)

    k = 0
    while k < total:
        shape = (blocks[total - k], blocks[total - 1 - k])
        end = k + 1
        while end < total and (blocks[total - end], blocks[total - 1 - end]) == shape:
            end += 1
        lax.fori_loop(k, end, lambda i, _: step(i, *shape), None)
        k = end


def blur_kernel(half, mine, other, weight, by, bz, out):
    planes, extent, ny = mine.shape
    parts = [(mine[x] + other[x]) * weight[x] for x in range(planes)]
    high, low = halves(jnp.concatenate(parts, axis=0))
    v = three(high, low, by[0], by[1])
    v = jnp.concatenate([v[x * extent:(x + 1) * extent] for x in range(planes)], axis=1)
    high, low = halves(v)
    block = 2 * half
    for b in range(out.shape[2] // block):
        rows = slice(b * block, b * block + 2 * block)
        w = dot(bz[0], high[rows]) + dot(bz[1], high[rows]) + dot(bz[0], low[rows])
        for x in range(planes):
            out[x, :, b * block:(b + 1) * block] = w[:, x * ny:(x + 1) * ny].T


def call(kernel, outs, in_spaces, scratch=(), flops=0):
    return pl.pallas_call(
        kernel,
        out_shape=outs,
        in_specs=[pl.BlockSpec(memory_space=space) for space in in_spaces],
        out_specs=jax.tree.map(lambda _: pl.BlockSpec(memory_space=VMEM), outs),
        scratch_shapes=list(scratch),
        compiler_params=pltpu.CompilerParams(vmem_limit_bytes=VMEM_BYTES),
        cost_estimate=pl.CostEstimate(flops=flops, bytes_accessed=1 << 20, transcendentals=0),
    )


def on_device(labels, classes, positions, phase_table, brightness, prop_taps, detect_taps):
    taps = prop_taps.shape[-1]
    plan = Plan(labels, positions.shape[0], taps)
    ny, half, block, cz = plan.ny, plan.half, plan.block, plan.cz
    f32, bf16 = jnp.float32, jnp.bfloat16
    tile, tiles = plan.tile, plan.tiles

    pieces = tile_pieces(plan, classes)
    far = [(swap(a, "sect", plan.cores), block_, ok) for a, block_, ok in pieces]

    def spread_over_cores(group, base):
        arrays, scalars = [], []
        for array, place, ok in group:
            for bits in range(plan.cores):
                arrays.append(array if bits == 0 else swap(array, "sect", bits))
                scalars += [base + (plan.core ^ bits) * plan.planes, place, ok]
        return arrays, scalars

    near_arrays, near_scalars = spread_over_cores(pieces, 0)
    far_arrays, far_scalars = spread_over_cores(far, plan.own)

    line = -(-max(4 * half, taps) // ny) * ny
    ky, kz, by, bz = call(
        functools.partial(prepare_kernel, ny, half),
        (
            jax.ShapeDtypeStruct((2, 2 * ny, 2 * ny), bf16),
            jax.ShapeDtypeStruct((2, 3, 2 * block, 2 * block), bf16),
            jax.ShapeDtypeStruct((2, ny, ny), bf16),
            jax.ShapeDtypeStruct((2, block, 2 * block), bf16),
        ),
        [VMEM] * 2,
        [pltpu.VMEM((8, line), f32)],
    )(prop_taps, detect_taps)

    table = jnp.stack([jnp.cos(phase_table), jnp.sin(phase_table)])
    size = 1 << (table.shape[1] - 1).bit_length()
    table = jnp.pad(table, [(0, 0), (0, size - table.shape[1])])
    spans = [plan.span(left) for left in range(plan.all_x + 1)]
    blocks = tuple(n for _, n in spans)
    width = plan.sheets * ny
    rows = plan.rows
    at = [plan.side, plan.home(), tile > 0, tile < tiles - 1, tile % 2, plan.core]

    def sweep(total, arrays, scalars, outs, *more):
        scal = at + scalars + [s for s, _ in spans[:total + 1]]
        scal = jnp.stack([jnp.asarray(s, jnp.int32) for s in scal])
        return call(
            functools.partial(beams_kernel, plan, blocks[:total + 1], len(arrays), total),
            outs,
            [SMEM] * 4 + [VMEM] * (2 + len(arrays) + len(more)),
            [
                pltpu.VMEM((total, rows, ny), f32),
                pltpu.VMEM((total, rows, ny), f32),
                pltpu.VMEM((2, rows + 2 * half, width), f32),
                pltpu.VMEM((2, rows + 2 * half, width), f32),
            ],
            flops=total * 6 * 10**8,
        )(scal, positions, table, brightness, ky, kz, *arrays, *more)

    even = tile % 2 == 0
    late, _ = lax.optimization_barrier((labels, pieces[-1][0]))
    first, last = late[..., :half], late[..., cz - half:]
    pairs = [(i, i ^ 1) for i in range(tiles) if i ^ 1 < tiles]
    gaps = [(i, ((i + 1) ^ 1) - 1) for i in range(1, tiles) if ((i + 1) ^ 1) - 1 < tiles]
    facing = lax.ppermute(jnp.where(even, last, first), "tile", pairs)
    beyond = lax.ppermute(jnp.where(even, first, last), "tile", gaps)

    sums = jax.ShapeDtypeStruct((plan.own, plan.extent, ny), f32)
    weights = jax.ShapeDtypeStruct((plan.planes, plan.extent, ny), f32)
    collected = sweep(plan.own, near_arrays, near_scalars, sums)
    collected, weight = sweep(
        2 * plan.own, near_arrays + far_arrays, near_scalars + far_scalars, (sums, weights),
        collected, labels, facing, beyond,
    )

    parts = collected.reshape(plan.cores, plan.planes, plan.extent, ny)
    mine = lax.dynamic_index_in_dim(parts, plan.core, 0, keepdims=False)
    other = jnp.zeros_like(mine)
    for bits in range(1, plan.cores):
        leaving = lax.dynamic_index_in_dim(parts, plan.core ^ bits, 0, keepdims=False)
        other = other + swap(leaving, "sect", bits) if bits > 1 else swap(leaving, "sect", bits)
    return call(
        functools.partial(blur_kernel, half),
        jax.ShapeDtypeStruct((plan.planes, ny, cz), f32),
        [VMEM] * 5,
    )(mine, other, weight, by, bz)


def solution(mesh):
    spread = P(("groups", "sect"), None, "tile")
    in_specs = (spread, spread, P("groups"), P(), P(), P(), P())
    return jax.shard_map(
        on_device, mesh=mesh, in_specs=in_specs, out_specs=spread, check_vma=False
    )
```

time: 622 us -> 52.4 us (0.08)
  local copies, waits for them, and re-layouts: 482 us -> 1.7 us
  starting transfers between devices: 55.5 us -> 18.9 us
  matrix products: 24.9 us -> 0 us
  Pallas kernels: 0 us -> 24 us
  waiting for transfers between devices: 20.5 us -> 5.43 us
  between operations: 14.4 us -> 0.26 us
  other arithmetic: 13.3 us -> 1.11 us
  blocking collectives: 8.62 us -> 0 us
    gather x6 -> x0, local copies, waits for them, and re-layouts: 477 us -> none  [the longest x3 320 us: toeplitz(): values = jnp.take(tap_rows, index, axis=-1)]
    ppermute x18, starting transfers between devices: 55.5 us -> 18.9 us  [the longest x16 12.4 us: swap(): return lax.ppermute(x, axis, [(i, i ^ bits) for i in range(count)])]
    dot_general x20 -> x0, matrix products: 24.9 us -> none  [the longest x1 11.4 us: on_device(): jnp.einsum('io,xiz->xoz', blur_y, excitation, precision=lax.Precision.HIG...]
    pallas_call x0 -> x4, Pallas kernels: none -> 24 us  [the longest x2 22.3 us: sweep(): call(functools.partial(beams_kernel, plan, blocks[:total + 1], len(arrays...]
    ppermute x18, waiting for transfers between devices: 20.4 us -> 5.43 us  [the longest x16 5.42 us: swap(): return lax.ppermute(x, axis, [(i, i ^ bits) for i in range(count)])]
    add x10 -> x0, other arithmetic: 11.6 us -> none  [the longest x2 11.4 us: lookup(): total = total + jnp.where(indices == entry, table[entry], 0.0)]
    all_gather x1 -> x0, blocking collectives: 8.62 us -> none  [on_device(): every_class = lax.all_gather(classes, 'sect', axis=0, tiled=True)]
  transfers between devices with their start and end apart: 19 -> 18, of which waited for: 16 -> 3; matrix products, arithmetic and copies ran while one was open for 48% -> 3% of each run, Pallas kernels for 0% -> 15%
where the time goes in v1:
time: 52.4 us; the launch traced here: 51.4 us
  Pallas kernels  24 us (46%)
  starting transfers between devices  18.9 us (36%)
  waiting for transfers between devices  5.43 us (10%)
  local copies, waits for them, and re-layouts  1.7 us (3%)
  other arithmetic  1.11 us (2%)
    pallas_call x2, Pallas kernels, sweep(): call(functools.partial(beams_kernel, plan, blocks[:total + 1], len(arrays...  22.3 us
    ppermute x16, starting transfers between devices, swap(): return lax.ppermute(x, axis, [(i, i ^ bits) for i in range(count)])  12.4 us
    ppermute x1, starting transfers between devices, on_device(): facing = lax.ppermute(jnp.where(even, last, first), 'tile', pairs)  5.87 us
    ppermute x16, waiting for transfers between devices, swap(): return lax.ppermute(x, axis, [(i, i ^ bits) for i in range(count)])  5.42 us
    unnamed x14, local copies, waits for them, and re-layouts  1.36 us
    pallas_call x1, Pallas kernels, on_device(): call(functools.partial(blur_kernel, half), jax.ShapeDtypeStruct((plan.pla...  1.24 us
    select_n x1, other arithmetic, on_device(): beyond = lax.ppermute(jnp.where(even, first, last), 'tile', gaps)  1.1 us
  transfers between devices with their start and end apart: 18, of which 3 were waited for; matrix products, arithmetic and copies ran while one was open for 3% of the time, Pallas kernels for 15%

profile of v1, /device:TPU:0, one launch (start us, length us, event | category | flops | bytes accessed | tf_op | source)
XLA Modules:
  0.0 51.4 jit_solution(12560192702792833805)
XLA Ops:
  0.0 5.0 %collective-permute-start.3 = (s32[2,128,128]{2,1,0:T(8,128)}, s32[2,128,128]{2,1,0:T(8,128)S(1)}, u32[]{:S(2)}, u32[]{:S(2)}) collective-permute-start(s32[2,128,128]{2,1,0:T(8,128)} %refs_0_.3), channel_id=1, source_target_pairs={{0,12},{4,8},{8,4},{12,0},{1,13},{5,9},{9,5},{13,1},{2,14},{6,10},... | collective-permute-start | bytes 393224 | tf_op jit(solution)/shard_map/ppermute | solution.py:58
  5.0 1.5 %collective-permute-start.7 = (s32[2,128,128]{2,1,0:T(8,128)}, s32[2,128,128]{2,1,0:T(8,128)S(1)}, u32[]{:S(2)}, u32[]{:S(2)}) collective-permute-start(s32[2,128,128]{2,1,0:T(8,128)} %refs_0_.3), channel_id=1, source_target_pairs={{0,2},{1,3},{2,0},{3,1},{4,6},{5,7},{6,4},{7,5},{8,10},{9,11},{10,... | collective-permute-start | bytes 393224 | tf_op jit(solution)/shard_map/ppermute | solution.py:58
  6.5 3.1 %collective-permute-done.3.refs_6_ = s32[2,128,128]{2,1,0:T(8,128)S(1)} collective-permute-done((s32[2,128,128]{2,1,0:T(8,128)}, s32[2,128,128]{2,1,0:T(8,128)S(1)}, u32[]{:S(2)}, u32[]{:S(2)}) %collective-permute-start.3) | collective-permute-done | bytes 131104 | tf_op jit(solution)/shard_map/ppermute | solution.py:58
  9.6 1.7 %collective-permute-start.13 = (s32[2,128,128]{2,1,0:T(8,128)S(1)}, s32[2,128,128]{2,1,0:T(8,128)S(1)}, u32[]{:S(2)}, u32[]{:S(2)}) collective-permute-start(s32[2,128,128]{2,1,0:T(8,128)S(1)} %collective-permute-done.3.refs_6_), channel_id=1, source_target_pairs={{0,2},{1,3},{2,0},{3,1},{4,6},{5,7},{6,4},{7,5},{8,10},{9,11},{10,... | collective-permute-start | bytes 393224 | tf_op jit(solution)/shard_map/ppermute | solution.py:58
  11.3 1.4 %collective-permute-start.4 = (s32[2,128,128]{2,1,0:T(8,128)S(1)}, s32[2,128,128]{2,1,0:T(8,128)S(1)}, u32[]{:S(2)}, u32[]{:S(2)}) collective-permute-start(s32[2,128,128]{2,1,0:T(8,128)S(1)} %collective-permute-done.3.refs_6_), channel_id=1, source_target_pairs={{0,4},{4,0},{8,12},{12,8},{1,5},{5,1},{9,13},{13,9},{2,6},{6,2},{1... | collective-permute-start | bytes 393224 | tf_op jit(solution)/shard_map/ppermute | solution.py:58
  12.8 1.1 %slice_select_fusion = (s32[2,128,64]{2,1,0:T(8,128)S(1)}, s32[2,128,64]{2,1,0:T(8,128)S(1)}) fusion(s32[2,128,128]{2,1,0:T(8,128)} %refs_17_.1, pred[]{:T(512)S(6)} %eq.7), kind=kLoop, calls=%fused_computation.2 | loop fusion | flops 32768 | bytes 262145 | tf_op jit(solution)/shard_map/jit(_where)/select_n | solution.py:390
  13.9 0.7 %collective-permute-start.16 = (s32[2,128,64]{2,1,0:T(8,128)S(1)}, s32[2,128,64]{2,1,0:T(8,128)S(1)}, u32[]{:S(2)}, u32[]{:S(2)}) collective-permute-start(s32[2,128,64]{2,1,0:T(8,128)S(1)} %get-tuple-element.21), channel_id=1, source_target_pairs={{4,8},{8,4},{5,9},{9,5},{6,10},{10,6},{7,11},{11,7},{20,24},{24,20... | collective-permute-start | bytes 196616 | tf_op jit(solution)/shard_map/ppermute | solution.py:390
  14.7 0.6 %collective-permute-start.9 = (s32[2,128,128]{2,1,0:T(8,128)S(1)}, s32[2,128,128]{2,1,0:T(8,128)S(1)}, u32[]{:S(2)}, u32[]{:S(2)}) collective-permute-start(s32[2,128,128]{2,1,0:T(8,128)S(1)} %collective-permute-done.1.refs_2_), channel_id=1, source_target_pairs={{0,2},{1,3},{2,0},{3,1},{4,6},{5,7},{6,4},{7,5},{8,10},{9,11},{10,... | collective-permute-start | bytes 393224 | tf_op jit(solution)/shard_map/ppermute | solution.py:58
  15.3 0.2 collective-permute-start.2
  15.4 0.8 %collective-permute-done.4.refs_4_ = s32[2,128,128]{2,1,0:T(8,128)S(1)} collective-permute-done((s32[2,128,128]{2,1,0:T(8,128)S(1)}, s32[2,128,128]{2,1,0:T(8,128)S(1)}, u32[]{:S(2)}, u32[]{:S(2)}) %collective-permute-start.4) | collective-permute-done | bytes 131104 | tf_op jit(solution)/shard_map/ppermute | solution.py:58
  16.3 0.7 %collective-permute-start.11 = (s32[2,128,128]{2,1,0:T(8,128)S(1)}, s32[2,128,128]{2,1,0:T(8,128)S(1)}, u32[]{:S(2)}, u32[]{:S(2)}) collective-permute-start(s32[2,128,128]{2,1,0:T(8,128)S(1)} %collective-permute-done.4.refs_4_), channel_id=1, source_target_pairs={{0,2},{1,3},{2,0},{3,1},{4,6},{5,7},{6,4},{7,5},{8,10},{9,11},{10,... | collective-permute-start | bytes 393224 | tf_op jit(solution)/shard_map/ppermute | solution.py:58
  17.2 0.7 %copy-done.1 = f32[2,2,129]{2,1,0:T(2,128)S(1)} copy-done((f32[2,2,129]{2,1,0:T(2,128)S(1)}, f32[2,2,129]{2,1,0:T(2,128)}, u32[]{:S(2)}) %copy-start.1) | copy-done | bytes 2088
  17.8 0.4 shard_map.73
  18.2 0.1 stack.170.scal
  18.3 0.1 stack.166.scal
  18.5 5.9 %collective-permute-start.15 = (s32[2,128,64]{2,1,0:T(8,128)S(1)}, s32[2,128,64]{2,1,0:T(8,128)S(1)}, u32[]{:S(2)}, u32[]{:S(2)}) collective-permute-start(s32[2,128,64]{2,1,0:T(8,128)S(1)} %get-tuple-element.22), channel_id=1, source_target_pairs={{0,4},{4,0},{8,12},{12,8},{1,5},{5,1},{9,13},{13,9},{2,6},{6,2},{1... | collective-permute-start | bytes 196616 | tf_op jit(solution)/shard_map/ppermute | solution.py:389
  24.4 0.5 collective-permute-start.14
  25.0 0.4 collective-permute-start.12
  25.4 0.6 %copy-done.4 = s32[4]{0:T(128)S(1)} copy-done((s32[4]{0:T(128)S(1)}, s32[4]{0:T(128)}, u32[]{:S(2)}) %copy-start.4) | copy-done | bytes 40
  26.1 7.5 %shard_map.74.refs_16_ = f32[4,256,128]{2,1,0:T(8,128)S(1)} custom-call(s32[35]{0:T(128)S(1)} %stack.170.scal, s32[4]{0:T(128)S(1)} %copy-done.4, f32[2,8]{1,0:T(2,128)S(1)} %pad_maximum_fusion.table, f32[16]{0:T(128)S(1)} %copy-done.5, bf16[2,256,256]{2,1,0:T(8,128)(2,1)S(1)} %get-tuple-element.12.ky, bf16[2,3,256,256]{3,2,1,0:T(8,128)(2,1)S(1)} %get-tuple-element.13.kz, ...), custom_call_target="tpu_custom_call" | custom-call | flops 2400000000 | bytes 1048576 | tf_op jit(solution)/shard_map/pallas_call | solution.py:371
  33.6 14.9 %shard_map.75 = (f32[4,256,128]{2,1,0:T(8,128)S(1)}, f32[2,256,128]{2,1,0:T(8,128)S(1)}) custom-call(s32[63]{0:T(128)S(1)} %stack.166.scal, s32[4]{0:T(128)S(1)} %copy-done.4, f32[2,8]{1,0:T(2,128)S(1)} %pad_maximum_fusion.table, f32[16]{0:T(128)S(1)} %copy-done.5, bf16[2,256,256]{2,1,0:T(8,128)(2,1)S(1)} %get-tuple-element.12.ky, ...), custom_call_target="tpu_custom_call" | custom-call | flops 4800000000 | bytes 1048576 | tf_op jit(solution)/shard_map/pallas_call | solution.py:371
  48.6 0.1 collective-permute-start.17
  48.7 1.5 %collective-permute-done.17.other = f32[2,256,128]{2,1,0:T(8,128)S(1)} collective-permute-done((f32[2,256,128]{2,1,0:T(8,128)S(1)}, f32[2,256,128]{2,1,0:T(8,128)S(1)}, u32[]{:S(2)}, u32[]{:S(2)}) %collective-permute-start.17) | collective-permute-done | bytes 262176 | tf_op jit(solution)/shard_map/ppermute | solution.py:58
  50.2 1.2 %shard_map.76 = f32[2,128,128]{2,1,0:T(8,128)} custom-call(f32[2,256,128]{2,1,0:T(8,128)S(1)} %get-tuple-element.20.mine, f32[2,256,128]{2,1,0:T(8,128)S(1)} %collective-permute-done.17.other, f32[2,256,128]{2,1,0:T(8,128)S(1)} %get-tuple-element.16.weight, bf16[2,128,128]{2,1,0:T(8,128)(2,1)S(1)} %get-tuple-element.17.by, ...), custom_call_target="tpu_custom_call" | custom-call | bytes 1048576 | tf_op jit(solution)/shard_map/pallas_call | solution.py:406
  (36 shorter events, 0.4 us)
Async XLA Ops:
  0.0 9.6 %collective-permute-start.3 = (s32[2,128,128]{2,1,0:T(8,128)}, s32[2,128,128]{2,1,0:T(8,128)S(1)}, u32[]{:S(2)}, u32[]{:S(2)}) collective-permute-start(s32[2,128,128]{2,1,0:T(8,128)} %refs_0_.3), channel_id=1, source_target_pairs={{0,12},{4,8},{8,4},{12,0},{1,13},{5,9},{9,5},{13,1},{2,14},{6,10},... | collective-permute-start | bytes 393224 | tf_op jit(solution)/shard_map/ppermute | solution.py:58
  5.0 8.9 %collective-permute-start.7 = (s32[2,128,128]{2,1,0:T(8,128)}, s32[2,128,128]{2,1,0:T(8,128)S(1)}, u32[]{:S(2)}, u32[]{:S(2)}) collective-permute-start(s32[2,128,128]{2,1,0:T(8,128)} %refs_0_.3), channel_id=1, source_target_pairs={{0,2},{1,3},{2,0},{3,1},{4,6},{5,7},{6,4},{7,5},{8,10},{9,11},{10,... | collective-permute-start | bytes 393224 | tf_op jit(solution)/shard_map/ppermute | solution.py:58
  6.5 8.0 %collective-permute-start.1 = (s32[2,128,128]{2,1,0:T(8,128)}, s32[2,128,128]{2,1,0:T(8,128)S(1)}, u32[]{:S(2)}, u32[]{:S(2)}) collective-permute-start(s32[2,128,128]{2,1,0:T(8,128)} %refs_0_.3), channel_id=1, source_target_pairs={{0,4},{4,0},{8,12},{12,8},{1,5},{5,1},{9,13},{13,9},{2,6},{6,2},{1... | collective-permute-start | bytes 393224 | tf_op jit(solution)/shard_map/ppermute | solution.py:58
  6.5 8.1 %collective-permute-start = (s32[2,128,128]{2,1,0:T(8,128)}, s32[2,128,128]{2,1,0:T(8,128)S(1)}, u32[]{:S(2)}, u32[]{:S(2)}) collective-permute-start(s32[2,128,128]{2,1,0:T(8,128)} %refs_0_.3), channel_id=1, source_target_pairs={{0,1},{1,0},{2,3},{3,2},{4,5},{5,4},{6,7},{7,6},{8,9},{9,8},{10,11... | collective-permute-start | bytes 393224 | tf_op jit(solution)/shard_map/ppermute | solution.py:58
  9.6 7.3 %collective-permute-start.13 = (s32[2,128,128]{2,1,0:T(8,128)S(1)}, s32[2,128,128]{2,1,0:T(8,128)S(1)}, u32[]{:S(2)}, u32[]{:S(2)}) collective-permute-start(s32[2,128,128]{2,1,0:T(8,128)S(1)} %collective-permute-done.3.refs_6_), channel_id=1, source_target_pairs={{0,2},{1,3},{2,0},{3,1},{4,6},{5,7},{6,4},{7,5},{8,10},{9,11},{10,... | collective-permute-start | bytes 393224 | tf_op jit(solution)/shard_map/ppermute | solution.py:58
  11.3 5.0 %collective-permute-start.4 = (s32[2,128,128]{2,1,0:T(8,128)S(1)}, s32[2,128,128]{2,1,0:T(8,128)S(1)}, u32[]{:S(2)}, u32[]{:S(2)}) collective-permute-start(s32[2,128,128]{2,1,0:T(8,128)S(1)} %collective-permute-done.3.refs_6_), channel_id=1, source_target_pairs={{0,4},{4,0},{8,12},{12,8},{1,5},{5,1},{9,13},{13,9},{2,6},{6,2},{1... | collective-permute-start | bytes 393224 | tf_op jit(solution)/shard_map/ppermute | solution.py:58
  12.8 12.7 %copy-start.3 = (s32[2,128,128]{2,1,0:T(8,128)S(1)}, s32[2,128,128]{2,1,0:T(8,128)}, u32[]{:S(2)}) copy-start(s32[2,128,128]{2,1,0:T(8,128)} %refs_0_.3) | copy-start | bytes 393220
  13.9 3.1 %copy-start.6 = (f32[8]{0:T(128)S(1)}, f32[8]{0:T(128)}, u32[]{:S(2)}) copy-start(f32[8]{0:T(128)} %param.10) | copy-start | bytes 100
  13.9 1.4 %collective-permute-start.16 = (s32[2,128,64]{2,1,0:T(8,128)S(1)}, s32[2,128,64]{2,1,0:T(8,128)S(1)}, u32[]{:S(2)}, u32[]{:S(2)}) collective-permute-start(s32[2,128,64]{2,1,0:T(8,128)S(1)} %get-tuple-element.21), channel_id=1, source_target_pairs={{4,8},{8,4},{5,9},{9,5},{6,10},{10,6},{7,11},{11,7},{20,24},{24,20... | collective-permute-start | bytes 196616 | tf_op jit(solution)/shard_map/ppermute | solution.py:390
  14.6 3.9 %collective-permute-start.6 = (s32[2,128,128]{2,1,0:T(8,128)S(1)}, s32[2,128,128]{2,1,0:T(8,128)S(1)}, u32[]{:S(2)}, u32[]{:S(2)}) collective-permute-start(s32[2,128,128]{2,1,0:T(8,128)S(1)} %collective-permute-done.3.refs_6_), channel_id=1, source_target_pairs={{0,1},{1,0},{2,3},{3,2},{4,5},{5,4},{6,7},{7,6},{8,9},{9,8},{10,11... | collective-permute-start | bytes 393224 | tf_op jit(solution)/shard_map/ppermute | solution.py:58
  14.7 9.7 %collective-permute-start.9 = (s32[2,128,128]{2,1,0:T(8,128)S(1)}, s32[2,128,128]{2,1,0:T(8,128)S(1)}, u32[]{:S(2)}, u32[]{:S(2)}) collective-permute-start(s32[2,128,128]{2,1,0:T(8,128)S(1)} %collective-permute-done.1.refs_2_), channel_id=1, source_target_pairs={{0,2},{1,3},{2,0},{3,1},{4,6},{5,7},{6,4},{7,5},{8,10},{9,11},{10,... | collective-permute-start | bytes 393224 | tf_op jit(solution)/shard_map/ppermute | solution.py:58
  15.3 9.1 %collective-permute-start.2 = (s32[2,128,128]{2,1,0:T(8,128)S(1)}, s32[2,128,128]{2,1,0:T(8,128)S(1)}, u32[]{:S(2)}, u32[]{:S(2)}) collective-permute-start(s32[2,128,128]{2,1,0:T(8,128)S(1)} %collective-permute-done.1.refs_2_), channel_id=1, source_target_pairs={{0,1},{1,0},{2,3},{3,2},{4,5},{5,4},{6,7},{7,6},{8,9},{9,8},{10,11... | collective-permute-start | bytes 393224 | tf_op jit(solution)/shard_map/ppermute | solution.py:58
  16.3 8.6 %collective-permute-start.11 = (s32[2,128,128]{2,1,0:T(8,128)S(1)}, s32[2,128,128]{2,1,0:T(8,128)S(1)}, u32[]{:S(2)}, u32[]{:S(2)}) collective-permute-start(s32[2,128,128]{2,1,0:T(8,128)S(1)} %collective-permute-done.4.refs_4_), channel_id=1, source_target_pairs={{0,2},{1,3},{2,0},{3,1},{4,6},{5,7},{6,4},{7,5},{8,10},{9,11},{10,... | collective-permute-start | bytes 393224 | tf_op jit(solution)/shard_map/ppermute | solution.py:58
  16.9 8.0 %collective-permute-start.5 = (s32[2,128,128]{2,1,0:T(8,128)S(1)}, s32[2,128,128]{2,1,0:T(8,128)S(1)}, u32[]{:S(2)}, u32[]{:S(2)}) collective-permute-start(s32[2,128,128]{2,1,0:T(8,128)S(1)} %collective-permute-done.4.refs_4_), channel_id=1, source_target_pairs={{0,1},{1,0},{2,3},{3,2},{4,5},{5,4},{6,7},{7,6},{8,9},{9,8},{10,11... | collective-permute-start | bytes 393224 | tf_op jit(solution)/shard_map/ppermute | solution.py:58
  17.1 0.7 %copy-start.1 = (f32[2,2,129]{2,1,0:T(2,128)S(1)}, f32[2,2,129]{2,1,0:T(2,128)}, u32[]{:S(2)}) copy-start(f32[2,2,129]{2,1,0:T(2,128)} %taps.1) | copy-start | bytes 6196
  17.1 0.7 %copy-start.2 = (f32[2,129]{1,0:T(2,128)S(1)}, f32[2,129]{1,0:T(2,128)}, u32[]{:S(2)}) copy-start(f32[2,129]{1,0:T(2,128)} %dtaps.1) | copy-start | bytes 3100
  18.5 15.1 %collective-permute-start.15 = (s32[2,128,64]{2,1,0:T(8,128)S(1)}, s32[2,128,64]{2,1,0:T(8,128)S(1)}, u32[]{:S(2)}, u32[]{:S(2)}) collective-permute-start(s32[2,128,64]{2,1,0:T(8,128)S(1)} %get-tuple-element.22), channel_id=1, source_target_pairs={{0,4},{4,0},{8,12},{12,8},{1,5},{5,1},{9,13},{13,9},{2,6},{6,2},{1... | collective-permute-start | bytes 196616 | tf_op jit(solution)/shard_map/ppermute | solution.py:389
  24.4 9.2 %collective-permute-start.8 = (s32[2,128,128]{2,1,0:T(8,128)S(1)}, s32[2,128,128]{2,1,0:T(8,128)S(1)}, u32[]{:S(2)}, u32[]{:S(2)}) collective-permute-start(s32[2,128,128]{2,1,0:T(8,128)S(1)} %collective-permute-done.7.refs_8_), channel_id=1, source_target_pairs={{0,1},{1,0},{2,3},{3,2},{4,5},{5,4},{6,7},{7,6},{8,9},{9,8},{10,11... | collective-permute-start | bytes 393224 | tf_op jit(solution)/shard_map/ppermute | solution.py:58
  24.4 9.2 %collective-permute-start.14 = (s32[2,128,128]{2,1,0:T(8,128)S(1)}, s32[2,128,128]{2,1,0:T(8,128)S(1)}, u32[]{:S(2)}, u32[]{:S(2)}) collective-permute-start(s32[2,128,128]{2,1,0:T(8,128)S(1)} %collective-permute-done.13.refs_14_), channel_id=1, source_target_pairs={{0,1},{1,0},{2,3},{3,2},{4,5},{5,4},{6,7},{7,6},{8,9},{9,8},{10,11... | collective-permute-start | bytes 393224 | tf_op jit(solution)/shard_map/ppermute | solution.py:58
  24.9 8.7 %collective-permute-start.10 = (s32[2,128,128]{2,1,0:T(8,128)S(1)}, s32[2,128,128]{2,1,0:T(8,128)S(1)}, u32[]{:S(2)}, u32[]{:S(2)}) collective-permute-start(s32[2,128,128]{2,1,0:T(8,128)S(1)} %collective-permute-done.9.refs_10_), channel_id=1, source_target_pairs={{0,1},{1,0},{2,3},{3,2},{4,5},{5,4},{6,7},{7,6},{8,9},{9,8},{10,11... | collective-permute-start | bytes 393224 | tf_op jit(solution)/shard_map/ppermute | solution.py:58
  25.0 8.6 %collective-permute-start.12 = (s32[2,128,128]{2,1,0:T(8,128)S(1)}, s32[2,128,128]{2,1,0:T(8,128)S(1)}, u32[]{:S(2)}, u32[]{:S(2)}) collective-permute-start(s32[2,128,128]{2,1,0:T(8,128)S(1)} %collective-permute-done.11.refs_12_), channel_id=1, source_target_pairs={{0,1},{1,0},{2,3},{3,2},{4,5},{5,4},{6,7},{7,6},{8,9},{9,8},{10,11... | collective-permute-start | bytes 393224 | tf_op jit(solution)/shard_map/ppermute | solution.py:58
  25.4 0.7 %copy-start.5 = (f32[16]{0:T(128)S(1)}, f32[16]{0:T(128)}, u32[]{:S(2)}) copy-start(f32[16]{0:T(128)} %bright.3) | copy-start | bytes 196
  26.1 7.5 %copy-start = (s32[2,128,128]{2,1,0:T(8,128)S(1)}, s32[2,128,128]{2,1,0:T(8,128)}, u32[]{:S(2)}) copy-start(s32[2,128,128]{2,1,0:T(8,128)} %refs_17_.1) | copy-start | bytes 393220
  48.6 1.6 %collective-permute-start.17 = (f32[2,256,128]{2,1,0:T(8,128)S(1)}, f32[2,256,128]{2,1,0:T(8,128)S(1)}, u32[]{:S(2)}, u32[]{:S(2)}) collective-permute-start(f32[2,256,128]{2,1,0:T(8,128)S(1)} %get-tuple-element.19), channel_id=1, source_target_pairs={{0,1},{1,0},{2,3},{3,2},{4,5},{5,4},{6,7},{7,6},{8,9},{9,8},{10,11... | collective-permute-start | bytes 786440 | tf_op jit(solution)/shard_map/ppermute | solution.py:58
  (1 other events, 0.7 us)

commit v2 on v1

v2 whole, which is shorter than its diff:
```python
import functools

import jax
import jax.numpy as jnp
from jax import lax
from jax.experimental import pallas as pl
from jax.experimental.pallas import tpu as pltpu
from jax.sharding import PartitionSpec as P

SHEET_WIDTH = 6.0
AMPLITUDE = 2.0
ROOM = 10 * 1024 * 1024
PIN = 1 << 40
SMEM = pltpu.SMEM
VMEM = pltpu.VMEM
HBM = pltpu.HBM


class Plan:
    def __init__(self, labels, positions, taps):
        self.planes, self.ny, self.cz = labels.shape
        self.half = taps // 2
        self.tiles = lax.axis_size("tile")
        self.cores = lax.axis_size("sect") // 2
        self.own = self.cores * self.planes
        self.all_x = 2 * self.own
        self.sheets = -(-positions // self.cores)
        self.block = 2 * self.half
        self.units = self.cz // self.half
        self.reach = -(-(self.all_x + 1) * self.half // self.cz)
        self.whole = self.tiles <= 2 * self.reach + 1
        self.window = self.tiles if self.whole else 2 * self.reach + 1
        self.rows = self.window * self.cz
        self.extent = self.cz + 2 * self.half
        self.width = self.sheets * self.ny

    def here(self):
        sect = lax.axis_index("sect")
        return lax.axis_index("tile"), sect // self.cores, lax.rem(sect, self.cores)

    def blocks(self, left):
        need = self.units + 2 + 2 * left
        return (min(need, self.window * self.units) if self.whole else need) // 2

    def start(self, left):
        if self.whole:
            last = jnp.maximum(self.window * self.units - (self.units + 2 + 2 * left), 0)
            unit = jnp.clip(lax.axis_index("tile") * self.units - 1 - left, 0, last)
        else:
            unit = self.reach * self.units - 1 - left
        return unit * self.half

    def home(self):
        return lax.axis_index("tile") * self.cz if self.whole else self.reach * self.cz


def swap(x, axis, bits):
    count = lax.axis_size(axis)
    return lax.ppermute(x, axis, [(i, i ^ bits) for i in range(count)])


def shift(x, axis, step):
    count = lax.axis_size(axis)
    return lax.ppermute(x, axis, [(i, i + step) for i in range(count) if 0 <= i + step < count])


def after(x, *done):
    return lax.optimization_barrier((x, *done))[0]


def tile_pieces(plan, mine, start, crossed):
    if plan.whole and plan.tiles & (plan.tiles - 1) == 0:
        got = {0: mine}
        if plan.tiles == 4:
            got[3] = swap(mine, "tile", 3)
            got[1] = swap(after(mine, *start), "tile", 1)
            got[2] = swap(after(got[3], *crossed), "tile", 1)
        else:
            for bits in range(1, plan.tiles):
                got[bits] = swap(mine, "tile", bits)
        return list(got.values()), [("xor", bits) for bits in got]
    if plan.whole:
        turns = range(plan.tiles)
        count = plan.tiles
        pieces = [
            lax.ppermute(mine, "tile", [(i, (i + k) % count) for i in range(count)]) if k else mine
            for k in turns
        ]
        return pieces, [("turn", k) for k in turns]
    steps = sorted(range(-plan.reach, plan.reach + 1), key=abs)
    return [shift(mine, "tile", -k) if k else mine for k in steps], [("step", k) for k in steps]


def block_of(plan, source):
    kind, k = source
    tile = lax.axis_index("tile")
    if kind == "xor":
        return tile ^ k, None
    if kind == "turn":
        return lax.rem(tile - k + plan.tiles, plan.tiles), None
    return k + plan.reach, (tile + k >= 0) & (tile + k < plan.tiles)


def halves(x):
    high = x.astype(jnp.bfloat16)
    return high, (x - high.astype(jnp.float32)).astype(jnp.bfloat16)


def dot(a, b):
    return jnp.dot(a, b, preferred_element_type=jnp.float32)


def three(high, low, matrix_high, matrix_low):
    return dot(high, matrix_high) + dot(low, matrix_high) + dot(high, matrix_low)


def circulant(row, size, half):
    wide = jnp.broadcast_to(row, (size, size))
    return pltpu.roll(wide, (size - half) % size, 1, stride=1, stride_axis=0).T


def band(row, size, wide):
    return pltpu.roll(jnp.broadcast_to(row, (size, wide)), 0, 1, stride=1, stride_axis=0)


def complex_matrix(diagonal, upper, lower):
    top = jnp.concatenate([diagonal, upper], axis=1)
    return jnp.concatenate([top, jnp.concatenate([lower, diagonal], axis=1)], axis=0)


def fetch(pairs, sems):
    copies = [pltpu.make_async_copy(src, dst, sems.at[i]) for i, (src, dst) in enumerate(pairs)]
    for copy in copies:
        copy.start()
    return copies


def build_bands(plan, taps, dtaps, phases, positions, ky, kz, by, bz, table, sheet, line):
    ny, half, block = plan.ny, plan.half, plan.block
    wide = 2 * block
    count = taps.shape[2]

    def padded(row):
        line[...] = jnp.zeros(line.shape, jnp.float32)
        line[0:1, :count] = row
        return line[0:1, :]

    def folded(row):
        spread = padded(row)
        return sum(spread[:, i:i + ny] for i in range(0, spread.shape[1], ny))

    def keep(ref, matrix, place=()):
        ref[(0, *place)], ref[(1, *place)] = halves(matrix)

    cyr = circulant(folded(taps[0, 0:1, :]), ny, half)
    cyi = circulant(folded(taps[0, 1:2, :]), ny, half)
    keep(ky, complex_matrix(cyr, cyi, -cyi))
    czr = band(padded(taps[1, 0:1, :])[:, :wide], block, wide)
    czi = band(padded(taps[1, 1:2, :])[:, :wide], block, wide)
    early = complex_matrix(czr[:, :block], -czi[:, :block], czi[:, :block])
    late = complex_matrix(czr[:, block:], -czi[:, block:], czi[:, block:])
    for number, matrix in enumerate((early, early + late, late)):
        keep(kz, matrix, (number,))
    keep(by, circulant(folded(dtaps[0:1, :]), ny, half))
    keep(bz, band(padded(dtaps[1:2, :])[:, :wide], block, wide))

    table[0:1, :] = jnp.cos(phases[...])
    table[1:2, :] = jnp.sin(phases[...])
    core = plan.here()[2]
    lane = lax.broadcasted_iota(jnp.int32, (1, ny), 1).astype(jnp.float32)
    for p in range(plan.sheets):
        number = core * plan.sheets + p
        live = number < positions.shape[0]
        centre = positions[jnp.where(live, number, 0)].astype(jnp.float32)
        offset = (lane - centre) / SHEET_WIDTH
        sheet[:, p * ny:(p + 1) * ny] = jnp.where(live, AMPLITUDE, 0.0) * jnp.exp(-offset * offset)


def choose(index, values):
    size = 1 << (len(values) - 1).bit_length()
    values = list(values) + [values[-1]] * (size - len(values))
    for b in range(size.bit_length() - 1):
        bit = (index & (1 << b)) != 0
        values = [jnp.where(bit, values[i + 1], values[i]) for i in range(0, len(values), 2)]
    return values[0]


def look_up(plan, sources, pieces, table, cosine, sine):
    cz = plan.cz
    core = plan.here()[2]
    entries = [[table[part:part + 1, e:e + 1] for e in range(table.shape[1])] for part in range(2)]
    for number, piece in pieces:
        block, valid = block_of(plan, sources[number // plan.cores])
        first = (core ^ (number % plan.cores)) * plan.planes
        row = pl.multiple_of(block * cz, cz)
        for plane in range(plan.planes):
            kind = piece[plane].T
            for values, target in zip(entries, (cosine, sine)):
                value = choose(kind, values)
                value = value if valid is None else jnp.where(valid, value, 0.0)
                target[first + plane, pl.ds(row, cz), :] = value


def enter(plan, sheet, field, spread):
    half, rows = plan.half, plan.rows
    wide = (rows, plan.width)
    field[0, half:half + rows, :] = jnp.broadcast_to(sheet[...], wide)
    field[1, half:half + rows, :] = jnp.zeros(wide, jnp.float32)
    for ref in (field, spread):
        for d in range(2):
            ref[d, :half, :] = jnp.zeros((half, plan.width), jnp.float32)
            ref[d, half + rows:, :] = jnp.zeros((half, plan.width), jnp.float32)


def propagate(plan, cos_at, sin_at, left, sources, targets, ky, kz, field, spread):
    ny, half, block, sheets = plan.ny, plan.half, plan.block, plan.sheets
    source, target = plan.start(left + 1), plan.start(left)

    def each(number, body):
        if plan.whole:
            for b in range(number):
                body(b)
        else:
            lax.fori_loop(0, number, lambda b, _: body(b), None)

    def turn(b):
        row = pl.multiple_of(source + b * block, half)
        cos, sin = cos_at(row, block), sin_at(row, block)
        parts = []
        for p in range(sheets):
            lanes = slice(p * ny, (p + 1) * ny)
            re = field[0, pl.ds(row + half, block), lanes]
            im = field[1, pl.ds(row + half, block), lanes]
            parts.append(jnp.concatenate([re * cos - im * sin, re * sin + im * cos], axis=1))
        high, low = halves(jnp.concatenate(parts, axis=0))
        v = three(high, low, ky[0], ky[1])
        for d in range(2):
            spread[d, pl.ds(row + half, block), :] = jnp.concatenate(
                [v[p * block:(p + 1) * block, d * ny:(d + 1) * ny] for p in range(sheets)], axis=1
            )

    def product(number, x):
        high, low = halves(x)
        return dot(kz[0, number], high) + dot(kz[1, number], high) + dot(kz[0, number], low)

    def window(row):
        return jnp.concatenate([spread[d, pl.ds(row, block), :] for d in range(2)], axis=0)

    def store(row, w):
        field[0, pl.ds(row + half, block), :] = w[:block]
        field[1, pl.ds(row + half, block), :] = w[block:]

    def pair(b):
        row = pl.multiple_of(target + 2 * b * block, half)
        x = [window(row + i * block) for i in range(3)]
        middle = product(1, x[1])
        store(row, product(0, x[0] - x[1]) + middle)
        store(row + block, product(2, x[2] - x[1]) + middle)

    def single(b):
        row = pl.multiple_of(target + b * block, half)
        store(row, product(0, window(row)) + product(2, window(row + block)))

    each(sources, turn)
    each(targets // 2, pair)
    if targets % 2:
        single(targets - 1)


def energy(plan, field):
    home = pl.multiple_of(plan.home(), plan.half)
    re = field[0, pl.ds(home, plan.extent), :]
    im = field[1, pl.ds(home, plan.extent), :]
    every = re * re + im * im
    total = every[:, :plan.ny]
    for p in range(1, plan.sheets):
        total = total + every[:, p * plan.ny:(p + 1) * plan.ny]
    return total


def steps_of(plan, begin, end, step, total):
    def shape(k):
        return plan.blocks(total - k), plan.blocks(total - 1 - k)

    k = begin
    while k < end:
        last = k + 1
        while last < end and shape(last) == shape(k):
            last += 1
        lax.fori_loop(k, last, lambda i, _, s=shape(k): step(i, *s), None)
        k = last


def short_kernel(plan, sources, hbm_taps, hbm_dtaps, hbm_phases, hbm_positions, hbm_mine, *refs):
    count = len(sources) * plan.cores - 1
    pieces = refs[:count]
    out, ky, kz, by, bz, table, sheet, hbm_cosine, hbm_sine = refs[count:count + 9]
    taps, dtaps, phases, positions, mine, cosine, sine, field, spread, line, sems = refs[count + 9:]
    pairs = [(hbm_phases, phases), (hbm_positions, positions), (hbm_taps, taps), (hbm_dtaps, dtaps)]
    *small, arriving = fetch([*pairs, (hbm_mine, mine)], sems)
    for copy in small:
        copy.wait()
    build_bands(plan, taps, dtaps, phases, positions, ky, kz, by, bz, table, sheet, line)
    own = plan.own
    enter(plan, sheet, field, spread)
    look_up(plan, sources, list(enumerate(pieces, 1)), table, cosine, sine)
    arriving.wait()
    look_up(plan, sources, [(0, mine)], table, cosine, sine)
    leaving = fetch([(cosine, hbm_cosine), (sine, hbm_sine)], sems)
    side = plan.here()[1]

    def step(k, reads, writes):
        slot = jnp.where(side == 0, k, own - 1 - k)
        maps = [lambda row, n, ref=ref: ref[slot, pl.ds(row, n), :] for ref in (cosine, sine)]
        propagate(plan, *maps, own - 1 - k, reads, writes, ky, kz, field, spread)
        out[slot] = energy(plan, field)

    steps_of(plan, 0, own, step, own)
    for copy in leaving:
        copy.wait()


def long_kernel(plan, sources, ky, kz, table, sheet, hbm_cosine, hbm_sine, earlier, *refs):
    count = len(sources) * plan.cores
    pieces = refs[:count]
    out, far_cosine, far_sine, cosine, sine, field, spread, sems = refs[count:]
    own = plan.own
    arriving = fetch([(hbm_cosine, cosine), (hbm_sine, sine)], sems)
    enter(plan, sheet, field, spread)
    look_up(plan, sources, list(enumerate(pieces)), table, far_cosine, far_sine)
    side = plan.here()[1]

    def far_step(k, reads, writes):
        slot = jnp.where(side == 0, own - 1 - k, k)
        maps = [lambda row, n, ref=ref: ref[slot, pl.ds(row, n), :] for ref in (far_cosine, far_sine)]
        propagate(plan, *maps, 2 * own - 1 - k, reads, writes, ky, kz, field, spread)

    def step(k, reads, writes):
        slot = jnp.where(side == 0, 2 * own - 1 - k, k - own)
        maps = [lambda row, n, ref=ref: ref[slot, pl.ds(row, n), :] for ref in (cosine, sine)]
        propagate(plan, *maps, 2 * own - 1 - k, reads, writes, ky, kz, field, spread)
        out[slot] = earlier[slot] + energy(plan, field)

    steps_of(plan, 0, own, far_step, 2 * own)
    for copy in arriving:
        copy.wait()
    steps_of(plan, own, 2 * own, step, 2 * own)


def blur_kernel(plan, mine, other, hbm_bright, hbm_labels, facing, beyond, by, bz, out, bright, labels, sems):
    half, ny, extent = plan.half, plan.ny, plan.extent
    first, arriving = fetch([(hbm_bright, bright), (hbm_labels, labels)], sems)
    first.wait()
    tile = lax.axis_index("tile")
    even = lax.rem(tile, 2) == 0
    first_half = lax.broadcasted_iota(jnp.int32, (ny, 2 * half), 1) < half
    ends = [(tile < plan.tiles - 1).astype(jnp.float32), (tile > 0).astype(jnp.float32)]
    inside = jnp.where(first_half, ends[0], ends[1])
    values = [bright[e] for e in range(bright.shape[0])]
    halos = []
    for x in range(plan.planes):
        before = jnp.where(even, beyond[x], facing[x])[:, -2 * half:]
        behind = jnp.where(even, facing[x], beyond[x])[:, :2 * half]
        halos.append((choose(jnp.where(first_half, behind, before), values) * inside).T)
    arriving.wait()
    parts = []
    for x in range(plan.planes):
        weight = jnp.concatenate([halos[x][half:], choose(labels[x], values).T, halos[x][:half]], axis=0)
        parts.append((mine[x] + other[x]) * weight)
    high, low = halves(jnp.concatenate(parts, axis=0))
    v = three(high, low, by[0], by[1])
    v = jnp.concatenate([v[x * extent:(x + 1) * extent] for x in range(plan.planes)], axis=1)
    high, low = halves(v)
    block = plan.block
    for b in range(plan.cz // block):
        rows = slice(b * block, b * block + 2 * block)
        w = dot(bz[0], high[rows]) + dot(bz[1], high[rows]) + dot(bz[0], low[rows])
        for x in range(plan.planes):
            out[x, :, b * block:(b + 1) * block] = w[:, x * ny:(x + 1) * ny].T


def size_of(x):
    return x.size * x.dtype.itemsize


def call(kernel, outs, in_spaces, scratch=(), flops=0, out_spaces=None):
    return lambda *args: call_with(args, kernel, outs, in_spaces, scratch, flops, out_spaces)


def call_with(args, kernel, outs, in_spaces, scratch, flops, out_spaces):
    args = [
        pltpu.with_memory_space_constraint(x, space) if space is HBM or size_of(x) > PIN else x
        for x, space in zip(args, in_spaces)
    ]
    held = [x for x, space in zip(args, in_spaces) if space is VMEM]
    held += jax.tree.leaves(outs)
    held += [jax.ShapeDtypeStruct(x.shape, x.dtype) for x in scratch if x.memory_space == VMEM]
    if out_spaces is None:
        out_spaces = jax.tree.map(lambda _: VMEM, outs)
    limit = ROOM + sum(size_of(x) for x in held)
    flat, tree = jax.tree.flatten(outs)
    spaces = jax.tree.leaves(out_spaces)
    outs = tree.unflatten(
        [HBM(x.shape, x.dtype) if space is HBM else x for x, space in zip(flat, spaces)]
    )
    return pl.pallas_call(
        kernel,
        out_shape=outs,
        in_specs=[pl.BlockSpec(memory_space=space) for space in in_spaces],
        out_specs=jax.tree.map(lambda space: pl.BlockSpec(memory_space=space), out_spaces),
        scratch_shapes=list(scratch),
        compiler_params=pltpu.CompilerParams(vmem_limit_bytes=limit),
        cost_estimate=pl.CostEstimate(flops=flops, bytes_accessed=1 << 20, transcendentals=0),
    )(*args)


def on_device(labels, classes, positions, phase_table, brightness, prop_taps, detect_taps):
    taps = prop_taps.shape[-1]
    plan = Plan(labels, positions.shape[0], taps)
    ny, half, block, rows = plan.ny, plan.half, plan.block, plan.rows
    tiles, cores = plan.tiles, plan.cores
    core = plan.here()[2]
    f32, bf16 = jnp.float32, jnp.bfloat16
    shape = jax.ShapeDtypeStruct

    def over_cores(array):
        return [array] + [swap(array, "sect", bits) for bits in range(1, cores)]

    crossed = [swap(classes, "sect", cores)]
    pieces, sources = tile_pieces(plan, classes, (), crossed)
    near = []
    for number, piece in enumerate(pieces):
        shared = over_cores(piece)
        near += shared
        if number:
            hold = number < len(pieces) - 1
            crossed.append(swap(after(piece, *shared[1:]) if hold else piece, "sect", cores))

    maps = shape((plan.own, rows, ny), f32)
    whole_maps = pltpu.VMEM((plan.own, rows, ny), f32)
    state = pltpu.VMEM((2, rows + 2 * half, plan.width), f32)
    sums = shape((plan.own, plan.extent, ny), f32)
    line = -(-max(4 * half, taps) // ny) * ny
    phases = phase_table[None]
    near[1] = after(near[1], crossed[len(crossed) // 2])
    sums, ky, kz, by, bz, table, sheet, cosine, sine = call(
        functools.partial(short_kernel, plan, sources),
        (
            sums,
            shape((2, 2 * ny, 2 * ny), bf16),
            shape((2, 3, 2 * block, 2 * block), bf16),
            shape((2, ny, ny), bf16),
            shape((2, block, 2 * block), bf16),
            shape((2, phases.shape[1]), f32),
            shape((1, plan.width), f32),
            maps,
            maps,
        ),
        [HBM] * 5 + [VMEM] * (len(near) - 1),
        [
            pltpu.VMEM(prop_taps.shape, f32),
            pltpu.VMEM(detect_taps.shape, f32),
            pltpu.VMEM(phases.shape, f32),
            pltpu.SMEM(positions.shape, positions.dtype),
            pltpu.VMEM(classes.shape, classes.dtype),
            whole_maps,
            whole_maps,
            state,
            state,
            pltpu.VMEM((8, line), f32),
            pltpu.SemaphoreType.DMA((5,)),
        ],
        flops=3 * 10**9,
        out_spaces=(VMEM,) * 7 + (HBM,) * 2,
    )(prop_taps, detect_taps, phases, positions, *near)

    pairs = [(i, i ^ 1) for i in range(tiles) if i ^ 1 < tiles]
    gaps = [(i, ((i + 1) ^ 1) - 1) for i in range(1, tiles) if ((i + 1) ^ 1) - 1 < tiles]
    if tiles == 4:
        gaps = [(i, i ^ 3) for i in range(tiles)]
    late = after(labels, sums)
    facing = lax.ppermute(late, "tile", pairs)
    beyond = lax.ppermute(late, "tile", gaps)

    far = []
    for number, piece in enumerate(crossed):
        last = number == len(crossed) - 1
        far += [piece] + over_cores(after(piece, sums) if last else piece)[1:]
    sums = call(
        functools.partial(long_kernel, plan, sources),
        shape((plan.own, plan.extent, ny), f32),
        [VMEM] * 4 + [HBM] * 2 + [VMEM] * (1 + len(far)),
        [whole_maps] * 4 + [state, state, pltpu.SemaphoreType.DMA((2,))],
        flops=6 * 10**9,
    )(ky, kz, table, sheet, cosine, sine, sums, *far)

    parts = sums.reshape(cores, plan.planes, plan.extent, ny)
    mine = lax.dynamic_index_in_dim(parts, core, 0, keepdims=False)
    other = None
    for bits in range(1, cores):
        leaving = lax.dynamic_index_in_dim(parts, core ^ bits, 0, keepdims=False)
        arrived = swap(after(leaving, facing, beyond), "sect", bits)
        other = arrived if other is None else other + arrived
    other = jnp.zeros_like(mine) if other is None else other
    return call(
        functools.partial(blur_kernel, plan),
        shape((plan.planes, ny, plan.cz), f32),
        [VMEM] * 2 + [HBM] * 2 + [VMEM] * 4,
        [
            pltpu.SMEM(brightness.shape, f32),
            pltpu.VMEM(labels.shape, labels.dtype),
            pltpu.SemaphoreType.DMA((2,)),
        ],
    )(mine, other, brightness, labels, facing, beyond, by, bz)


def solution(mesh):
    spread = P(("groups", "sect"), None, "tile")
    in_specs = (spread, spread, P("groups"), P(), P(), P(), P())
    return jax.shard_map(
        on_device, mesh=mesh, in_specs=in_specs, out_specs=spread, check_vma=False
    )
```

time: 52.4 us -> 48.5 us (0.926); the launches traced: 51.4 us -> 48.3 us
  waiting for transfers between devices: 5.43 us -> 8.75 us
  starting transfers between devices: 18.9 us -> 16.1 us
  local copies, waits for them, and re-layouts: 1.7 us -> 0.05 us
  other arithmetic: 1.11 us -> 0 us
  Pallas kernels: 24 us -> 23.4 us
    ppermute x16, waiting for transfers between devices: 5.42 us -> 8.75 us  [swap(): return lax.ppermute(x, axis, [(i, i ^ bits) for i in range(count)])]
    ppermute x2, starting transfers between devices: 6.54 us -> 3.22 us  [the longest x1 2.61 us: on_device(): beyond = lax.ppermute(late, 'tile', gaps)]
    unnamed x14 -> x2, local copies, waits for them, and re-layouts: 1.36 us -> 0.01 us
    select_n x1 -> x0, other arithmetic: 1.1 us -> none  [on_device(): beyond = lax.ppermute(jnp.where(even, first, last), 'tile', gaps)]
    pallas_call x4 -> x3, Pallas kernels: 24 us -> 23.4 us  [call_with(): pl.pallas_call(kernel, out_shape=outs, in_specs=[pl.BlockSpec(memory_spac...]
  transfers between devices with their start and end apart: 18 -> 18, of which waited for: 3 -> 3; matrix products, arithmetic and copies ran while one was open for 3% -> 0% of each run, Pallas kernels for 15% -> 44%
where the time goes in v2:
time: 48.5 us; the launch traced here: 48.3 us
  Pallas kernels  23.4 us (48%)
  starting transfers between devices  16.1 us (33%)
  waiting for transfers between devices  8.75 us (18%)
    pallas_call x3, Pallas kernels, call_with(): pl.pallas_call(kernel, out_shape=outs, in_specs=[pl.BlockSpec(memory_spac...  23.4 us
    ppermute x16, starting transfers between devices, swap(): return lax.ppermute(x, axis, [(i, i ^ bits) for i in range(count)])  12.9 us
    ppermute x16, waiting for transfers between devices, swap(): return lax.ppermute(x, axis, [(i, i ^ bits) for i in range(count)])  8.75 us
    ppermute x1, starting transfers between devices, on_device(): beyond = lax.ppermute(late, 'tile', gaps)  2.61 us
  transfers between devices with their start and end apart: 18, of which 3 were waited for; matrix products, arithmetic and copies ran while one was open for 0% of the time, Pallas kernels for 44%

profile of v2, /device:TPU:0, one launch (start us, length us, event | category | flops | bytes accessed | tf_op | source)
XLA Modules:
  0.0 48.3 jit_solution(3348261177527256086)
XLA Ops:
  0.0 3.0 %collective-permute-start.1 = (s32[2,128,128]{2,1,0:T(8,128)}, s32[2,128,128]{2,1,0:T(8,128)S(1)}, u32[]{:S(2)}, u32[]{:S(2)}) collective-permute-start(s32[2,128,128]{2,1,0:T(8,128)} %hbm_mine.1), channel_id=1, source_target_pairs={{0,4},{4,0},{8,12},{12,8},{1,5},{5,1},{9,13},{13,9},{2,6},{6,2},{1... | collective-permute-start | bytes 393224 | tf_op jit(solution)/shard_map/ppermute | solution.py:59
  3.0 2.5 %collective-permute-start.4 = (s32[2,128,128]{2,1,0:T(8,128)}, s32[2,128,128]{2,1,0:T(8,128)S(1)}, u32[]{:S(2)}, u32[]{:S(2)}) collective-permute-start(s32[2,128,128]{2,1,0:T(8,128)} %hbm_mine.1), channel_id=1, source_target_pairs={{0,12},{4,8},{8,4},{12,0},{1,13},{5,9},{9,5},{13,1},{2,14},{6,10},... | collective-permute-start | bytes 393224 | tf_op jit(solution)/shard_map/ppermute | solution.py:59
  5.5 1.5 %collective-permute-start.6 = (s32[2,128,128]{2,1,0:T(8,128)}, s32[2,128,128]{2,1,0:T(8,128)S(1)}, u32[]{:S(2)}, u32[]{:S(2)}) collective-permute-start(s32[2,128,128]{2,1,0:T(8,128)} %hbm_mine.1), channel_id=1, source_target_pairs={{0,2},{1,3},{2,0},{3,1},{4,6},{5,7},{6,4},{7,5},{8,10},{9,11},{10,... | collective-permute-start | bytes 393224 | tf_op jit(solution)/shard_map/ppermute | solution.py:59
  7.0 0.0 collective-permute-done.1.refs_3_
  7.0 0.0 collective-permute-start.2
  7.0 4.8 %collective-permute-done.4.refs_1_ = s32[2,128,128]{2,1,0:T(8,128)S(1)} collective-permute-done((s32[2,128,128]{2,1,0:T(8,128)}, s32[2,128,128]{2,1,0:T(8,128)S(1)}, u32[]{:S(2)}, u32[]{:S(2)}) %collective-permute-start.4) | collective-permute-done | bytes 131104 | tf_op jit(solution)/shard_map/ppermute | solution.py:59
  11.8 0.0 collective-permute-done.6.refs_0_
  11.8 0.6 %collective-permute-start.7 = (s32[2,128,128]{2,1,0:T(8,128)S(1)}, s32[2,128,128]{2,1,0:T(8,128)S(1)}, u32[]{:S(2)}, u32[]{:S(2)}) collective-permute-start(s32[2,128,128]{2,1,0:T(8,128)S(1)} %collective-permute-done.4.refs_1_), channel_id=1, source_target_pairs={{0,4},{4,0},{8,12},{12,8},{1,5},{5,1},{9,13},{13,9},{2,6},{6,2},{1... | collective-permute-start | bytes 393224 | tf_op jit(solution)/shard_map/ppermute | solution.py:59
  12.5 0.5 %collective-permute-start = (s32[2,128,128]{2,1,0:T(8,128)}, s32[2,128,128]{2,1,0:T(8,128)S(1)}, u32[]{:S(2)}, u32[]{:S(2)}) collective-permute-start(s32[2,128,128]{2,1,0:T(8,128)} %hbm_mine.1), channel_id=1, source_target_pairs={{0,1},{1,0},{2,3},{3,2},{4,5},{5,4},{6,7},{7,6},{8,9},{9,8},{10,11... | collective-permute-start | bytes 393224 | tf_op jit(solution)/shard_map/ppermute | solution.py:59
  13.0 1.5 %collective-permute-start.3 = (s32[2,128,128]{2,1,0:T(8,128)S(1)}, s32[2,128,128]{2,1,0:T(8,128)S(1)}, u32[]{:S(2)}, u32[]{:S(2)}) collective-permute-start(s32[2,128,128]{2,1,0:T(8,128)S(1)} %collective-permute-done.1.refs_3_), channel_id=1, source_target_pairs={{0,2},{1,3},{2,0},{3,1},{4,6},{5,7},{6,4},{7,5},{8,10},{9,11},{10,... | collective-permute-start | bytes 393224 | tf_op jit(solution)/shard_map/ppermute | solution.py:59
  14.5 2.4 %collective-permute-done.7.refs_5_ = s32[2,128,128]{2,1,0:T(8,128)S(1)} collective-permute-done((s32[2,128,128]{2,1,0:T(8,128)S(1)}, s32[2,128,128]{2,1,0:T(8,128)S(1)}, u32[]{:S(2)}, u32[]{:S(2)}) %collective-permute-start.7) | collective-permute-done | bytes 131104 | tf_op jit(solution)/shard_map/ppermute | solution.py:59
  16.8 0.5 %collective-permute-start.9 = (s32[2,128,128]{2,1,0:T(8,128)S(1)}, s32[2,128,128]{2,1,0:T(8,128)S(1)}, u32[]{:S(2)}, u32[]{:S(2)}) collective-permute-start(s32[2,128,128]{2,1,0:T(8,128)S(1)} %collective-permute-done.6.refs_0_), channel_id=1, source_target_pairs={{0,1},{1,0},{2,3},{3,2},{4,5},{5,4},{6,7},{7,6},{8,9},{9,8},{10,11... | collective-permute-start | bytes 393224 | tf_op jit(solution)/shard_map/ppermute | solution.py:59
  17.3 1.5 %collective-permute-start.10 = (s32[2,128,128]{2,1,0:T(8,128)S(1)}, s32[2,128,128]{2,1,0:T(8,128)S(1)}, u32[]{:S(2)}, u32[]{:S(2)}) collective-permute-start(s32[2,128,128]{2,1,0:T(8,128)S(1)} %collective-permute-done.4.refs_1_), channel_id=1, source_target_pairs={{0,2},{1,3},{2,0},{3,1},{4,6},{5,7},{6,4},{7,5},{8,10},{9,11},{10,... | collective-permute-start | bytes 393224 | tf_op jit(solution)/shard_map/ppermute | solution.py:59
  18.8 0.5 %collective-permute-start.13 = (s32[2,128,128]{2,1,0:T(8,128)S(1)}, s32[2,128,128]{2,1,0:T(8,128)S(1)}, u32[]{:S(2)}, u32[]{:S(2)}) collective-permute-start(s32[2,128,128]{2,1,0:T(8,128)S(1)} %collective-permute-done.7.refs_5_), channel_id=1, source_target_pairs={{0,2},{1,3},{2,0},{3,1},{4,6},{5,7},{6,4},{7,5},{8,10},{9,11},{10,... | collective-permute-start | bytes 393224 | tf_op jit(solution)/shard_map/ppermute | solution.py:59
  19.4 8.3 %shard_map.73 = (f32[4,256,128]{2,1,0:T(8,128)S(1)}, bf16[2,256,256]{2,1,0:T(8,128)(2,1)S(1)}, bf16[2,3,256,256]{3,2,1,0:T(8,128)(2,1)S(1)}, bf16[2,128,128]{2,1...) custom-call(f32[2,2,129]{2,1,0:T(2,128)} %hbm_taps.1, ...), custom_call_target="tpu_custom_call" | custom-call | flops 3000000000 | bytes 1048576 | tf_op jit(solution)/shard_map/pallas_call | solution.py:406
  27.7 0.1 collective-permute-start.14
  27.8 0.5 %collective-permute-start.11 = (s32[2,128,128]{2,1,0:T(8,128)S(1)}, s32[2,128,128]{2,1,0:T(8,128)S(1)}, u32[]{:S(2)}, u32[]{:S(2)}) collective-permute-start(s32[2,128,128]{2,1,0:T(8,128)S(1)} %collective-permute-done.10.refs_2_), channel_id=1, source_target_pairs={{0,1},{1,0},{2,3},{3,2},{4,5},{5,4},{6,7},{7,6},{8,9},{9,8},{10,11... | collective-permute-start | bytes 393224 | tf_op jit(solution)/shard_map/ppermute | solution.py:59
  28.3 0.1 collective-permute-start.12
  28.4 0.6 %collective-permute-start.15 = (s32[2,128,128]{2,1,0:T(8,128)S(1)}, s32[2,128,128]{2,1,0:T(8,128)S(1)}, u32[]{:S(2)}, u32[]{:S(2)}) collective-permute-start(s32[2,128,128]{2,1,0:T(8,128)S(1)} %copy-done), channel_id=1, source_target_pairs={{0,4},{4,0},{8,12},{12,8},{1,5},{5,1},{9,13},{13,9},{2,6},{6,2},{1... | collective-permute-start | bytes 393224 | tf_op jit(solution)/shard_map/ppermute | solution.py:482
  29.0 2.6 %collective-permute-start.16 = (s32[2,128,128]{2,1,0:T(8,128)S(1)}, s32[2,128,128]{2,1,0:T(8,128)S(1)}, u32[]{:S(2)}, u32[]{:S(2)}) collective-permute-start(s32[2,128,128]{2,1,0:T(8,128)S(1)} %copy-done), channel_id=1, source_target_pairs={{0,12},{4,8},{8,4},{12,0},{1,13},{5,9},{9,5},{13,1},{2,14},{6,10},... | collective-permute-start | bytes 393224 | tf_op jit(solution)/shard_map/ppermute | solution.py:483
  31.6 12.8 %shard_map.74 = f32[4,256,128]{2,1,0:T(8,128)S(1)} custom-call(bf16[2,256,256]{2,1,0:T(8,128)(2,1)S(1)} %get-tuple-element.24.ky, bf16[2,3,256,256]{3,2,1,0:T(8,128)(2,1)S(1)} %get-tuple-element.25.kz, f32[2,8]{1,0:T(2,128)S(1)} %get-tuple-element.26.table, f32[1,256]{1,0:T(1,128)S(1)} %get-tuple-element.27.sheet, ...), custom_call_target="tpu_custom_call" | custom-call | flops 6000000000 | bytes 1048576 | tf_op jit(solution)/shard_map/pallas_call | solution.py:406
  44.5 0.1 collective-permute-start.17
  44.6 1.5 %collective-permute-done.17.other = f32[2,256,128]{2,1,0:T(8,128)S(1)} collective-permute-done((f32[2,256,128]{2,1,0:T(8,128)S(1)}, f32[2,256,128]{2,1,0:T(8,128)S(1)}, u32[]{:S(2)}, u32[]{:S(2)}) %collective-permute-start.17) | collective-permute-done | bytes 262176 | tf_op jit(solution)/shard_map/ppermute | solution.py:59
  46.1 2.2 %shard_map.75 = f32[2,128,128]{2,1,0:T(8,128)} custom-call(f32[2,256,128]{2,1,0:T(8,128)S(1)} %get-tuple-element.38.mine, f32[2,256,128]{2,1,0:T(8,128)S(1)} %collective-permute-done.17.other, f32[16]{0:T(128)} %hbm_bright.1, s32[2,128,128]{2,1,0:T(8,128)} %hbm_labels.1, s32[2,128,128]{2,1,0:T(8,128)S(1)} %collective-permute-done.15.facing, ...), custom_call_target="tpu_custom_call" | custom-call | bytes 1048576 | tf_op jit(solution)/shard_map/pallas_call | solution.py:406
  (18 shorter events, 0.1 us)
Async XLA Ops:
  0.0 7.0 %collective-permute-start.1 = (s32[2,128,128]{2,1,0:T(8,128)}, s32[2,128,128]{2,1,0:T(8,128)S(1)}, u32[]{:S(2)}, u32[]{:S(2)}) collective-permute-start(s32[2,128,128]{2,1,0:T(8,128)} %hbm_mine.1), channel_id=1, source_target_pairs={{0,4},{4,0},{8,12},{12,8},{1,5},{5,1},{9,13},{13,9},{2,6},{6,2},{1... | collective-permute-start | bytes 393224 | tf_op jit(solution)/shard_map/ppermute | solution.py:59
  3.0 8.8 %collective-permute-start.4 = (s32[2,128,128]{2,1,0:T(8,128)}, s32[2,128,128]{2,1,0:T(8,128)S(1)}, u32[]{:S(2)}, u32[]{:S(2)}) collective-permute-start(s32[2,128,128]{2,1,0:T(8,128)} %hbm_mine.1), channel_id=1, source_target_pairs={{0,12},{4,8},{8,4},{12,0},{1,13},{5,9},{9,5},{13,1},{2,14},{6,10},... | collective-permute-start | bytes 393224 | tf_op jit(solution)/shard_map/ppermute | solution.py:59
  5.5 6.3 %collective-permute-start.6 = (s32[2,128,128]{2,1,0:T(8,128)}, s32[2,128,128]{2,1,0:T(8,128)S(1)}, u32[]{:S(2)}, u32[]{:S(2)}) collective-permute-start(s32[2,128,128]{2,1,0:T(8,128)} %hbm_mine.1), channel_id=1, source_target_pairs={{0,2},{1,3},{2,0},{3,1},{4,6},{5,7},{6,4},{7,5},{8,10},{9,11},{10,... | collective-permute-start | bytes 393224 | tf_op jit(solution)/shard_map/ppermute | solution.py:59
  7.0 6.0 %collective-permute-start.2 = (s32[2,128,128]{2,1,0:T(8,128)S(1)}, s32[2,128,128]{2,1,0:T(8,128)S(1)}, u32[]{:S(2)}, u32[]{:S(2)}) collective-permute-start(s32[2,128,128]{2,1,0:T(8,128)S(1)} %collective-permute-done.1.refs_3_), channel_id=1, source_target_pairs={{0,1},{1,0},{2,3},{3,2},{4,5},{5,4},{6,7},{7,6},{8,9},{9,8},{10,11... | collective-permute-start | bytes 393224 | tf_op jit(solution)/shard_map/ppermute | solution.py:59
  11.8 5.0 %collective-permute-start.7 = (s32[2,128,128]{2,1,0:T(8,128)S(1)}, s32[2,128,128]{2,1,0:T(8,128)S(1)}, u32[]{:S(2)}, u32[]{:S(2)}) collective-permute-start(s32[2,128,128]{2,1,0:T(8,128)S(1)} %collective-permute-done.4.refs_1_), channel_id=1, source_target_pairs={{0,4},{4,0},{8,12},{12,8},{1,5},{5,1},{9,13},{13,9},{2,6},{6,2},{1... | collective-permute-start | bytes 393224 | tf_op jit(solution)/shard_map/ppermute | solution.py:59
  12.4 4.9 %collective-permute-start.5 = (s32[2,128,128]{2,1,0:T(8,128)S(1)}, s32[2,128,128]{2,1,0:T(8,128)S(1)}, u32[]{:S(2)}, u32[]{:S(2)}) collective-permute-start(s32[2,128,128]{2,1,0:T(8,128)S(1)} %collective-permute-done.4.refs_1_), channel_id=1, source_target_pairs={{0,1},{1,0},{2,3},{3,2},{4,5},{5,4},{6,7},{7,6},{8,9},{9,8},{10,11... | collective-permute-start | bytes 393224 | tf_op jit(solution)/shard_map/ppermute | solution.py:59
  12.5 6.4 %collective-permute-start = (s32[2,128,128]{2,1,0:T(8,128)}, s32[2,128,128]{2,1,0:T(8,128)S(1)}, u32[]{:S(2)}, u32[]{:S(2)}) collective-permute-start(s32[2,128,128]{2,1,0:T(8,128)} %hbm_mine.1), channel_id=1, source_target_pairs={{0,1},{1,0},{2,3},{3,2},{4,5},{5,4},{6,7},{7,6},{8,9},{9,8},{10,11... | collective-permute-start | bytes 393224 | tf_op jit(solution)/shard_map/ppermute | solution.py:59
  13.0 6.4 %collective-permute-start.3 = (s32[2,128,128]{2,1,0:T(8,128)S(1)}, s32[2,128,128]{2,1,0:T(8,128)S(1)}, u32[]{:S(2)}, u32[]{:S(2)}) collective-permute-start(s32[2,128,128]{2,1,0:T(8,128)S(1)} %collective-permute-done.1.refs_3_), channel_id=1, source_target_pairs={{0,2},{1,3},{2,0},{3,1},{4,6},{5,7},{6,4},{7,5},{8,10},{9,11},{10,... | collective-permute-start | bytes 393224 | tf_op jit(solution)/shard_map/ppermute | solution.py:59
  16.8 2.6 %collective-permute-start.8 = (s32[2,128,128]{2,1,0:T(8,128)S(1)}, s32[2,128,128]{2,1,0:T(8,128)S(1)}, u32[]{:S(2)}, u32[]{:S(2)}) collective-permute-start(s32[2,128,128]{2,1,0:T(8,128)S(1)} %collective-permute-done.7.refs_5_), channel_id=1, source_target_pairs={{0,1},{1,0},{2,3},{3,2},{4,5},{5,4},{6,7},{7,6},{8,9},{9,8},{10,11... | collective-permute-start | bytes 393224 | tf_op jit(solution)/shard_map/ppermute | solution.py:59
  16.8 12.2 %collective-permute-start.9 = (s32[2,128,128]{2,1,0:T(8,128)S(1)}, s32[2,128,128]{2,1,0:T(8,128)S(1)}, u32[]{:S(2)}, u32[]{:S(2)}) collective-permute-start(s32[2,128,128]{2,1,0:T(8,128)S(1)} %collective-permute-done.6.refs_0_), channel_id=1, source_target_pairs={{0,1},{1,0},{2,3},{3,2},{4,5},{5,4},{6,7},{7,6},{8,9},{9,8},{10,11... | collective-permute-start | bytes 393224 | tf_op jit(solution)/shard_map/ppermute | solution.py:59
  17.3 10.5 %collective-permute-start.10 = (s32[2,128,128]{2,1,0:T(8,128)S(1)}, s32[2,128,128]{2,1,0:T(8,128)S(1)}, u32[]{:S(2)}, u32[]{:S(2)}) collective-permute-start(s32[2,128,128]{2,1,0:T(8,128)S(1)} %collective-permute-done.4.refs_1_), channel_id=1, source_target_pairs={{0,2},{1,3},{2,0},{3,1},{4,6},{5,7},{6,4},{7,5},{8,10},{9,11},{10,... | collective-permute-start | bytes 393224 | tf_op jit(solution)/shard_map/ppermute | solution.py:59
  18.8 8.9 %collective-permute-start.13 = (s32[2,128,128]{2,1,0:T(8,128)S(1)}, s32[2,128,128]{2,1,0:T(8,128)S(1)}, u32[]{:S(2)}, u32[]{:S(2)}) collective-permute-start(s32[2,128,128]{2,1,0:T(8,128)S(1)} %collective-permute-done.7.refs_5_), channel_id=1, source_target_pairs={{0,2},{1,3},{2,0},{3,1},{4,6},{5,7},{6,4},{7,5},{8,10},{9,11},{10,... | collective-permute-start | bytes 393224 | tf_op jit(solution)/shard_map/ppermute | solution.py:59
  19.4 9.0 %copy-start = (s32[2,128,128]{2,1,0:T(8,128)S(1)}, s32[2,128,128]{2,1,0:T(8,128)}, u32[]{:S(2)}) copy-start(s32[2,128,128]{2,1,0:T(8,128)} %hbm_labels.1) | copy-start | bytes 393220
  27.7 3.9 %collective-permute-start.14 = (s32[2,128,128]{2,1,0:T(8,128)S(1)}, s32[2,128,128]{2,1,0:T(8,128)S(1)}, u32[]{:S(2)}, u32[]{:S(2)}) collective-permute-start(s32[2,128,128]{2,1,0:T(8,128)S(1)} %collective-permute-done.13.refs_6_), channel_id=1, source_target_pairs={{0,1},{1,0},{2,3},{3,2},{4,5},{5,4},{6,7},{7,6},{8,9},{9,8},{10,11... | collective-permute-start | bytes 393224 | tf_op jit(solution)/shard_map/ppermute | solution.py:59
  27.8 3.8 %collective-permute-start.11 = (s32[2,128,128]{2,1,0:T(8,128)S(1)}, s32[2,128,128]{2,1,0:T(8,128)S(1)}, u32[]{:S(2)}, u32[]{:S(2)}) collective-permute-start(s32[2,128,128]{2,1,0:T(8,128)S(1)} %collective-permute-done.10.refs_2_), channel_id=1, source_target_pairs={{0,1},{1,0},{2,3},{3,2},{4,5},{5,4},{6,7},{7,6},{8,9},{9,8},{10,11... | collective-permute-start | bytes 393224 | tf_op jit(solution)/shard_map/ppermute | solution.py:59
  28.3 3.3 %collective-permute-start.12 = (s32[2,128,128]{2,1,0:T(8,128)S(1)}, s32[2,128,128]{2,1,0:T(8,128)S(1)}, u32[]{:S(2)}, u32[]{:S(2)}) collective-permute-start(s32[2,128,128]{2,1,0:T(8,128)S(1)} %collective-permute-done.3.refs_4_), channel_id=1, source_target_pairs={{0,1},{1,0},{2,3},{3,2},{4,5},{5,4},{6,7},{7,6},{8,9},{9,8},{10,11... | collective-permute-start | bytes 393224 | tf_op jit(solution)/shard_map/ppermute | solution.py:59
  28.4 16.1 %collective-permute-start.15 = (s32[2,128,128]{2,1,0:T(8,128)S(1)}, s32[2,128,128]{2,1,0:T(8,128)S(1)}, u32[]{:S(2)}, u32[]{:S(2)}) collective-permute-start(s32[2,128,128]{2,1,0:T(8,128)S(1)} %copy-done), channel_id=1, source_target_pairs={{0,4},{4,0},{8,12},{12,8},{1,5},{5,1},{9,13},{13,9},{2,6},{6,2},{1... | collective-permute-start | bytes 393224 | tf_op jit(solution)/shard_map/ppermute | solution.py:482
  29.0 15.5 %collective-permute-start.16 = (s32[2,128,128]{2,1,0:T(8,128)S(1)}, s32[2,128,128]{2,1,0:T(8,128)S(1)}, u32[]{:S(2)}, u32[]{:S(2)}) collective-permute-start(s32[2,128,128]{2,1,0:T(8,128)S(1)} %copy-done), channel_id=1, source_target_pairs={{0,12},{4,8},{8,4},{12,0},{1,13},{5,9},{9,5},{13,1},{2,14},{6,10},... | collective-permute-start | bytes 393224 | tf_op jit(solution)/shard_map/ppermute | solution.py:483
  44.5 1.6 %collective-permute-start.17 = (f32[2,256,128]{2,1,0:T(8,128)S(1)}, f32[2,256,128]{2,1,0:T(8,128)S(1)}, u32[]{:S(2)}, u32[]{:S(2)}) collective-permute-start(f32[2,256,128]{2,1,0:T(8,128)S(1)} %get-tuple-element.34), channel_id=1, source_target_pairs={{0,1},{1,0},{2,3},{3,2},{4,5},{5,4},{6,7},{7,6},{8,9},{9,8},{10,11... | collective-permute-start | bytes 786440 | tf_op jit(solution)/shard_map/ppermute | solution.py:59

commit v3 on v2

--- a/solution.py
+++ b/solution.py
@@ -1,4 +1,5 @@
 import functools
+import operator
 
 import jax
 import jax.numpy as jnp
@@ -43,9 +44,10 @@
         return (min(need, self.window * self.units) if self.whole else need) // 2
 
     def start(self, left):
+        left = operator.index(left)
         if self.whole:
-            last = jnp.maximum(self.window * self.units - (self.units + 2 + 2 * left), 0)
-            unit = jnp.clip(lax.axis_index("tile") * self.units - 1 - left, 0, last)
+            last = max(self.window * self.units - (self.units + 2 + 2 * left), 0)
+            unit = 0 if last == 0 else jnp.clip(lax.axis_index("tile") * self.units - 1 - left, 0, last)
         else:
             unit = self.reach * self.units - 1 - left
         return unit * self.half
@@ -68,12 +70,12 @@
     return lax.optimization_barrier((x, *done))[0]
 
 
-def tile_pieces(plan, mine, start, crossed):
+def tile_pieces(plan, mine, crossed):
     if plan.whole and plan.tiles & (plan.tiles - 1) == 0:
         got = {0: mine}
         if plan.tiles == 4:
             got[3] = swap(mine, "tile", 3)
-            got[1] = swap(after(mine, *start), "tile", 1)
+            got[1] = swap(mine, "tile", 1)
             got[2] = swap(after(got[3], *crossed), "tile", 1)
         else:
             for bits in range(1, plan.tiles):
@@ -101,6 +103,10 @@
     return k + plan.reach, (tile + k >= 0) & (tile + k < plan.tiles)
 
 
+def aligned(row, size):
+    return row if isinstance(row, int) else pl.multiple_of(row, size)
+
+
 def halves(x):
     high = x.astype(jnp.bfloat16)
     return high, (x - high.astype(jnp.float32)).astype(jnp.bfloat16)
@@ -135,10 +141,18 @@
     return copies
 
 
-def build_bands(plan, taps, dtaps, phases, positions, ky, kz, by, bz, table, sheet, line):
+def prepare_kernel(plan, count, hbm_taps, hbm_dtaps, hbm_phases, hbm_positions, *refs):
+    joined, refs = refs[:count], refs[count:]
+    ky, kz, km, by, bz, table, sheet, together, taps, dtaps, phases, positions, line, sems = refs
     ny, half, block = plan.ny, plan.half, plan.block
     wide = 2 * block
     count = taps.shape[2]
+    pairs = [(hbm_taps, taps), (hbm_dtaps, dtaps), (hbm_phases, phases), (hbm_positions, positions)]
+    copies = fetch(pairs, sems)
+    for number, piece in enumerate(joined):
+        together[number * plan.planes:(number + 1) * plan.planes] = piece[...]
+    for copy in copies:
+        copy.wait()
 
     def padded(row):
         line[...] = jnp.zeros(line.shape, jnp.float32)
@@ -159,8 +173,21 @@
     czi = band(padded(taps[1, 1:2, :])[:, :wide], block, wide)
     early = complex_matrix(czr[:, :block], -czi[:, :block], czi[:, :block])
     late = complex_matrix(czr[:, block:], -czi[:, block:], czi[:, block:])
-    for number, matrix in enumerate((early, early + late, late)):
-        keep(kz, matrix, (number,))
+    keep(kz, early, (0,))
+    keep(kz, late, (1,))
+    middle = early + late
+    quarter = [
+        [[middle[d:d + half, c + e:c + e + half] for c in (0, block)] for d in (0, block)] for e in (0, half)
+    ]
+    for number, sign in enumerate((1.0, -1.0)):
+        part = jnp.concatenate(
+            [jnp.concatenate([quarter[0][d][c] + sign * quarter[1][d][c] for c in range(2)], axis=1) for d in range(2)],
+            axis=0,
+        )
+        high, low = halves(0.5 * part)
+        km[number] = jnp.concatenate(
+            [jnp.concatenate([high, high], axis=1), jnp.concatenate([low, low], axis=1)], axis=0
+        )
     keep(by, circulant(folded(dtaps[0:1, :]), ny, half))
     keep(bz, band(padded(dtaps[1:2, :])[:, :wide], block, wide))
 
@@ -185,20 +212,21 @@
     return values[0]
 
 
-def look_up(plan, sources, pieces, table, cosine, sine):
+def look_up(plan, groups, pieces, table, cosine, sine):
     cz = plan.cz
     core = plan.here()[2]
     entries = [[table[part:part + 1, e:e + 1] for e in range(table.shape[1])] for part in range(2)]
     for number, piece in pieces:
-        block, valid = block_of(plan, sources[number // plan.cores])
         first = (core ^ (number % plan.cores)) * plan.planes
-        row = pl.multiple_of(block * cz, cz)
-        for plane in range(plan.planes):
-            kind = piece[plane].T
-            for values, target in zip(entries, (cosine, sine)):
-                value = choose(kind, values)
-                value = value if valid is None else jnp.where(valid, value, 0.0)
-                target[first + plane, pl.ds(row, cz), :] = value
+        for place, source in enumerate(groups[number // plan.cores]):
+            block, valid = block_of(plan, source)
+            row = pl.multiple_of(block * cz, cz)
+            for plane in range(plan.planes):
+                kind = piece[place * plan.planes + plane].T
+                for values, target in zip(entries, (cosine, sine)):
+                    value = choose(kind, values)
+                    value = value if valid is None else jnp.where(valid, value, 0.0)
+                    target[first + plane, pl.ds(row, cz), :] = value
 
 
 def enter(plan, sheet, field, spread):
@@ -212,9 +240,10 @@
             ref[d, half + rows:, :] = jnp.zeros((half, plan.width), jnp.float32)
 
 
-def propagate(plan, cos_at, sin_at, left, sources, targets, ky, kz, field, spread):
+def propagate(plan, cos_at, sin_at, left, ky, kz, km, field, spread):
     ny, half, block, sheets = plan.ny, plan.half, plan.block, plan.sheets
     source, target = plan.start(left + 1), plan.start(left)
+    sources, targets = plan.blocks(left + 1), plan.blocks(left)
 
     def each(number, body):
         if plan.whole:
@@ -224,7 +253,7 @@
             lax.fori_loop(0, number, lambda b, _: body(b), None)
 
     def turn(b):
-        row = pl.multiple_of(source + b * block, half)
+        row = aligned(source + b * block, half)
         cos, sin = cos_at(row, block), sin_at(row, block)
         parts = []
         for p in range(sheets):
@@ -243,6 +272,16 @@
         high, low = halves(x)
         return dot(kz[0, number], high) + dot(kz[1, number], high) + dot(kz[0, number], low)
 
+    def circular(x):
+        top = jnp.concatenate([x[:half], x[block:block + half]], axis=0)
+        bottom = jnp.concatenate([x[half:block], x[block + half:]], axis=0)
+        sides = []
+        for number, part in enumerate((top + bottom, top - bottom)):
+            w = dot(km[number], jnp.concatenate(halves(part), axis=0))
+            sides.append(w[:block] + w[block:])
+        top, bottom = sides[0] + sides[1], sides[0] - sides[1]
+        return jnp.concatenate([top[:half], bottom[:half], top[half:], bottom[half:]], axis=0)
+
     def window(row):
         return jnp.concatenate([spread[d, pl.ds(row, block), :] for d in range(2)], axis=0)
 
@@ -251,15 +290,15 @@
         field[1, pl.ds(row + half, block), :] = w[block:]
 
     def pair(b):
-        row = pl.multiple_of(target + 2 * b * block, half)
+        row = aligned(target + 2 * b * block, half)
         x = [window(row + i * block) for i in range(3)]
-        middle = product(1, x[1])
-        store(row, product(0, x[0] - x[1]) + middle)
-        store(row + block, product(2, x[2] - x[1]) + middle)
+        shared = circular(x[1])
+        store(row, product(0, x[0] - x[1]) + shared)
+        store(row + block, product(1, x[2] - x[1]) + shared)
 
     def single(b):
-        row = pl.multiple_of(target + b * block, half)
-        store(row, product(0, window(row)) + product(2, window(row + block)))
+        row = aligned(target + b * block, half)
+        store(row, product(0, window(row)) + product(1, window(row + block)))
 
     each(sources, turn)
     each(targets // 2, pair)
@@ -278,77 +317,62 @@
     return total
 
 
-def steps_of(plan, begin, end, step, total):
-    def shape(k):
-        return plan.blocks(total - k), plan.blocks(total - 1 - k)
-
-    k = begin
-    while k < end:
-        last = k + 1
-        while last < end and shape(last) == shape(k):
-            last += 1
-        lax.fori_loop(k, last, lambda i, _, s=shape(k): step(i, *s), None)
-        k = last
-
-
-def short_kernel(plan, sources, hbm_taps, hbm_dtaps, hbm_phases, hbm_positions, hbm_mine, *refs):
-    count = len(sources) * plan.cores - 1
+def short_kernel(plan, groups, hbm_mine, ky, kz, km, table, sheet, *refs):
+    count = len(groups) * plan.cores - 1
     pieces = refs[:count]
-    out, ky, kz, by, bz, table, sheet, hbm_cosine, hbm_sine = refs[count:count + 9]
-    taps, dtaps, phases, positions, mine, cosine, sine, field, spread, line, sems = refs[count + 9:]
-    pairs = [(hbm_phases, phases), (hbm_positions, positions), (hbm_taps, taps), (hbm_dtaps, dtaps)]
-    *small, arriving = fetch([*pairs, (hbm_mine, mine)], sems)
-    for copy in small:
-        copy.wait()
-    build_bands(plan, taps, dtaps, phases, positions, ky, kz, by, bz, table, sheet, line)
+    out, hbm_cosine, hbm_sine, mine, cosine, sine, field, spread, sems = refs[count:]
     own = plan.own
+    (arriving,) = fetch([(hbm_mine, mine)], sems)
     enter(plan, sheet, field, spread)
-    look_up(plan, sources, list(enumerate(pieces, 1)), table, cosine, sine)
+    look_up(plan, groups, list(enumerate(pieces, 1)), table, cosine, sine)
     arriving.wait()
-    look_up(plan, sources, [(0, mine)], table, cosine, sine)
+    look_up(plan, groups, [(0, mine)], table, cosine, sine)
     leaving = fetch([(cosine, hbm_cosine), (sine, hbm_sine)], sems)
     side = plan.here()[1]
 
-    def step(k, reads, writes):
+    def step(k, left):
         slot = jnp.where(side == 0, k, own - 1 - k)
         maps = [lambda row, n, ref=ref: ref[slot, pl.ds(row, n), :] for ref in (cosine, sine)]
-        propagate(plan, *maps, own - 1 - k, reads, writes, ky, kz, field, spread)
+        propagate(plan, *maps, left, ky, kz, km, field, spread)
         out[slot] = energy(plan, field)
 
-    steps_of(plan, 0, own, step, own)
+    for k in range(own):
+        step(k, own - 1 - k)
     for copy in leaving:
         copy.wait()
 
 
-def long_kernel(plan, sources, ky, kz, table, sheet, hbm_cosine, hbm_sine, earlier, *refs):
-    count = len(sources) * plan.cores
+def long_kernel(plan, groups, ky, kz, km, table, sheet, hbm_cosine, hbm_sine, earlier, *refs):
+    count = len(groups) * plan.cores
     pieces = refs[:count]
     out, far_cosine, far_sine, cosine, sine, field, spread, sems = refs[count:]
     own = plan.own
     arriving = fetch([(hbm_cosine, cosine), (hbm_sine, sine)], sems)
     enter(plan, sheet, field, spread)
-    look_up(plan, sources, list(enumerate(pieces)), table, far_cosine, far_sine)
+    look_up(plan, groups, list(enumerate(pieces)), table, far_cosine, far_sine)
     side = plan.here()[1]
 
-    def far_step(k, reads, writes):
+    def far_step(k, left):
         slot = jnp.where(side == 0, own - 1 - k, k)
         maps = [lambda row, n, ref=ref: ref[slot, pl.ds(row, n), :] for ref in (far_cosine, far_sine)]
-        propagate(plan, *maps, 2 * own - 1 - k, reads, writes, ky, kz, field, spread)
-
-    def step(k, reads, writes):
+        propagate(plan, *maps, left, ky, kz, km, field, spread)
+
+    def step(k, left):
         slot = jnp.where(side == 0, 2 * own - 1 - k, k - own)
         maps = [lambda row, n, ref=ref: ref[slot, pl.ds(row, n), :] for ref in (cosine, sine)]
-        propagate(plan, *maps, 2 * own - 1 - k, reads, writes, ky, kz, field, spread)
+        propagate(plan, *maps, left, ky, kz, km, field, spread)
         out[slot] = earlier[slot] + energy(plan, field)
 
-    steps_of(plan, 0, own, far_step, 2 * own)
+    for k in range(own):
+        far_step(k, 2 * own - 1 - k)
     for copy in arriving:
         copy.wait()
-    steps_of(plan, own, 2 * own, step, 2 * own)
-
-
-def blur_kernel(plan, mine, other, hbm_bright, hbm_labels, facing, beyond, by, bz, out, bright, labels, sems):
-    half, ny, extent = plan.half, plan.ny, plan.extent
+    for k in range(own, 2 * own):
+        step(k, 2 * own - 1 - k)
+
+
+def weight_kernel(plan, hbm_bright, hbm_labels, facing, beyond, weight, bright, labels, sems):
+    half, ny, cz = plan.half, plan.ny, plan.cz
     first, arriving = fetch([(hbm_bright, bright), (hbm_labels, labels)], sems)
     first.wait()
     tile = lax.axis_index("tile")
@@ -357,21 +381,24 @@
     ends = [(tile < plan.tiles - 1).astype(jnp.float32), (tile > 0).astype(jnp.float32)]
     inside = jnp.where(first_half, ends[0], ends[1])
     values = [bright[e] for e in range(bright.shape[0])]
-    halos = []
     for x in range(plan.planes):
         before = jnp.where(even, beyond[x], facing[x])[:, -2 * half:]
         behind = jnp.where(even, facing[x], beyond[x])[:, :2 * half]
-        halos.append((choose(jnp.where(first_half, behind, before), values) * inside).T)
+        halo = (choose(jnp.where(first_half, behind, before), values) * inside).T
+        weight[x, :half, :] = halo[half:]
+        weight[x, half + cz:, :] = halo[:half]
     arriving.wait()
-    parts = []
     for x in range(plan.planes):
-        weight = jnp.concatenate([halos[x][half:], choose(labels[x], values).T, halos[x][:half]], axis=0)
-        parts.append((mine[x] + other[x]) * weight)
+        weight[x, half:half + cz, :] = choose(labels[x], values).T
+
+
+def blur_kernel(plan, mine, other, weight, by, bz, out):
+    ny, extent, block = plan.ny, plan.extent, plan.block
+    parts = [(mine[x] + other[x]) * weight[x] for x in range(plan.planes)]
     high, low = halves(jnp.concatenate(parts, axis=0))
     v = three(high, low, by[0], by[1])
     v = jnp.concatenate([v[x * extent:(x + 1) * extent] for x in range(plan.planes)], axis=1)
     high, low = halves(v)
-    block = plan.block
     for b in range(plan.cz // block):
         rows = slice(b * block, b * block + 2 * block)
         w = dot(bz[0], high[rows]) + dot(bz[1], high[rows]) + dot(bz[0], low[rows])
@@ -427,52 +454,58 @@
         return [array] + [swap(array, "sect", bits) for bits in range(1, cores)]
 
     crossed = [swap(classes, "sect", cores)]
-    pieces, sources = tile_pieces(plan, classes, (), crossed)
-    near = []
-    for number, piece in enumerate(pieces):
-        shared = over_cores(piece)
-        near += shared
-        if number:
-            hold = number < len(pieces) - 1
-            crossed.append(swap(after(piece, *shared[1:]) if hold else piece, "sect", cores))
-
-    maps = shape((plan.own, rows, ny), f32)
-    whole_maps = pltpu.VMEM((plan.own, rows, ny), f32)
-    state = pltpu.VMEM((2, rows + 2 * half, plan.width), f32)
-    sums = shape((plan.own, plan.extent, ny), f32)
+    pieces, sources = tile_pieces(plan, classes, crossed)
+    joined = pieces[1:-1]
+    groups = (sources[:1], sources[1:-1], sources[-1:])
     line = -(-max(4 * half, taps) // ny) * ny
     phases = phase_table[None]
-    near[1] = after(near[1], crossed[len(crossed) // 2])
-    sums, ky, kz, by, bz, table, sheet, cosine, sine = call(
-        functools.partial(short_kernel, plan, sources),
+    ky, kz, km, by, bz, table, sheet, together = call(
+        functools.partial(prepare_kernel, plan, len(joined)),
         (
-            sums,
             shape((2, 2 * ny, 2 * ny), bf16),
-            shape((2, 3, 2 * block, 2 * block), bf16),
+            shape((2, 2, 2 * block, 2 * block), bf16),
+            shape((2, 2 * block, 2 * block), bf16),
             shape((2, ny, ny), bf16),
             shape((2, block, 2 * block), bf16),
             shape((2, phases.shape[1]), f32),
             shape((1, plan.width), f32),
-            maps,
-            maps,
+            shape((len(joined) * plan.planes, ny, plan.cz), classes.dtype),
         ),
-        [HBM] * 5 + [VMEM] * (len(near) - 1),
+        [HBM] * 4 + [VMEM] * len(joined),
         [
             pltpu.VMEM(prop_taps.shape, f32),
             pltpu.VMEM(detect_taps.shape, f32),
             pltpu.VMEM(phases.shape, f32),
             pltpu.SMEM(positions.shape, positions.dtype),
+            pltpu.VMEM((8, line), f32),
+            pltpu.SemaphoreType.DMA((4,)),
+        ],
+    )(prop_taps, detect_taps, phases, positions, *joined)
+    near = []
+    for number, piece in enumerate((classes, together, pieces[-1])):
+        near += over_cores(piece)
+        if number:
+            crossed.append(swap(piece, "sect", cores))
+
+    maps = shape((plan.own, rows, ny), f32)
+    whole_maps = pltpu.VMEM((plan.own, rows, ny), f32)
+    state = pltpu.VMEM((2, rows + 2 * half, plan.width), f32)
+    sums = shape((plan.own, plan.extent, ny), f32)
+    sums, cosine, sine = call(
+        functools.partial(short_kernel, plan, groups),
+        (sums, maps, maps),
+        [HBM] + [VMEM] * (4 + len(near)),
+        [
             pltpu.VMEM(classes.shape, classes.dtype),
             whole_maps,
             whole_maps,
             state,
             state,
-            pltpu.VMEM((8, line), f32),
-            pltpu.SemaphoreType.DMA((5,)),
+            pltpu.SemaphoreType.DMA((2,)),
         ],
         flops=3 * 10**9,
-        out_spaces=(VMEM,) * 7 + (HBM,) * 2,
-    )(prop_taps, detect_taps, phases, positions, *near)
+        out_spaces=(VMEM, HBM, HBM),
+    )(near[0], ky, kz, km, table, sheet, *near[1:])
 
     pairs = [(i, i ^ 1) for i in range(tiles) if i ^ 1 < tiles]
     gaps = [(i, ((i + 1) ^ 1) - 1) for i in range(1, tiles) if ((i + 1) ^ 1) - 1 < tiles]
@@ -483,16 +516,15 @@
     beyond = lax.ppermute(late, "tile", gaps)
 
     far = []
-    for number, piece in enumerate(crossed):
-        last = number == len(crossed) - 1
-        far += [piece] + over_cores(after(piece, sums) if last else piece)[1:]
+    for piece in crossed:
+        far += [piece] + over_cores(after(piece, sums))[1:]
     sums = call(
-        functools.partial(long_kernel, plan, sources),
+        functools.partial(long_kernel, plan, groups),
         shape((plan.own, plan.extent, ny), f32),
-        [VMEM] * 4 + [HBM] * 2 + [VMEM] * (1 + len(far)),
+        [VMEM] * 5 + [HBM] * 2 + [VMEM] * (1 + len(far)),
         [whole_maps] * 4 + [state, state, pltpu.SemaphoreType.DMA((2,))],
         flops=6 * 10**9,
-    )(ky, kz, table, sheet, cosine, sine, sums, *far)
+    )(ky, kz, km, table, sheet, cosine, sine, sums, *far)
 
     parts = sums.reshape(cores, plan.planes, plan.extent, ny)
     mine = lax.dynamic_index_in_dim(parts, core, 0, keepdims=False)
@@ -502,16 +534,21 @@
         arrived = swap(after(leaving, facing, beyond), "sect", bits)
         other = arrived if other is None else other + arrived
     other = jnp.zeros_like(mine) if other is None else other
-    return call(
-        functools.partial(blur_kernel, plan),
-        shape((plan.planes, ny, plan.cz), f32),
-        [VMEM] * 2 + [HBM] * 2 + [VMEM] * 4,
+    weight = call(
+        functools.partial(weight_kernel, plan),
+        shape((plan.planes, plan.extent, ny), f32),
+        [HBM] * 2 + [VMEM] * 2,
         [
             pltpu.SMEM(brightness.shape, f32),
             pltpu.VMEM(labels.shape, labels.dtype),
             pltpu.SemaphoreType.DMA((2,)),
         ],
-    )(mine, other, brightness, labels, facing, beyond, by, bz)
+    )(brightness, labels, facing, beyond)
+    return call(
+        functools.partial(blur_kernel, plan),
+        shape((plan.planes, ny, plan.cz), f32),
+        [VMEM] * 5,
+    )(mine, other, weight, by, bz)
 
 
 def solution(mesh):

time: 48.5 us -> 43.7 us (0.901)
  starting transfers between devices: 16.1 us -> 14.3 us
  Pallas kernels: 23.4 us -> 21.7 us
  waiting for transfers between devices: 8.75 us -> 7.32 us
    ppermute x16 -> x13, starting transfers between devices: 12.9 us -> 11 us  [swap(): return lax.ppermute(x, axis, [(i, i ^ bits) for i in range(count)])]
    pallas_call x3 -> x5, Pallas kernels: 23.4 us -> 21.7 us  [call_with(): pl.pallas_call(kernel, out_shape=outs, in_specs=[pl.BlockSpec(memory_spac...]
    ppermute x16 -> x13, waiting for transfers between devices: 8.75 us -> 7.31 us  [swap(): return lax.ppermute(x, axis, [(i, i ^ bits) for i in range(count)])]
  transfers between devices with their start and end apart: 18 -> 15, of which waited for: 3 -> 6; matrix products, arithmetic and copies ran while one was open for 0% -> 0% of each run, Pallas kernels for 44% -> 47%
where the time goes in v3:
time: 43.7 us; the launch traced here: 43.5 us
  Pallas kernels  21.7 us (50%)
  starting transfers between devices  14.3 us (33%)
  waiting for transfers between devices  7.32 us (17%)
    pallas_call x5, Pallas kernels, call_with(): pl.pallas_call(kernel, out_shape=outs, in_specs=[pl.BlockSpec(memory_spac...  21.7 us
    ppermute x13, starting transfers between devices, swap(): return lax.ppermute(x, axis, [(i, i ^ bits) for i in range(count)])  11 us
    ppermute x13, waiting for transfers between devices, swap(): return lax.ppermute(x, axis, [(i, i ^ bits) for i in range(count)])  7.31 us
    ppermute x1, starting transfers between devices, on_device(): beyond = lax.ppermute(late, 'tile', gaps)  2.24 us
    ppermute x1, starting transfers between devices, on_device(): facing = lax.ppermute(late, 'tile', pairs)  1.06 us
  transfers between devices with their start and end apart: 15, of which 6 were waited for; matrix products, arithmetic and copies ran while one was open for 0% of the time, Pallas kernels for 47%

profile of v3, /device:TPU:0, one launch (start us, length us, event | category | flops | bytes accessed | tf_op | source)
XLA Modules:
  0.0 43.5 jit_solution(8891343567880494295)
XLA Ops:
  0.0 5.0 %collective-permute-start = (s32[2,128,128]{2,1,0:T(8,128)}, s32[2,128,128]{2,1,0:T(8,128)S(1)}, u32[]{:S(2)}, u32[]{:S(2)}) collective-permute-start(s32[2,128,128]{2,1,0:T(8,128)} %hbm_mine.1), channel_id=1, source_target_pairs={{0,12},{4,8},{8,4},{12,0},{1,13},{5,9},{9,5},{13,1},{2,14},{6,10},... | collective-permute-start | bytes 393224 | tf_op jit(solution)/shard_map/ppermute | solution.py:61
  5.0 1.5 %collective-permute-start.4 = (s32[2,128,128]{2,1,0:T(8,128)}, s32[2,128,128]{2,1,0:T(8,128)S(1)}, u32[]{:S(2)}, u32[]{:S(2)}) collective-permute-start(s32[2,128,128]{2,1,0:T(8,128)} %hbm_mine.1), channel_id=1, source_target_pairs={{0,2},{1,3},{2,0},{3,1},{4,6},{5,7},{6,4},{7,5},{8,10},{9,11},{10,... | collective-permute-start | bytes 393224 | tf_op jit(solution)/shard_map/ppermute | solution.py:61
  6.5 3.1 %collective-permute-done.refs_0_ = s32[2,128,128]{2,1,0:T(8,128)S(1)} collective-permute-done((s32[2,128,128]{2,1,0:T(8,128)}, s32[2,128,128]{2,1,0:T(8,128)S(1)}, u32[]{:S(2)}, u32[]{:S(2)}) %collective-permute-start) | collective-permute-done | bytes 131104 | tf_op jit(solution)/shard_map/ppermute | solution.py:61
  9.6 0.6 %collective-permute-done.4.refs_0_ = s32[2,128,128]{2,1,0:T(8,128)S(1)} collective-permute-done((s32[2,128,128]{2,1,0:T(8,128)}, s32[2,128,128]{2,1,0:T(8,128)S(1)}, u32[]{:S(2)}, u32[]{:S(2)}) %collective-permute-start.4) | collective-permute-done | bytes 131104 | tf_op jit(solution)/shard_map/ppermute | solution.py:61
  10.2 1.1 %collective-permute-start.5 = (s32[2,128,128]{2,1,0:T(8,128)S(1)}, s32[2,128,128]{2,1,0:T(8,128)S(1)}, u32[]{:S(2)}, u32[]{:S(2)}) collective-permute-start(s32[2,128,128]{2,1,0:T(8,128)S(1)} %collective-permute-done.refs_0_), channel_id=1, source_target_pairs={{0,4},{4,0},{8,12},{12,8},{1,5},{5,1},{9,13},{13,9},{2,6},{6,2},{1... | collective-permute-start | bytes 393224 | tf_op jit(solution)/shard_map/ppermute | solution.py:61
  11.3 1.0 %collective-permute-done.1.refs_1_ = s32[2,128,128]{2,1,0:T(8,128)S(1)} collective-permute-done((s32[2,128,128]{2,1,0:T(8,128)}, s32[2,128,128]{2,1,0:T(8,128)S(1)}, u32[]{:S(2)}, u32[]{:S(2)}) %collective-permute-start.1) | collective-permute-done | bytes 131104 | tf_op jit(solution)/shard_map/ppermute | solution.py:61
  12.3 1.5 %shard_map.73 = (bf16[2,256,256]{2,1,0:T(8,128)(2,1)S(1)}, bf16[2,2,256,256]{3,2,1,0:T(8,128)(2,1)S(1)}, bf16[2,256,256]{2,1,0:T(8,128)(2,1)S(1)}, bf16[2,128,12...) custom-call(f32[2,2,129]{2,1,0:T(2,128)} %hbm_taps.1, ...), custom_call_target="tpu_custom_call" | custom-call | bytes 1048576 | tf_op jit(solution)/shard_map/pallas_call | solution.py:433
  13.8 0.1 collective-permute-start.3
  13.9 0.5 %collective-permute-start.2 = (s32[2,128,128]{2,1,0:T(8,128)S(1)}, s32[2,128,128]{2,1,0:T(8,128)S(1)}, u32[]{:S(2)}, u32[]{:S(2)}) collective-permute-start(s32[2,128,128]{2,1,0:T(8,128)S(1)} %copy-done.1), channel_id=1, source_target_pairs={{0,1},{1,0},{2,3},{3,2},{4,5},{5,4},{6,7},{7,6},{8,9},{9,8},{10,11... | collective-permute-start | bytes 393224 | tf_op jit(solution)/shard_map/ppermute | solution.py:61
  14.4 0.8 %collective-permute-done.5.refs_3_ = s32[2,128,128]{2,1,0:T(8,128)S(1)} collective-permute-done((s32[2,128,128]{2,1,0:T(8,128)S(1)}, s32[2,128,128]{2,1,0:T(8,128)S(1)}, u32[]{:S(2)}, u32[]{:S(2)}) %collective-permute-start.5) | collective-permute-done | bytes 131104 | tf_op jit(solution)/shard_map/ppermute | solution.py:61
  15.2 1.5 %collective-permute-start.8 = (s32[4,128,128]{2,1,0:T(8,128)S(1)}, s32[4,128,128]{2,1,0:T(8,128)S(1)}, u32[]{:S(2)}, u32[]{:S(2)}) collective-permute-start(s32[4,128,128]{2,1,0:T(8,128)S(1)} %get-tuple-element.27.refs_1_), channel_id=1, source_target_pairs={{0,2},{1,3},{2,0},{3,1},{4,6},{5,7},{6,4},{7,5},{8,10},{9,11},{10,... | collective-permute-start | bytes 786440 | tf_op jit(solution)/shard_map/ppermute | solution.py:61
  16.7 0.5 %collective-permute-start.10 = (s32[2,128,128]{2,1,0:T(8,128)S(1)}, s32[2,128,128]{2,1,0:T(8,128)S(1)}, u32[]{:S(2)}, u32[]{:S(2)}) collective-permute-start(s32[2,128,128]{2,1,0:T(8,128)S(1)} %collective-permute-done.5.refs_3_), channel_id=1, source_target_pairs={{0,2},{1,3},{2,0},{3,1},{4,6},{5,7},{6,4},{7,5},{8,10},{9,11},{10,... | collective-permute-start | bytes 393224 | tf_op jit(solution)/shard_map/ppermute | solution.py:61
  17.2 0.0 copy-start
  17.3 7.4 %shard_map.74 = (f32[4,256,128]{2,1,0:T(8,128)S(1)}, f32[4,512,128]{2,1,0:T(8,128)}, f32[4,512,128]{2,1,0:T(8,128)}) custom-call(s32[2,128,128]{2,1,0:T(8,128)} %hbm_mine.1, bf16[2,256,256]{2,1,0:T(8,128)(2,1)S(1)} %get-tuple-element.22.ky, bf16[2,2,256,256]{3,2,1,0:T(8,128)(2,1)S(1)} %get-tuple-element.23.kz, ...), custom_call_target="tpu_custom_call" | custom-call | flops 3000000000 | bytes 1048576 | tf_op jit(solution)/shard_map/pallas_call | solution.py:433
  24.7 0.1 collective-permute-start.9
  24.7 0.5 %collective-permute-start.7 = (s32[2,128,128]{2,1,0:T(8,128)S(1)}, s32[2,128,128]{2,1,0:T(8,128)S(1)}, u32[]{:S(2)}, u32[]{:S(2)}) collective-permute-start(s32[2,128,128]{2,1,0:T(8,128)S(1)} %collective-permute-done.4.refs_0_), channel_id=1, source_target_pairs={{0,1},{1,0},{2,3},{3,2},{4,5},{5,4},{6,7},{7,6},{8,9},{9,8},{10,11... | collective-permute-start | bytes 393224 | tf_op jit(solution)/shard_map/ppermute | solution.py:61
  25.2 1.5 %collective-permute-done.10.refs_4_ = s32[2,128,128]{2,1,0:T(8,128)S(1)} collective-permute-done((s32[2,128,128]{2,1,0:T(8,128)S(1)}, s32[2,128,128]{2,1,0:T(8,128)S(1)}, u32[]{:S(2)}, u32[]{:S(2)}) %collective-permute-start.10) | collective-permute-done | bytes 131104 | tf_op jit(solution)/shard_map/ppermute | solution.py:61
  26.7 1.1 %collective-permute-start.12 = (s32[2,128,128]{2,1,0:T(8,128)S(1)}, s32[2,128,128]{2,1,0:T(8,128)S(1)}, u32[]{:S(2)}, u32[]{:S(2)}) collective-permute-start(s32[2,128,128]{2,1,0:T(8,128)S(1)} %copy-done), channel_id=1, source_target_pairs={{0,4},{4,0},{8,12},{12,8},{1,5},{5,1},{9,13},{13,9},{2,6},{6,2},{1... | collective-permute-start | bytes 393224 | tf_op jit(solution)/shard_map/ppermute | solution.py:515
  27.8 2.2 %collective-permute-start.13 = (s32[2,128,128]{2,1,0:T(8,128)S(1)}, s32[2,128,128]{2,1,0:T(8,128)S(1)}, u32[]{:S(2)}, u32[]{:S(2)}) collective-permute-start(s32[2,128,128]{2,1,0:T(8,128)S(1)} %copy-done), channel_id=1, source_target_pairs={{0,12},{4,8},{8,4},{12,0},{1,13},{5,9},{9,5},{13,1},{2,14},{6,10},... | collective-permute-start | bytes 393224 | tf_op jit(solution)/shard_map/ppermute | solution.py:516
  30.0 10.5 %shard_map.75 = f32[4,256,128]{2,1,0:T(8,128)S(1)} custom-call(bf16[2,256,256]{2,1,0:T(8,128)(2,1)S(1)} %get-tuple-element.22.ky, bf16[2,2,256,256]{3,2,1,0:T(8,128)(2,1)S(1)} %get-tuple-element.23.kz, bf16[2,256,256]{2,1,0:T(8,128)(2,1)S(1)} %get-tuple-element.24.km, f32[2,8]{1,0:T(2,128)S(1)} %get-tuple-element.25.table, ...), custom_call_target="tpu_custom_call" | custom-call | flops 6000000000 | bytes 1048576 | tf_op jit(solution)/shard_map/pallas_call | solution.py:433
  40.7 0.2 collective-permute-start.14
  40.9 1.1 %shard_map.76.weight = f32[2,256,128]{2,1,0:T(8,128)S(1)} custom-call(f32[16]{0:T(128)} %hbm_bright.1, s32[2,128,128]{2,1,0:T(8,128)} %hbm_labels.1, s32[2,128,128]{2,1,0:T(8,128)S(1)} %collective-permute-done.12.facing, s32[2,128,128]{2,1,0:T(8,128)S(1)} %collective-permute-done.13.beyond), custom_call_target="tpu_custom_call" | custom-call | bytes 1048576 | tf_op jit(solution)/shard_map/pallas_call | solution.py:433
  42.0 0.3 collective-permute-done.14.other
  42.3 1.2 %shard_map.77 = f32[2,128,128]{2,1,0:T(8,128)} custom-call(f32[2,256,128]{2,1,0:T(8,128)S(1)} %get-tuple-element.40.mine, f32[2,256,128]{2,1,0:T(8,128)S(1)} %collective-permute-done.14.other, f32[2,256,128]{2,1,0:T(8,128)S(1)} %shard_map.76.weight, bf16[2,128,128]{2,1,0:T(8,128)(2,1)S(1)} %get-tuple-element.37.by, bf16[2,128,256]{2,1,0:T(8,128)(2,1)S(1)} %get-tuple-element.38.bz), custom_call_target="tpu_custom_call" | custom-call | bytes 1048576 | tf_op jit(solution)/shard_map/pallas_call | solution.py:433
  (16 shorter events, 0.1 us)
Async XLA Ops:
  0.0 9.6 %collective-permute-start = (s32[2,128,128]{2,1,0:T(8,128)}, s32[2,128,128]{2,1,0:T(8,128)S(1)}, u32[]{:S(2)}, u32[]{:S(2)}) collective-permute-start(s32[2,128,128]{2,1,0:T(8,128)} %hbm_mine.1), channel_id=1, source_target_pairs={{0,12},{4,8},{8,4},{12,0},{1,13},{5,9},{9,5},{13,1},{2,14},{6,10},... | collective-permute-start | bytes 393224 | tf_op jit(solution)/shard_map/ppermute | solution.py:61
  5.0 5.2 %collective-permute-start.4 = (s32[2,128,128]{2,1,0:T(8,128)}, s32[2,128,128]{2,1,0:T(8,128)S(1)}, u32[]{:S(2)}, u32[]{:S(2)}) collective-permute-start(s32[2,128,128]{2,1,0:T(8,128)} %hbm_mine.1), channel_id=1, source_target_pairs={{0,2},{1,3},{2,0},{3,1},{4,6},{5,7},{6,4},{7,5},{8,10},{9,11},{10,... | collective-permute-start | bytes 393224 | tf_op jit(solution)/shard_map/ppermute | solution.py:61
  6.5 5.8 %collective-permute-start.1 = (s32[2,128,128]{2,1,0:T(8,128)}, s32[2,128,128]{2,1,0:T(8,128)S(1)}, u32[]{:S(2)}, u32[]{:S(2)}) collective-permute-start(s32[2,128,128]{2,1,0:T(8,128)} %hbm_mine.1), channel_id=1, source_target_pairs={{0,4},{4,0},{8,12},{12,8},{1,5},{5,1},{9,13},{13,9},{2,6},{6,2},{1... | collective-permute-start | bytes 393224 | tf_op jit(solution)/shard_map/ppermute | solution.py:61
  10.2 5.0 %collective-permute-start.5 = (s32[2,128,128]{2,1,0:T(8,128)S(1)}, s32[2,128,128]{2,1,0:T(8,128)S(1)}, u32[]{:S(2)}, u32[]{:S(2)}) collective-permute-start(s32[2,128,128]{2,1,0:T(8,128)S(1)} %collective-permute-done.refs_0_), channel_id=1, source_target_pairs={{0,4},{4,0},{8,12},{12,8},{1,5},{5,1},{9,13},{13,9},{2,6},{6,2},{1... | collective-permute-start | bytes 393224 | tf_op jit(solution)/shard_map/ppermute | solution.py:61
  12.3 1.6 %copy-start.1 = (s32[2,128,128]{2,1,0:T(8,128)S(1)}, s32[2,128,128]{2,1,0:T(8,128)}, u32[]{:S(2)}) copy-start(s32[2,128,128]{2,1,0:T(8,128)} %hbm_mine.1) | copy-start | bytes 393220
  13.8 3.4 %collective-permute-start.3 = (s32[4,128,128]{2,1,0:T(8,128)S(1)}, s32[4,128,128]{2,1,0:T(8,128)S(1)}, u32[]{:S(2)}, u32[]{:S(2)}) collective-permute-start(s32[4,128,128]{2,1,0:T(8,128)S(1)} %get-tuple-element.27.refs_1_), channel_id=1, source_target_pairs={{0,1},{1,0},{2,3},{3,2},{4,5},{5,4},{6,7},{7,6},{8,9},{9,8},{10,11... | collective-permute-start | bytes 786440 | tf_op jit(solution)/shard_map/ppermute | solution.py:61
  13.9 3.3 %collective-permute-start.2 = (s32[2,128,128]{2,1,0:T(8,128)S(1)}, s32[2,128,128]{2,1,0:T(8,128)S(1)}, u32[]{:S(2)}, u32[]{:S(2)}) collective-permute-start(s32[2,128,128]{2,1,0:T(8,128)S(1)} %copy-done.1), channel_id=1, source_target_pairs={{0,1},{1,0},{2,3},{3,2},{4,5},{5,4},{6,7},{7,6},{8,9},{9,8},{10,11... | collective-permute-start | bytes 393224 | tf_op jit(solution)/shard_map/ppermute | solution.py:61
  15.2 2.0 %collective-permute-start.6 = (s32[2,128,128]{2,1,0:T(8,128)S(1)}, s32[2,128,128]{2,1,0:T(8,128)S(1)}, u32[]{:S(2)}, u32[]{:S(2)}) collective-permute-start(s32[2,128,128]{2,1,0:T(8,128)S(1)} %collective-permute-done.5.refs_3_), channel_id=1, source_target_pairs={{0,1},{1,0},{2,3},{3,2},{4,5},{5,4},{6,7},{7,6},{8,9},{9,8},{10,11... | collective-permute-start | bytes 393224 | tf_op jit(solution)/shard_map/ppermute | solution.py:61
  15.2 9.5 %collective-permute-start.8 = (s32[4,128,128]{2,1,0:T(8,128)S(1)}, s32[4,128,128]{2,1,0:T(8,128)S(1)}, u32[]{:S(2)}, u32[]{:S(2)}) collective-permute-start(s32[4,128,128]{2,1,0:T(8,128)S(1)} %get-tuple-element.27.refs_1_), channel_id=1, source_target_pairs={{0,2},{1,3},{2,0},{3,1},{4,6},{5,7},{6,4},{7,5},{8,10},{9,11},{10,... | collective-permute-start | bytes 786440 | tf_op jit(solution)/shard_map/ppermute | solution.py:61
  16.7 10.0 %collective-permute-start.10 = (s32[2,128,128]{2,1,0:T(8,128)S(1)}, s32[2,128,128]{2,1,0:T(8,128)S(1)}, u32[]{:S(2)}, u32[]{:S(2)}) collective-permute-start(s32[2,128,128]{2,1,0:T(8,128)S(1)} %collective-permute-done.5.refs_3_), channel_id=1, source_target_pairs={{0,2},{1,3},{2,0},{3,1},{4,6},{5,7},{6,4},{7,5},{8,10},{9,11},{10,... | collective-permute-start | bytes 393224 | tf_op jit(solution)/shard_map/ppermute | solution.py:61
  17.2 9.5 %copy-start = (s32[2,128,128]{2,1,0:T(8,128)S(1)}, s32[2,128,128]{2,1,0:T(8,128)}, u32[]{:S(2)}) copy-start(s32[2,128,128]{2,1,0:T(8,128)} %hbm_labels.1) | copy-start | bytes 393220
  24.7 5.4 %collective-permute-start.9 = (s32[4,128,128]{2,1,0:T(8,128)S(1)}, s32[4,128,128]{2,1,0:T(8,128)S(1)}, u32[]{:S(2)}, u32[]{:S(2)}) collective-permute-start(s32[4,128,128]{2,1,0:T(8,128)S(1)} %collective-permute-done.8.refs_2_), channel_id=1, source_target_pairs={{0,1},{1,0},{2,3},{3,2},{4,5},{5,4},{6,7},{7,6},{8,9},{9,8},{10,11... | collective-permute-start | bytes 786440 | tf_op jit(solution)/shard_map/ppermute | solution.py:61
  24.7 5.3 %collective-permute-start.7 = (s32[2,128,128]{2,1,0:T(8,128)S(1)}, s32[2,128,128]{2,1,0:T(8,128)S(1)}, u32[]{:S(2)}, u32[]{:S(2)}) collective-permute-start(s32[2,128,128]{2,1,0:T(8,128)S(1)} %collective-permute-done.4.refs_0_), channel_id=1, source_target_pairs={{0,1},{1,0},{2,3},{3,2},{4,5},{5,4},{6,7},{7,6},{8,9},{9,8},{10,11... | collective-permute-start | bytes 393224 | tf_op jit(solution)/shard_map/ppermute | solution.py:61
  26.7 3.3 %collective-permute-start.11 = (s32[2,128,128]{2,1,0:T(8,128)S(1)}, s32[2,128,128]{2,1,0:T(8,128)S(1)}, u32[]{:S(2)}, u32[]{:S(2)}) collective-permute-start(s32[2,128,128]{2,1,0:T(8,128)S(1)} %collective-permute-done.10.refs_4_), channel_id=1, source_target_pairs={{0,1},{1,0},{2,3},{3,2},{4,5},{5,4},{6,7},{7,6},{8,9},{9,8},{10,11... | collective-permute-start | bytes 393224 | tf_op jit(solution)/shard_map/ppermute | solution.py:61
  26.7 13.9 %collective-permute-start.12 = (s32[2,128,128]{2,1,0:T(8,128)S(1)}, s32[2,128,128]{2,1,0:T(8,128)S(1)}, u32[]{:S(2)}, u32[]{:S(2)}) collective-permute-start(s32[2,128,128]{2,1,0:T(8,128)S(1)} %copy-done), channel_id=1, source_target_pairs={{0,4},{4,0},{8,12},{12,8},{1,5},{5,1},{9,13},{13,9},{2,6},{6,2},{1... | collective-permute-start | bytes 393224 | tf_op jit(solution)/shard_map/ppermute | solution.py:515
  27.8 12.9 %collective-permute-start.13 = (s32[2,128,128]{2,1,0:T(8,128)S(1)}, s32[2,128,128]{2,1,0:T(8,128)S(1)}, u32[]{:S(2)}, u32[]{:S(2)}) collective-permute-start(s32[2,128,128]{2,1,0:T(8,128)S(1)} %copy-done), channel_id=1, source_target_pairs={{0,12},{4,8},{8,4},{12,0},{1,13},{5,9},{9,5},{13,1},{2,14},{6,10},... | collective-permute-start | bytes 393224 | tf_op jit(solution)/shard_map/ppermute | solution.py:516
  40.7 1.6 %collective-permute-start.14 = (f32[2,256,128]{2,1,0:T(8,128)S(1)}, f32[2,256,128]{2,1,0:T(8,128)S(1)}, u32[]{:S(2)}, u32[]{:S(2)}) collective-permute-start(f32[2,256,128]{2,1,0:T(8,128)S(1)} %get-tuple-element.36), channel_id=1, source_target_pairs={{0,1},{1,0},{2,3},{3,2},{4,5},{5,4},{6,7},{7,6},{8,9},{9,8},{10,11... | collective-permute-start | bytes 786440 | tf_op jit(solution)/shard_map/ppermute | solution.py:61

commit v4 on v3

--- a/solution.py
+++ b/solution.py
@@ -76,7 +76,7 @@
         if plan.tiles == 4:
             got[3] = swap(mine, "tile", 3)
             got[1] = swap(mine, "tile", 1)
-            got[2] = swap(after(got[3], *crossed), "tile", 1)
+            got[2] = swap(after(got[3], got[1], *crossed), "tile", 1)
         else:
             for bits in range(1, plan.tiles):
                 got[bits] = swap(mine, "tile", bits)
@@ -229,18 +229,15 @@
                     target[first + plane, pl.ds(row, cz), :] = value
 
 
-def enter(plan, sheet, field, spread):
+def clear(plan, field, spread):
     half, rows = plan.half, plan.rows
-    wide = (rows, plan.width)
-    field[0, half:half + rows, :] = jnp.broadcast_to(sheet[...], wide)
-    field[1, half:half + rows, :] = jnp.zeros(wide, jnp.float32)
     for ref in (field, spread):
         for d in range(2):
             ref[d, :half, :] = jnp.zeros((half, plan.width), jnp.float32)
             ref[d, half + rows:, :] = jnp.zeros((half, plan.width), jnp.float32)
 
 
-def propagate(plan, cos_at, sin_at, left, ky, kz, km, field, spread):
+def propagate(plan, cos_at, sin_at, left, sheet, ky, kz, km, field, spread):
     ny, half, block, sheets = plan.ny, plan.half, plan.block, plan.sheets
     source, target = plan.start(left + 1), plan.start(left)
     sources, targets = plan.blocks(left + 1), plan.blocks(left)
@@ -258,6 +255,10 @@
         parts = []
         for p in range(sheets):
             lanes = slice(p * ny, (p + 1) * ny)
+            if sheet is not None:
+                plane = sheet[:, lanes]
+                parts.append(jnp.concatenate([plane * cos, plane * sin], axis=1))
+                continue
             re = field[0, pl.ds(row + half, block), lanes]
             im = field[1, pl.ds(row + half, block), lanes]
             parts.append(jnp.concatenate([re * cos - im * sin, re * sin + im * cos], axis=1))
@@ -323,7 +324,7 @@
     out, hbm_cosine, hbm_sine, mine, cosine, sine, field, spread, sems = refs[count:]
     own = plan.own
     (arriving,) = fetch([(hbm_mine, mine)], sems)
-    enter(plan, sheet, field, spread)
+    clear(plan, field, spread)
     look_up(plan, groups, list(enumerate(pieces, 1)), table, cosine, sine)
     arriving.wait()
     look_up(plan, groups, [(0, mine)], table, cosine, sine)
@@ -331,9 +332,10 @@
     side = plan.here()[1]
 
     def step(k, left):
+        entering = None if k else sheet
         slot = jnp.where(side == 0, k, own - 1 - k)
         maps = [lambda row, n, ref=ref: ref[slot, pl.ds(row, n), :] for ref in (cosine, sine)]
-        propagate(plan, *maps, left, ky, kz, km, field, spread)
+        propagate(plan, *maps, left, entering, ky, kz, km, field, spread)
         out[slot] = energy(plan, field)
 
     for k in range(own):
@@ -348,19 +350,21 @@
     out, far_cosine, far_sine, cosine, sine, field, spread, sems = refs[count:]
     own = plan.own
     arriving = fetch([(hbm_cosine, cosine), (hbm_sine, sine)], sems)
-    enter(plan, sheet, field, spread)
+    clear(plan, field, spread)
     look_up(plan, groups, list(enumerate(pieces)), table, far_cosine, far_sine)
     side = plan.here()[1]
 
     def far_step(k, left):
+        entering = None if k else sheet
         slot = jnp.where(side == 0, own - 1 - k, k)
         maps = [lambda row, n, ref=ref: ref[slot, pl.ds(row, n), :] for ref in (far_cosine, far_sine)]
-        propagate(plan, *maps, left, ky, kz, km, field, spread)
+        propagate(plan, *maps, left, entering, ky, kz, km, field, spread)
 
     def step(k, left):
+        entering = None
         slot = jnp.where(side == 0, 2 * own - 1 - k, k - own)
         maps = [lambda row, n, ref=ref: ref[slot, pl.ds(row, n), :] for ref in (cosine, sine)]
-        propagate(plan, *maps, left, ky, kz, km, field, spread)
+        propagate(plan, *maps, left, entering, ky, kz, km, field, spread)
         out[slot] = earlier[slot] + energy(plan, field)
 
     for k in range(own):
@@ -455,8 +459,10 @@
 
     crossed = [swap(classes, "sect", cores)]
     pieces, sources = tile_pieces(plan, classes, crossed)
-    joined = pieces[1:-1]
-    groups = (sources[:1], sources[1:-1], sources[-1:])
+    near = [over_cores(piece) for piece in pieces]
+    joined = [after(pieces[1], *near[1][1:]), *pieces[2:-1]]
+    near_groups = tuple((source,) for source in sources)
+    far_groups = (sources[:1], sources[1:-1], sources[-1:])
     line = -(-max(4 * half, taps) // ny) * ny
     phases = phase_table[None]
     ky, kz, km, by, bz, table, sheet, together = call(
@@ -481,18 +487,15 @@
             pltpu.SemaphoreType.DMA((4,)),
         ],
     )(prop_taps, detect_taps, phases, positions, *joined)
-    near = []
-    for number, piece in enumerate((classes, together, pieces[-1])):
-        near += over_cores(piece)
-        if number:
-            crossed.append(swap(piece, "sect", cores))
+    near = sum(near, [])
+    crossed += [swap(together, "sect", cores), swap(pieces[-1], "sect", cores)]
 
     maps = shape((plan.own, rows, ny), f32)
     whole_maps = pltpu.VMEM((plan.own, rows, ny), f32)
     state = pltpu.VMEM((2, rows + 2 * half, plan.width), f32)
     sums = shape((plan.own, plan.extent, ny), f32)
     sums, cosine, sine = call(
-        functools.partial(short_kernel, plan, groups),
+        functools.partial(short_kernel, plan, near_groups),
         (sums, maps, maps),
         [HBM] + [VMEM] * (4 + len(near)),
         [
@@ -503,7 +506,7 @@
             state,
             pltpu.SemaphoreType.DMA((2,)),
         ],
-        flops=3 * 10**9,
+        flops=1,
         out_spaces=(VMEM, HBM, HBM),
     )(near[0], ky, kz, km, table, sheet, *near[1:])
 
@@ -519,7 +522,7 @@
     for piece in crossed:
         far += [piece] + over_cores(after(piece, sums))[1:]
     sums = call(
-        functools.partial(long_kernel, plan, groups),
+        functools.partial(long_kernel, plan, far_groups),
         shape((plan.own, plan.extent, ny), f32),
         [VMEM] * 5 + [HBM] * 2 + [VMEM] * (1 + len(far)),
         [whole_maps] * 4 + [state, state, pltpu.SemaphoreType.DMA((2,))],

time: 43.7 us -> 43.1 us (0.986)
  waiting for transfers between devices: 7.32 us -> 5.68 us
  starting transfers between devices: 14.3 us -> 15.3 us
    ppermute x13 -> x14, waiting for transfers between devices: 7.31 us -> 5.67 us  [swap(): return lax.ppermute(x, axis, [(i, i ^ bits) for i in range(count)])]
    ppermute x13 -> x14, starting transfers between devices: 11 us -> 12.4 us  [swap(): return lax.ppermute(x, axis, [(i, i ^ bits) for i in range(count)])]
    ppermute x1, starting transfers between devices: 2.24 us -> 1.33 us  [on_device(): beyond = lax.ppermute(late, 'tile', gaps)]
    ppermute x1, starting transfers between devices: 1.06 us -> 1.62 us  [on_device(): facing = lax.ppermute(late, 'tile', pairs)]
  transfers between devices with their start and end apart: 15 -> 16, of which waited for: 6 -> 4; matrix products, arithmetic and copies ran while one was open for 0% -> 0% of each run, Pallas kernels for 47% -> 48%
where the time goes in v4:
time: 43.1 us; the launch traced here: 43 us
  Pallas kernels  21.8 us (51%)
  starting transfers between devices  15.3 us (35%)
  waiting for transfers between devices  5.68 us (13%)
    pallas_call x5, Pallas kernels, call_with(): pl.pallas_call(kernel, out_shape=outs, in_specs=[pl.BlockSpec(memory_spac...  21.8 us
    ppermute x14, starting transfers between devices, swap(): return lax.ppermute(x, axis, [(i, i ^ bits) for i in range(count)])  12.4 us
    ppermute x14, waiting for transfers between devices, swap(): return lax.ppermute(x, axis, [(i, i ^ bits) for i in range(count)])  5.67 us
    ppermute x1, starting transfers between devices, on_device(): facing = lax.ppermute(late, 'tile', pairs)  1.62 us
    ppermute x1, starting transfers between devices, on_device(): beyond = lax.ppermute(late, 'tile', gaps)  1.33 us
  transfers between devices with their start and end apart: 16, of which 4 were waited for; matrix products, arithmetic and copies ran while one was open for 0% of the time, Pallas kernels for 48%

profile of v4, /device:TPU:0, one launch (start us, length us, event | category | flops | bytes accessed | tf_op | source)
XLA Modules:
  0.0 43.0 jit_solution(12316877815645673339)
XLA Ops:
  0.0 5.0 %collective-permute-start = (s32[2,128,128]{2,1,0:T(8,128)}, s32[2,128,128]{2,1,0:T(8,128)S(1)}, u32[]{:S(2)}, u32[]{:S(2)}) collective-permute-start(s32[2,128,128]{2,1,0:T(8,128)} %hbm_mine.1), channel_id=1, source_target_pairs={{0,12},{4,8},{8,4},{12,0},{1,13},{5,9},{9,5},{13,1},{2,14},{6,10},... | collective-permute-start | bytes 393224 | tf_op jit(solution)/shard_map/ppermute | solution.py:61
  5.0 0.0 collective-permute-start.2
  5.1 1.5 %collective-permute-start.5 = (s32[2,128,128]{2,1,0:T(8,128)}, s32[2,128,128]{2,1,0:T(8,128)S(1)}, u32[]{:S(2)}, u32[]{:S(2)}) collective-permute-start(s32[2,128,128]{2,1,0:T(8,128)} %hbm_mine.1), channel_id=1, source_target_pairs={{0,2},{1,3},{2,0},{3,1},{4,6},{5,7},{6,4},{7,5},{8,10},{9,11},{10,... | collective-permute-start | bytes 393224 | tf_op jit(solution)/shard_map/ppermute | solution.py:61
  6.5 3.1 %collective-permute-done.refs_0_.refs_1_ = s32[2,128,128]{2,1,0:T(8,128)S(1)} collective-permute-done((s32[2,128,128]{2,1,0:T(8,128)}, s32[2,128,128]{2,1,0:T(8,128)S(1)}, u32[]{:S(2)}, u32[]{:S(2)}) %collective-permute-start) | collective-permute-done | bytes 131104 | tf_op jit(solution)/shard_map/ppermute | solution.py:61
  9.6 2.0 %collective-permute-done.2.refs_1_.refs_3_ = s32[2,128,128]{2,1,0:T(8,128)S(1)} collective-permute-done((s32[2,128,128]{2,1,0:T(8,128)}, s32[2,128,128]{2,1,0:T(8,128)S(1)}, u32[]{:S(2)}, u32[]{:S(2)}) %collective-permute-start.2) | collective-permute-done | bytes 131104 | tf_op jit(solution)/shard_map/ppermute | solution.py:61
  11.7 1.7 %collective-permute-start.6 = (s32[2,128,128]{2,1,0:T(8,128)S(1)}, s32[2,128,128]{2,1,0:T(8,128)S(1)}, u32[]{:S(2)}, u32[]{:S(2)}) collective-permute-start(s32[2,128,128]{2,1,0:T(8,128)S(1)} %collective-permute-done.refs_0_.refs_1_), channel_id=1, source_target_pairs={{0,4},{4,0},{8,12},{12,8},{1,5},{5,1},{9,13},{13,9},{2,6},{6,2},{1... | collective-permute-start | bytes 393224 | tf_op jit(solution)/shard_map/ppermute | solution.py:61
  13.4 0.0 collective-permute-done.1.refs_2_
  13.4 1.5 %shard_map.73 = (bf16[2,256,256]{2,1,0:T(8,128)(2,1)S(1)}, bf16[2,2,256,256]{3,2,1,0:T(8,128)(2,1)S(1)}, bf16[2,256,256]{2,1,0:T(8,128)(2,1)S(1)}, bf16[2,128,12...) custom-call(f32[2,2,129]{2,1,0:T(2,128)} %hbm_taps.1, ...), custom_call_target="tpu_custom_call" | custom-call | bytes 1048576 | tf_op jit(solution)/shard_map/pallas_call | solution.py:437
  14.8 1.6 %collective-permute-start.9 = (s32[4,128,128]{2,1,0:T(8,128)S(1)}, s32[4,128,128]{2,1,0:T(8,128)S(1)}, u32[]{:S(2)}, u32[]{:S(2)}) collective-permute-start(s32[4,128,128]{2,1,0:T(8,128)S(1)} %get-tuple-element.34), channel_id=1, source_target_pairs={{0,2},{1,3},{2,0},{3,1},{4,6},{5,7},{6,4},{7,5},{8,10},{9,11},{10,... | collective-permute-start | bytes 786440 | tf_op jit(solution)/shard_map/ppermute | solution.py:61
  16.4 0.5 %collective-permute-start.4 = (s32[2,128,128]{2,1,0:T(8,128)S(1)}, s32[2,128,128]{2,1,0:T(8,128)S(1)}, u32[]{:S(2)}, u32[]{:S(2)}) collective-permute-start(s32[2,128,128]{2,1,0:T(8,128)S(1)} %collective-permute-done.2.refs_1_.refs_3_), channel_id=1, source_target_pairs={{0,1},{1,0},{2,3},{3,2},{4,5},{5,4},{6,7},{7,6},{8,9},{9,8},{10,11... | collective-permute-start | bytes 393224 | tf_op jit(solution)/shard_map/ppermute | solution.py:61
  16.9 0.0 collective-permute-start.7
  16.9 1.2 %collective-permute-start.11 = (s32[2,128,128]{2,1,0:T(8,128)S(1)}, s32[2,128,128]{2,1,0:T(8,128)S(1)}, u32[]{:S(2)}, u32[]{:S(2)}) collective-permute-start(s32[2,128,128]{2,1,0:T(8,128)S(1)} %collective-permute-done.6.refs_5_), channel_id=1, source_target_pairs={{0,2},{1,3},{2,0},{3,1},{4,6},{5,7},{6,4},{7,5},{8,10},{9,11},{10,... | collective-permute-start | bytes 393224 | tf_op jit(solution)/shard_map/ppermute | solution.py:61
  18.2 0.1 collective-permute-done.7.refs_6_
  18.3 7.4 %shard_map.74 = (f32[4,256,128]{2,1,0:T(8,128)S(1)}, f32[4,512,128]{2,1,0:T(8,128)}, f32[4,512,128]{2,1,0:T(8,128)}) custom-call(s32[2,128,128]{2,1,0:T(8,128)} %hbm_mine.1, bf16[2,256,256]{2,1,0:T(8,128)(2,1)S(1)} %get-tuple-element.24.ky, bf16[2,2,256,256]{3,2,1,0:T(8,128)(2,1)S(1)} %get-tuple-element.25.kz, ...), custom_call_target="tpu_custom_call" | custom-call | flops 1 | bytes 1048576 | tf_op jit(solution)/shard_map/pallas_call | solution.py:437
  25.7 0.2 collective-permute-start.10
  25.9 0.3 collective-permute-start.8
  26.3 0.2 collective-permute-start.12
  26.4 1.6 %collective-permute-start.13 = (s32[2,128,128]{2,1,0:T(8,128)S(1)}, s32[2,128,128]{2,1,0:T(8,128)S(1)}, u32[]{:S(2)}, u32[]{:S(2)}) collective-permute-start(s32[2,128,128]{2,1,0:T(8,128)S(1)} %copy-done.1), channel_id=1, source_target_pairs={{0,4},{4,0},{8,12},{12,8},{1,5},{5,1},{9,13},{13,9},{2,6},{6,2},{1... | collective-permute-start | bytes 393224 | tf_op jit(solution)/shard_map/ppermute | solution.py:518
  28.1 1.3 %collective-permute-start.14 = (s32[2,128,128]{2,1,0:T(8,128)S(1)}, s32[2,128,128]{2,1,0:T(8,128)S(1)}, u32[]{:S(2)}, u32[]{:S(2)}) collective-permute-start(s32[2,128,128]{2,1,0:T(8,128)S(1)} %copy-done.1), channel_id=1, source_target_pairs={{0,12},{4,8},{8,4},{12,0},{1,13},{5,9},{9,5},{13,1},{2,14},{6,10},... | collective-permute-start | bytes 393224 | tf_op jit(solution)/shard_map/ppermute | solution.py:519
  29.4 10.6 %shard_map.75 = f32[4,256,128]{2,1,0:T(8,128)S(1)} custom-call(bf16[2,256,256]{2,1,0:T(8,128)(2,1)S(1)} %get-tuple-element.24.ky, bf16[2,2,256,256]{3,2,1,0:T(8,128)(2,1)S(1)} %get-tuple-element.25.kz, bf16[2,256,256]{2,1,0:T(8,128)(2,1)S(1)} %get-tuple-element.26.km, f32[2,8]{1,0:T(2,128)S(1)} %get-tuple-element.27.table, ...), custom_call_target="tpu_custom_call" | custom-call | flops 6000000000 | bytes 1048576 | tf_op jit(solution)/shard_map/pallas_call | solution.py:437
  40.1 0.1 collective-permute-start.15
  40.2 1.1 %shard_map.76.weight = f32[2,256,128]{2,1,0:T(8,128)S(1)} custom-call(f32[16]{0:T(128)} %hbm_bright.1, s32[2,128,128]{2,1,0:T(8,128)} %hbm_labels.1, s32[2,128,128]{2,1,0:T(8,128)S(1)} %collective-permute-done.13.facing, s32[2,128,128]{2,1,0:T(8,128)S(1)} %collective-permute-done.14.beyond), custom_call_target="tpu_custom_call" | custom-call | bytes 1048576 | tf_op jit(solution)/shard_map/pallas_call | solution.py:437
  41.3 0.4 collective-permute-done.15.other
  41.7 1.2 %shard_map.77 = f32[2,128,128]{2,1,0:T(8,128)} custom-call(f32[2,256,128]{2,1,0:T(8,128)S(1)} %get-tuple-element.42.mine, f32[2,256,128]{2,1,0:T(8,128)S(1)} %collective-permute-done.15.other, f32[2,256,128]{2,1,0:T(8,128)S(1)} %shard_map.76.weight, bf16[2,128,128]{2,1,0:T(8,128)(2,1)S(1)} %get-tuple-element.39.by, bf16[2,128,256]{2,1,0:T(8,128)(2,1)S(1)} %get-tuple-element.40.bz), custom_call_target="tpu_custom_call" | custom-call | bytes 1048576 | tf_op jit(solution)/shard_map/pallas_call | solution.py:437
  (18 shorter events, 0.1 us)
Async XLA Ops:
  0.0 9.6 %collective-permute-start = (s32[2,128,128]{2,1,0:T(8,128)}, s32[2,128,128]{2,1,0:T(8,128)S(1)}, u32[]{:S(2)}, u32[]{:S(2)}) collective-permute-start(s32[2,128,128]{2,1,0:T(8,128)} %hbm_mine.1), channel_id=1, source_target_pairs={{0,12},{4,8},{8,4},{12,0},{1,13},{5,9},{9,5},{13,1},{2,14},{6,10},... | collective-permute-start | bytes 393224 | tf_op jit(solution)/shard_map/ppermute | solution.py:61
  5.0 6.6 %collective-permute-start.2 = (s32[2,128,128]{2,1,0:T(8,128)}, s32[2,128,128]{2,1,0:T(8,128)S(1)}, u32[]{:S(2)}, u32[]{:S(2)}) collective-permute-start(s32[2,128,128]{2,1,0:T(8,128)} %hbm_mine.1), channel_id=1, source_target_pairs={{0,4},{4,0},{8,12},{12,8},{1,5},{5,1},{9,13},{13,9},{2,6},{6,2},{1... | collective-permute-start | bytes 393224 | tf_op jit(solution)/shard_map/ppermute | solution.py:61
  5.1 6.6 %collective-permute-start.5 = (s32[2,128,128]{2,1,0:T(8,128)}, s32[2,128,128]{2,1,0:T(8,128)S(1)}, u32[]{:S(2)}, u32[]{:S(2)}) collective-permute-start(s32[2,128,128]{2,1,0:T(8,128)} %hbm_mine.1), channel_id=1, source_target_pairs={{0,2},{1,3},{2,0},{3,1},{4,6},{5,7},{6,4},{7,5},{8,10},{9,11},{10,... | collective-permute-start | bytes 393224 | tf_op jit(solution)/shard_map/ppermute | solution.py:61
  9.6 3.7 %collective-permute-start.1 = (s32[2,128,128]{2,1,0:T(8,128)S(1)}, s32[2,128,128]{2,1,0:T(8,128)S(1)}, u32[]{:S(2)}, u32[]{:S(2)}) collective-permute-start(s32[2,128,128]{2,1,0:T(8,128)S(1)} %collective-permute-done.refs_0_.refs_1_), channel_id=1, source_target_pairs={{0,1},{1,0},{2,3},{3,2},{4,5},{5,4},{6,7},{7,6},{8,9},{9,8},{10,11... | collective-permute-start | bytes 393224 | tf_op jit(solution)/shard_map/ppermute | solution.py:61
  11.7 5.3 %collective-permute-start.6 = (s32[2,128,128]{2,1,0:T(8,128)S(1)}, s32[2,128,128]{2,1,0:T(8,128)S(1)}, u32[]{:S(2)}, u32[]{:S(2)}) collective-permute-start(s32[2,128,128]{2,1,0:T(8,128)S(1)} %collective-permute-done.refs_0_.refs_1_), channel_id=1, source_target_pairs={{0,4},{4,0},{8,12},{12,8},{1,5},{5,1},{9,13},{13,9},{2,6},{6,2},{1... | collective-permute-start | bytes 393224 | tf_op jit(solution)/shard_map/ppermute | solution.py:61
  13.4 3.0 %copy-start = (s32[2,128,128]{2,1,0:T(8,128)S(1)}, s32[2,128,128]{2,1,0:T(8,128)}, u32[]{:S(2)}) copy-start(s32[2,128,128]{2,1,0:T(8,128)} %hbm_mine.1) | copy-start | bytes 393220
  14.8 10.8 %collective-permute-start.9 = (s32[4,128,128]{2,1,0:T(8,128)S(1)}, s32[4,128,128]{2,1,0:T(8,128)S(1)}, u32[]{:S(2)}, u32[]{:S(2)}) collective-permute-start(s32[4,128,128]{2,1,0:T(8,128)S(1)} %get-tuple-element.34), channel_id=1, source_target_pairs={{0,2},{1,3},{2,0},{3,1},{4,6},{5,7},{6,4},{7,5},{8,10},{9,11},{10,... | collective-permute-start | bytes 786440 | tf_op jit(solution)/shard_map/ppermute | solution.py:61
  16.4 1.8 %collective-permute-start.3 = (s32[2,128,128]{2,1,0:T(8,128)S(1)}, s32[2,128,128]{2,1,0:T(8,128)S(1)}, u32[]{:S(2)}, u32[]{:S(2)}) collective-permute-start(s32[2,128,128]{2,1,0:T(8,128)S(1)} %copy-done), channel_id=1, source_target_pairs={{0,1},{1,0},{2,3},{3,2},{4,5},{5,4},{6,7},{7,6},{8,9},{9,8},{10,11... | collective-permute-start | bytes 393224 | tf_op jit(solution)/shard_map/ppermute | solution.py:61
  16.4 1.8 %collective-permute-start.4 = (s32[2,128,128]{2,1,0:T(8,128)S(1)}, s32[2,128,128]{2,1,0:T(8,128)S(1)}, u32[]{:S(2)}, u32[]{:S(2)}) collective-permute-start(s32[2,128,128]{2,1,0:T(8,128)S(1)} %collective-permute-done.2.refs_1_.refs_3_), channel_id=1, source_target_pairs={{0,1},{1,0},{2,3},{3,2},{4,5},{5,4},{6,7},{7,6},{8,9},{9,8},{10,11... | collective-permute-start | bytes 393224 | tf_op jit(solution)/shard_map/ppermute | solution.py:61
  16.9 1.3 %collective-permute-start.7 = (s32[2,128,128]{2,1,0:T(8,128)S(1)}, s32[2,128,128]{2,1,0:T(8,128)S(1)}, u32[]{:S(2)}, u32[]{:S(2)}) collective-permute-start(s32[2,128,128]{2,1,0:T(8,128)S(1)} %collective-permute-done.6.refs_5_), channel_id=1, source_target_pairs={{0,1},{1,0},{2,3},{3,2},{4,5},{5,4},{6,7},{7,6},{8,9},{9,8},{10,11... | collective-permute-start | bytes 393224 | tf_op jit(solution)/shard_map/ppermute | solution.py:61
  16.9 9.3 %collective-permute-start.11 = (s32[2,128,128]{2,1,0:T(8,128)S(1)}, s32[2,128,128]{2,1,0:T(8,128)S(1)}, u32[]{:S(2)}, u32[]{:S(2)}) collective-permute-start(s32[2,128,128]{2,1,0:T(8,128)S(1)} %collective-permute-done.6.refs_5_), channel_id=1, source_target_pairs={{0,2},{1,3},{2,0},{3,1},{4,6},{5,7},{6,4},{7,5},{8,10},{9,11},{10,... | collective-permute-start | bytes 393224 | tf_op jit(solution)/shard_map/ppermute | solution.py:61
  18.3 8.2 %copy-start.1 = (s32[2,128,128]{2,1,0:T(8,128)S(1)}, s32[2,128,128]{2,1,0:T(8,128)}, u32[]{:S(2)}) copy-start(s32[2,128,128]{2,1,0:T(8,128)} %hbm_labels.1) | copy-start | bytes 393220
  25.7 3.7 %collective-permute-start.10 = (s32[4,128,128]{2,1,0:T(8,128)S(1)}, s32[4,128,128]{2,1,0:T(8,128)S(1)}, u32[]{:S(2)}, u32[]{:S(2)}) collective-permute-start(s32[4,128,128]{2,1,0:T(8,128)S(1)} %collective-permute-done.9.refs_2_), channel_id=1, source_target_pairs={{0,1},{1,0},{2,3},{3,2},{4,5},{5,4},{6,7},{7,6},{8,9},{9,8},{10,11... | collective-permute-start | bytes 786440 | tf_op jit(solution)/shard_map/ppermute | solution.py:61
  25.9 3.5 %collective-permute-start.8 = (s32[2,128,128]{2,1,0:T(8,128)S(1)}, s32[2,128,128]{2,1,0:T(8,128)S(1)}, u32[]{:S(2)}, u32[]{:S(2)}) collective-permute-start(s32[2,128,128]{2,1,0:T(8,128)S(1)} %collective-permute-done.5.refs_0_), channel_id=1, source_target_pairs={{0,1},{1,0},{2,3},{3,2},{4,5},{5,4},{6,7},{7,6},{8,9},{9,8},{10,11... | collective-permute-start | bytes 393224 | tf_op jit(solution)/shard_map/ppermute | solution.py:61
  26.3 3.1 %collective-permute-start.12 = (s32[2,128,128]{2,1,0:T(8,128)S(1)}, s32[2,128,128]{2,1,0:T(8,128)S(1)}, u32[]{:S(2)}, u32[]{:S(2)}) collective-permute-start(s32[2,128,128]{2,1,0:T(8,128)S(1)} %collective-permute-done.11.refs_4_), channel_id=1, source_target_pairs={{0,1},{1,0},{2,3},{3,2},{4,5},{5,4},{6,7},{7,6},{8,9},{9,8},{10,11... | collective-permute-start | bytes 393224 | tf_op jit(solution)/shard_map/ppermute | solution.py:61
  26.4 13.7 %collective-permute-start.13 = (s32[2,128,128]{2,1,0:T(8,128)S(1)}, s32[2,128,128]{2,1,0:T(8,128)S(1)}, u32[]{:S(2)}, u32[]{:S(2)}) collective-permute-start(s32[2,128,128]{2,1,0:T(8,128)S(1)} %copy-done.1), channel_id=1, source_target_pairs={{0,4},{4,0},{8,12},{12,8},{1,5},{5,1},{9,13},{13,9},{2,6},{6,2},{1... | collective-permute-start | bytes 393224 | tf_op jit(solution)/shard_map/ppermute | solution.py:518
  28.1 12.0 %collective-permute-start.14 = (s32[2,128,128]{2,1,0:T(8,128)S(1)}, s32[2,128,128]{2,1,0:T(8,128)S(1)}, u32[]{:S(2)}, u32[]{:S(2)}) collective-permute-start(s32[2,128,128]{2,1,0:T(8,128)S(1)} %copy-done.1), channel_id=1, source_target_pairs={{0,12},{4,8},{8,4},{12,0},{1,13},{5,9},{9,5},{13,1},{2,14},{6,10},... | collective-permute-start | bytes 393224 | tf_op jit(solution)/shard_map/ppermute | solution.py:519
  40.1 1.6 %collective-permute-start.15 = (f32[2,256,128]{2,1,0:T(8,128)S(1)}, f32[2,256,128]{2,1,0:T(8,128)S(1)}, u32[]{:S(2)}, u32[]{:S(2)}) collective-permute-start(f32[2,256,128]{2,1,0:T(8,128)S(1)} %get-tuple-element.38), channel_id=1, source_target_pairs={{0,1},{1,0},{2,3},{3,2},{4,5},{5,4},{6,7},{7,6},{8,9},{9,8},{10,11... | collective-permute-start | bytes 786440 | tf_op jit(solution)/shard_map/ppermute | solution.py:61

commit v5 on v4

--- a/solution.py
+++ b/solution.py
@@ -191,8 +191,11 @@
     keep(by, circulant(folded(dtaps[0:1, :]), ny, half))
     keep(bz, band(padded(dtaps[1:2, :])[:, :wide], block, wide))
 
-    table[0:1, :] = jnp.cos(phases[...])
-    table[1:2, :] = jnp.sin(phases[...])
+    number = phases.shape[1]
+    for part, row in enumerate((jnp.cos(phases[...]), jnp.sin(phases[...]))):
+        for e in range(number):
+            place = part * number + e
+            table[place:place + 1, :] = jnp.broadcast_to(row[:, e:e + 1], (1, table.shape[1]))
     core = plan.here()[2]
     lane = lax.broadcasted_iota(jnp.int32, (1, ny), 1).astype(jnp.float32)
     for p in range(plan.sheets):
@@ -203,19 +206,23 @@
         sheet[:, p * ny:(p + 1) * ny] = jnp.where(live, AMPLITUDE, 0.0) * jnp.exp(-offset * offset)
 
 
-def choose(index, values):
-    size = 1 << (len(values) - 1).bit_length()
-    values = list(values) + [values[-1]] * (size - len(values))
+def choose(index, *tables):
+    count = len(tables[0])
+    size = 1 << (count - 1).bit_length()
+    tables = [list(values) + [values[-1]] * (size - count) for values in tables]
     for b in range(size.bit_length() - 1):
         bit = (index & (1 << b)) != 0
-        values = [jnp.where(bit, values[i + 1], values[i]) for i in range(0, len(values), 2)]
-    return values[0]
+        tables = [
+            [jnp.where(bit, values[i + 1], values[i]) for i in range(0, len(values), 2)] for values in tables
+        ]
+    return [values[0] for values in tables]
 
 
 def look_up(plan, groups, pieces, table, cosine, sine):
     cz = plan.cz
     core = plan.here()[2]
-    entries = [[table[part:part + 1, e:e + 1] for e in range(table.shape[1])] for part in range(2)]
+    count = table.shape[0] // 2
+    entries = [[table[part * count + e:part * count + e + 1, :] for e in range(count)] for part in range(2)]
     for number, piece in pieces:
         first = (core ^ (number % plan.cores)) * plan.planes
         for place, source in enumerate(groups[number // plan.cores]):
@@ -223,8 +230,7 @@
             row = pl.multiple_of(block * cz, cz)
             for plane in range(plan.planes):
                 kind = piece[place * plan.planes + plane].T
-                for values, target in zip(entries, (cosine, sine)):
-                    value = choose(kind, values)
+                for value, target in zip(choose(kind, *entries), (cosine, sine)):
                     value = value if valid is None else jnp.where(valid, value, 0.0)
                     target[first + plane, pl.ds(row, cz), :] = value
 
@@ -318,15 +324,13 @@
     return total
 
 
-def short_kernel(plan, groups, hbm_mine, ky, kz, km, table, sheet, *refs):
+def short_kernel(plan, groups, mine, ky, kz, km, table, sheet, *refs):
     count = len(groups) * plan.cores - 1
     pieces = refs[:count]
-    out, hbm_cosine, hbm_sine, mine, cosine, sine, field, spread, sems = refs[count:]
+    out, hbm_cosine, hbm_sine, cosine, sine, field, spread, sems = refs[count:]
     own = plan.own
-    (arriving,) = fetch([(hbm_mine, mine)], sems)
     clear(plan, field, spread)
     look_up(plan, groups, list(enumerate(pieces, 1)), table, cosine, sine)
-    arriving.wait()
     look_up(plan, groups, [(0, mine)], table, cosine, sine)
     leaving = fetch([(cosine, hbm_cosine), (sine, hbm_sine)], sems)
     side = plan.here()[1]
@@ -388,12 +392,12 @@
     for x in range(plan.planes):
         before = jnp.where(even, beyond[x], facing[x])[:, -2 * half:]
         behind = jnp.where(even, facing[x], beyond[x])[:, :2 * half]
-        halo = (choose(jnp.where(first_half, behind, before), values) * inside).T
+        halo = (choose(jnp.where(first_half, behind, before), values)[0] * inside).T
         weight[x, :half, :] = halo[half:]
         weight[x, half + cz:, :] = halo[:half]
     arriving.wait()
     for x in range(plan.planes):
-        weight[x, half:half + cz, :] = choose(labels[x], values).T
+        weight[x, half:half + cz, :] = choose(labels[x], values)[0].T
 
 
 def blur_kernel(plan, mine, other, weight, by, bz, out):
@@ -473,7 +477,7 @@
             shape((2, 2 * block, 2 * block), bf16),
             shape((2, ny, ny), bf16),
             shape((2, block, 2 * block), bf16),
-            shape((2, phases.shape[1]), f32),
+            shape((2 * phases.shape[1], ny), f32),
             shape((1, plan.width), f32),
             shape((len(joined) * plan.planes, ny, plan.cz), classes.dtype),
         ),
@@ -497,9 +501,8 @@
     sums, cosine, sine = call(
         functools.partial(short_kernel, plan, near_groups),
         (sums, maps, maps),
-        [HBM] + [VMEM] * (4 + len(near)),
+        [VMEM] * (5 + len(near)),
         [
-            pltpu.VMEM(classes.shape, classes.dtype),
             whole_maps,
             whole_maps,
             state,

time: 43.1 us -> 41.7 us (0.968)
  Pallas kernels: 21.8 us -> 20.5 us
    pallas_call x5, Pallas kernels: 21.8 us -> 20.5 us  [call_with(): pl.pallas_call(kernel, out_shape=outs, in_specs=[pl.BlockSpec(memory_spac...]
  transfers between devices with their start and end apart: 16 -> 16, of which waited for: 4 -> 4; matrix products, arithmetic and copies ran while one was open for 0% -> 0% of each run, Pallas kernels for 48% -> 46%
where the time goes in v5:
time: 41.7 us; the launch traced here: 41.6 us
  Pallas kernels  20.5 us (49%)
  starting transfers between devices  15.3 us (37%)
  waiting for transfers between devices  5.69 us (14%)
    pallas_call x5, Pallas kernels, call_with(): pl.pallas_call(kernel, out_shape=outs, in_specs=[pl.BlockSpec(memory_spac...  20.5 us
    ppermute x14, starting transfers between devices, swap(): return lax.ppermute(x, axis, [(i, i ^ bits) for i in range(count)])  12.4 us
    ppermute x14, waiting for transfers between devices, swap(): return lax.ppermute(x, axis, [(i, i ^ bits) for i in range(count)])  5.68 us
    ppermute x1, starting transfers between devices, on_device(): facing = lax.ppermute(late, 'tile', pairs)  1.6 us
    ppermute x1, starting transfers between devices, on_device(): beyond = lax.ppermute(late, 'tile', gaps)  1.33 us
  transfers between devices with their start and end apart: 16, of which 4 were waited for; matrix products, arithmetic and copies ran while one was open for 0% of the time, Pallas kernels for 46%

profile of v5, /device:TPU:0, one launch (start us, length us, event | category | flops | bytes accessed | tf_op | source)
XLA Modules:
  0.0 41.6 jit_solution(7464072554926976804)
XLA Ops:
  0.0 5.0 %collective-permute-start = (s32[2,128,128]{2,1,0:T(8,128)}, s32[2,128,128]{2,1,0:T(8,128)S(1)}, u32[]{:S(2)}, u32[]{:S(2)}) collective-permute-start(s32[2,128,128]{2,1,0:T(8,128)} %mine.1), channel_id=1, source_target_pairs={{0,12},{4,8},{8,4},{12,0},{1,13},{5,9},{9,5},{13,1},{2,14},{6,10},... | collective-permute-start | bytes 393224 | tf_op jit(solution)/shard_map/ppermute | solution.py:61
  5.1 1.5 %collective-permute-start.5 = (s32[2,128,128]{2,1,0:T(8,128)}, s32[2,128,128]{2,1,0:T(8,128)S(1)}, u32[]{:S(2)}, u32[]{:S(2)}) collective-permute-start(s32[2,128,128]{2,1,0:T(8,128)} %mine.1), channel_id=1, source_target_pairs={{0,2},{1,3},{2,0},{3,1},{4,6},{5,7},{6,4},{7,5},{8,10},{9,11},{10,... | collective-permute-start | bytes 393224 | tf_op jit(solution)/shard_map/ppermute | solution.py:61
  6.5 3.1 %collective-permute-done.refs_0_.refs_1_ = s32[2,128,128]{2,1,0:T(8,128)S(1)} collective-permute-done((s32[2,128,128]{2,1,0:T(8,128)}, s32[2,128,128]{2,1,0:T(8,128)S(1)}, u32[]{:S(2)}, u32[]{:S(2)}) %collective-permute-start) | collective-permute-done | bytes 131104 | tf_op jit(solution)/shard_map/ppermute | solution.py:61
  9.6 0.0 collective-permute-start.1
  9.6 2.0 %collective-permute-done.2.refs_1_.refs_3_ = s32[2,128,128]{2,1,0:T(8,128)S(1)} collective-permute-done((s32[2,128,128]{2,1,0:T(8,128)}, s32[2,128,128]{2,1,0:T(8,128)S(1)}, u32[]{:S(2)}, u32[]{:S(2)}) %collective-permute-start.2) | collective-permute-done | bytes 131104 | tf_op jit(solution)/shard_map/ppermute | solution.py:61
  11.7 1.7 %collective-permute-start.6 = (s32[2,128,128]{2,1,0:T(8,128)S(1)}, s32[2,128,128]{2,1,0:T(8,128)S(1)}, u32[]{:S(2)}, u32[]{:S(2)}) collective-permute-start(s32[2,128,128]{2,1,0:T(8,128)S(1)} %collective-permute-done.refs_0_.refs_1_), channel_id=1, source_target_pairs={{0,4},{4,0},{8,12},{12,8},{1,5},{5,1},{9,13},{13,9},{2,6},{6,2},{1... | collective-permute-start | bytes 393224 | tf_op jit(solution)/shard_map/ppermute | solution.py:61
  13.4 0.0 collective-permute-done.1.refs_2_
  13.4 1.5 %shard_map.73 = (bf16[2,256,256]{2,1,0:T(8,128)(2,1)S(1)}, bf16[2,2,256,256]{3,2,1,0:T(8,128)(2,1)S(1)}, bf16[2,256,256]{2,1,0:T(8,128)(2,1)S(1)}, bf16[2,128,12...) custom-call(f32[2,2,129]{2,1,0:T(2,128)} %hbm_taps.1, ...), custom_call_target="tpu_custom_call" | custom-call | bytes 1048576 | tf_op jit(solution)/shard_map/pallas_call | solution.py:441
  14.9 1.6 %collective-permute-start.9 = (s32[4,128,128]{2,1,0:T(8,128)S(1)}, s32[4,128,128]{2,1,0:T(8,128)S(1)}, u32[]{:S(2)}, u32[]{:S(2)}) collective-permute-start(s32[4,128,128]{2,1,0:T(8,128)S(1)} %get-tuple-element.34), channel_id=1, source_target_pairs={{0,2},{1,3},{2,0},{3,1},{4,6},{5,7},{6,4},{7,5},{8,10},{9,11},{10,... | collective-permute-start | bytes 786440 | tf_op jit(solution)/shard_map/ppermute | solution.py:61
  16.4 0.5 %collective-permute-start.4 = (s32[2,128,128]{2,1,0:T(8,128)S(1)}, s32[2,128,128]{2,1,0:T(8,128)S(1)}, u32[]{:S(2)}, u32[]{:S(2)}) collective-permute-start(s32[2,128,128]{2,1,0:T(8,128)S(1)} %collective-permute-done.2.refs_1_.refs_3_), channel_id=1, source_target_pairs={{0,1},{1,0},{2,3},{3,2},{4,5},{5,4},{6,7},{7,6},{8,9},{9,8},{10,11... | collective-permute-start | bytes 393224 | tf_op jit(solution)/shard_map/ppermute | solution.py:61
  16.9 0.0 collective-permute-start.7
  16.9 1.2 %collective-permute-start.11 = (s32[2,128,128]{2,1,0:T(8,128)S(1)}, s32[2,128,128]{2,1,0:T(8,128)S(1)}, u32[]{:S(2)}, u32[]{:S(2)}) collective-permute-start(s32[2,128,128]{2,1,0:T(8,128)S(1)} %collective-permute-done.6.refs_5_), channel_id=1, source_target_pairs={{0,2},{1,3},{2,0},{3,1},{4,6},{5,7},{6,4},{7,5},{8,10},{9,11},{10,... | collective-permute-start | bytes 393224 | tf_op jit(solution)/shard_map/ppermute | solution.py:61
  18.2 0.1 collective-permute-done.7.refs_6_
  18.3 6.5 %shard_map.74 = (f32[4,256,128]{2,1,0:T(8,128)S(1)}, f32[4,512,128]{2,1,0:T(8,128)}, f32[4,512,128]{2,1,0:T(8,128)}) custom-call(s32[2,128,128]{2,1,0:T(8,128)S(1)} %copy-done, bf16[2,256,256]{2,1,0:T(8,128)(2,1)S(1)} %get-tuple-element.24.ky, bf16[2,2,256,256]{3,2,1,0:T(8,128)(2,1)S(1)} %get-tuple-element.25.kz, ...), custom_call_target="tpu_custom_call" | custom-call | flops 1 | bytes 1048576 | tf_op jit(solution)/shard_map/pallas_call | solution.py:441
  24.8 0.2 collective-permute-start.10
  25.0 0.3 collective-permute-start.8
  25.4 0.2 collective-permute-start.12
  25.5 1.6 %collective-permute-start.13 = (s32[2,128,128]{2,1,0:T(8,128)S(1)}, s32[2,128,128]{2,1,0:T(8,128)S(1)}, u32[]{:S(2)}, u32[]{:S(2)}) collective-permute-start(s32[2,128,128]{2,1,0:T(8,128)S(1)} %copy-done.1), channel_id=1, source_target_pairs={{0,4},{4,0},{8,12},{12,8},{1,5},{5,1},{9,13},{13,9},{2,6},{6,2},{1... | collective-permute-start | bytes 393224 | tf_op jit(solution)/shard_map/ppermute | solution.py:521
  27.1 1.3 %collective-permute-start.14 = (s32[2,128,128]{2,1,0:T(8,128)S(1)}, s32[2,128,128]{2,1,0:T(8,128)S(1)}, u32[]{:S(2)}, u32[]{:S(2)}) collective-permute-start(s32[2,128,128]{2,1,0:T(8,128)S(1)} %copy-done.1), channel_id=1, source_target_pairs={{0,12},{4,8},{8,4},{12,0},{1,13},{5,9},{9,5},{13,1},{2,14},{6,10},... | collective-permute-start | bytes 393224 | tf_op jit(solution)/shard_map/ppermute | solution.py:522
  28.5 10.2 %shard_map.75 = f32[4,256,128]{2,1,0:T(8,128)S(1)} custom-call(bf16[2,256,256]{2,1,0:T(8,128)(2,1)S(1)} %get-tuple-element.24.ky, bf16[2,2,256,256]{3,2,1,0:T(8,128)(2,1)S(1)} %get-tuple-element.25.kz, bf16[2,256,256]{2,1,0:T(8,128)(2,1)S(1)} %get-tuple-element.26.km, f32[16,128]{1,0:T(8,128)S(1)} %get-tuple-element.27.table, ...), custom_call_target="tpu_custom_call" | custom-call | flops 6000000000 | bytes 1048576 | tf_op jit(solution)/shard_map/pallas_call | solution.py:441
  38.7 0.1 collective-permute-start.15
  38.8 1.1 %shard_map.76.weight = f32[2,256,128]{2,1,0:T(8,128)S(1)} custom-call(f32[16]{0:T(128)} %hbm_bright.1, s32[2,128,128]{2,1,0:T(8,128)} %hbm_labels.1, s32[2,128,128]{2,1,0:T(8,128)S(1)} %collective-permute-done.13.facing, s32[2,128,128]{2,1,0:T(8,128)S(1)} %collective-permute-done.14.beyond), custom_call_target="tpu_custom_call" | custom-call | bytes 1048576 | tf_op jit(solution)/shard_map/pallas_call | solution.py:441
  39.9 0.4 %collective-permute-done.15.other = f32[2,256,128]{2,1,0:T(8,128)S(1)} collective-permute-done((f32[2,256,128]{2,1,0:T(8,128)S(1)}, f32[2,256,128]{2,1,0:T(8,128)S(1)}, u32[]{:S(2)}, u32[]{:S(2)}) %collective-permute-start.15) | collective-permute-done | bytes 262176 | tf_op jit(solution)/shard_map/ppermute | solution.py:61
  40.3 1.2 %shard_map.77 = f32[2,128,128]{2,1,0:T(8,128)} custom-call(f32[2,256,128]{2,1,0:T(8,128)S(1)} %get-tuple-element.42.mine, f32[2,256,128]{2,1,0:T(8,128)S(1)} %collective-permute-done.15.other, f32[2,256,128]{2,1,0:T(8,128)S(1)} %shard_map.76.weight, bf16[2,128,128]{2,1,0:T(8,128)(2,1)S(1)} %get-tuple-element.39.by, bf16[2,128,256]{2,1,0:T(8,128)(2,1)S(1)} %get-tuple-element.40.bz), custom_call_target="tpu_custom_call" | custom-call | bytes 1048576 | tf_op jit(solution)/shard_map/pallas_call | solution.py:441
  (18 shorter events, 0.1 us)
Async XLA Ops:
  0.0 9.6 %collective-permute-start = (s32[2,128,128]{2,1,0:T(8,128)}, s32[2,128,128]{2,1,0:T(8,128)S(1)}, u32[]{:S(2)}, u32[]{:S(2)}) collective-permute-start(s32[2,128,128]{2,1,0:T(8,128)} %mine.1), channel_id=1, source_target_pairs={{0,12},{4,8},{8,4},{12,0},{1,13},{5,9},{9,5},{13,1},{2,14},{6,10},... | collective-permute-start | bytes 393224 | tf_op jit(solution)/shard_map/ppermute | solution.py:61
  5.0 6.6 %collective-permute-start.2 = (s32[2,128,128]{2,1,0:T(8,128)}, s32[2,128,128]{2,1,0:T(8,128)S(1)}, u32[]{:S(2)}, u32[]{:S(2)}) collective-permute-start(s32[2,128,128]{2,1,0:T(8,128)} %mine.1), channel_id=1, source_target_pairs={{0,4},{4,0},{8,12},{12,8},{1,5},{5,1},{9,13},{13,9},{2,6},{6,2},{1... | collective-permute-start | bytes 393224 | tf_op jit(solution)/shard_map/ppermute | solution.py:61
  5.1 6.6 %collective-permute-start.5 = (s32[2,128,128]{2,1,0:T(8,128)}, s32[2,128,128]{2,1,0:T(8,128)S(1)}, u32[]{:S(2)}, u32[]{:S(2)}) collective-permute-start(s32[2,128,128]{2,1,0:T(8,128)} %mine.1), channel_id=1, source_target_pairs={{0,2},{1,3},{2,0},{3,1},{4,6},{5,7},{6,4},{7,5},{8,10},{9,11},{10,... | collective-permute-start | bytes 393224 | tf_op jit(solution)/shard_map/ppermute | solution.py:61
  9.6 3.7 %collective-permute-start.1 = (s32[2,128,128]{2,1,0:T(8,128)S(1)}, s32[2,128,128]{2,1,0:T(8,128)S(1)}, u32[]{:S(2)}, u32[]{:S(2)}) collective-permute-start(s32[2,128,128]{2,1,0:T(8,128)S(1)} %collective-permute-done.refs_0_.refs_1_), channel_id=1, source_target_pairs={{0,1},{1,0},{2,3},{3,2},{4,5},{5,4},{6,7},{7,6},{8,9},{9,8},{10,11... | collective-permute-start | bytes 393224 | tf_op jit(solution)/shard_map/ppermute | solution.py:61
  11.7 5.3 %collective-permute-start.6 = (s32[2,128,128]{2,1,0:T(8,128)S(1)}, s32[2,128,128]{2,1,0:T(8,128)S(1)}, u32[]{:S(2)}, u32[]{:S(2)}) collective-permute-start(s32[2,128,128]{2,1,0:T(8,128)S(1)} %collective-permute-done.refs_0_.refs_1_), channel_id=1, source_target_pairs={{0,4},{4,0},{8,12},{12,8},{1,5},{5,1},{9,13},{13,9},{2,6},{6,2},{1... | collective-permute-start | bytes 393224 | tf_op jit(solution)/shard_map/ppermute | solution.py:61
  13.4 3.1 %copy-start = (s32[2,128,128]{2,1,0:T(8,128)S(1)}, s32[2,128,128]{2,1,0:T(8,128)}, u32[]{:S(2)}) copy-start(s32[2,128,128]{2,1,0:T(8,128)} %mine.1) | copy-start | bytes 393220
  14.9 9.9 %collective-permute-start.9 = (s32[4,128,128]{2,1,0:T(8,128)S(1)}, s32[4,128,128]{2,1,0:T(8,128)S(1)}, u32[]{:S(2)}, u32[]{:S(2)}) collective-permute-start(s32[4,128,128]{2,1,0:T(8,128)S(1)} %get-tuple-element.34), channel_id=1, source_target_pairs={{0,2},{1,3},{2,0},{3,1},{4,6},{5,7},{6,4},{7,5},{8,10},{9,11},{10,... | collective-permute-start | bytes 786440 | tf_op jit(solution)/shard_map/ppermute | solution.py:61
  16.4 1.7 %collective-permute-start.3 = (s32[2,128,128]{2,1,0:T(8,128)S(1)}, s32[2,128,128]{2,1,0:T(8,128)S(1)}, u32[]{:S(2)}, u32[]{:S(2)}) collective-permute-start(s32[2,128,128]{2,1,0:T(8,128)S(1)} %copy-done), channel_id=1, source_target_pairs={{0,1},{1,0},{2,3},{3,2},{4,5},{5,4},{6,7},{7,6},{8,9},{9,8},{10,11... | collective-permute-start | bytes 393224 | tf_op jit(solution)/shard_map/ppermute | solution.py:61
  16.4 1.7 %collective-permute-start.4 = (s32[2,128,128]{2,1,0:T(8,128)S(1)}, s32[2,128,128]{2,1,0:T(8,128)S(1)}, u32[]{:S(2)}, u32[]{:S(2)}) collective-permute-start(s32[2,128,128]{2,1,0:T(8,128)S(1)} %collective-permute-done.2.refs_1_.refs_3_), channel_id=1, source_target_pairs={{0,1},{1,0},{2,3},{3,2},{4,5},{5,4},{6,7},{7,6},{8,9},{9,8},{10,11... | collective-permute-start | bytes 393224 | tf_op jit(solution)/shard_map/ppermute | solution.py:61
  16.9 1.3 %collective-permute-start.7 = (s32[2,128,128]{2,1,0:T(8,128)S(1)}, s32[2,128,128]{2,1,0:T(8,128)S(1)}, u32[]{:S(2)}, u32[]{:S(2)}) collective-permute-start(s32[2,128,128]{2,1,0:T(8,128)S(1)} %collective-permute-done.6.refs_5_), channel_id=1, source_target_pairs={{0,1},{1,0},{2,3},{3,2},{4,5},{5,4},{6,7},{7,6},{8,9},{9,8},{10,11... | collective-permute-start | bytes 393224 | tf_op jit(solution)/shard_map/ppermute | solution.py:61
  16.9 8.4 %collective-permute-start.11 = (s32[2,128,128]{2,1,0:T(8,128)S(1)}, s32[2,128,128]{2,1,0:T(8,128)S(1)}, u32[]{:S(2)}, u32[]{:S(2)}) collective-permute-start(s32[2,128,128]{2,1,0:T(8,128)S(1)} %collective-permute-done.6.refs_5_), channel_id=1, source_target_pairs={{0,2},{1,3},{2,0},{3,1},{4,6},{5,7},{6,4},{7,5},{8,10},{9,11},{10,... | collective-permute-start | bytes 393224 | tf_op jit(solution)/shard_map/ppermute | solution.py:61
  18.3 7.3 %copy-start.1 = (s32[2,128,128]{2,1,0:T(8,128)S(1)}, s32[2,128,128]{2,1,0:T(8,128)}, u32[]{:S(2)}) copy-start(s32[2,128,128]{2,1,0:T(8,128)} %hbm_labels.1) | copy-start | bytes 393220
  24.8 3.7 %collective-permute-start.10 = (s32[4,128,128]{2,1,0:T(8,128)S(1)}, s32[4,128,128]{2,1,0:T(8,128)S(1)}, u32[]{:S(2)}, u32[]{:S(2)}) collective-permute-start(s32[4,128,128]{2,1,0:T(8,128)S(1)} %collective-permute-done.9.refs_2_), channel_id=1, source_target_pairs={{0,1},{1,0},{2,3},{3,2},{4,5},{5,4},{6,7},{7,6},{8,9},{9,8},{10,11... | collective-permute-start | bytes 786440 | tf_op jit(solution)/shard_map/ppermute | solution.py:61
  25.0 3.5 %collective-permute-start.8 = (s32[2,128,128]{2,1,0:T(8,128)S(1)}, s32[2,128,128]{2,1,0:T(8,128)S(1)}, u32[]{:S(2)}, u32[]{:S(2)}) collective-permute-start(s32[2,128,128]{2,1,0:T(8,128)S(1)} %collective-permute-done.5.refs_0_), channel_id=1, source_target_pairs={{0,1},{1,0},{2,3},{3,2},{4,5},{5,4},{6,7},{7,6},{8,9},{9,8},{10,11... | collective-permute-start | bytes 393224 | tf_op jit(solution)/shard_map/ppermute | solution.py:61
  25.4 3.1 %collective-permute-start.12 = (s32[2,128,128]{2,1,0:T(8,128)S(1)}, s32[2,128,128]{2,1,0:T(8,128)S(1)}, u32[]{:S(2)}, u32[]{:S(2)}) collective-permute-start(s32[2,128,128]{2,1,0:T(8,128)S(1)} %collective-permute-done.11.refs_4_), channel_id=1, source_target_pairs={{0,1},{1,0},{2,3},{3,2},{4,5},{5,4},{6,7},{7,6},{8,9},{9,8},{10,11... | collective-permute-start | bytes 393224 | tf_op jit(solution)/shard_map/ppermute | solution.py:61
  25.5 13.2 %collective-permute-start.13 = (s32[2,128,128]{2,1,0:T(8,128)S(1)}, s32[2,128,128]{2,1,0:T(8,128)S(1)}, u32[]{:S(2)}, u32[]{:S(2)}) collective-permute-start(s32[2,128,128]{2,1,0:T(8,128)S(1)} %copy-done.1), channel_id=1, source_target_pairs={{0,4},{4,0},{8,12},{12,8},{1,5},{5,1},{9,13},{13,9},{2,6},{6,2},{1... | collective-permute-start | bytes 393224 | tf_op jit(solution)/shard_map/ppermute | solution.py:521
  27.1 11.6 %collective-permute-start.14 = (s32[2,128,128]{2,1,0:T(8,128)S(1)}, s32[2,128,128]{2,1,0:T(8,128)S(1)}, u32[]{:S(2)}, u32[]{:S(2)}) collective-permute-start(s32[2,128,128]{2,1,0:T(8,128)S(1)} %copy-done.1), channel_id=1, source_target_pairs={{0,12},{4,8},{8,4},{12,0},{1,13},{5,9},{9,5},{13,1},{2,14},{6,10},... | collective-permute-start | bytes 393224 | tf_op jit(solution)/shard_map/ppermute | solution.py:522
  38.7 1.6 %collective-permute-start.15 = (f32[2,256,128]{2,1,0:T(8,128)S(1)}, f32[2,256,128]{2,1,0:T(8,128)S(1)}, u32[]{:S(2)}, u32[]{:S(2)}) collective-permute-start(f32[2,256,128]{2,1,0:T(8,128)S(1)} %get-tuple-element.38), channel_id=1, source_target_pairs={{0,1},{1,0},{2,3},{3,2},{4,5},{5,4},{6,7},{7,6},{8,9},{9,8},{10,11... | collective-permute-start | bytes 786440 | tf_op jit(solution)/shard_map/ppermute | solution.py:61

commit v6 on v5

--- a/solution.py
+++ b/solution.py
@@ -141,30 +141,36 @@
     return copies
 
 
-def prepare_kernel(plan, count, hbm_taps, hbm_dtaps, hbm_phases, hbm_positions, *refs):
+def tap_rows(ny, line):
+    def padded(row):
+        line[...] = jnp.zeros(line.shape, jnp.float32)
+        line[0:1, :row.shape[1]] = row
+        return line[0:1, :]
+
+    def folded(row):
+        spread = padded(row)
+        return sum(spread[:, i:i + ny] for i in range(0, spread.shape[1], ny))
+
+    return padded, folded
+
+
+def keep(ref, matrix, place=()):
+    ref[(0, *place)], ref[(1, *place)] = halves(matrix)
+
+
+def prepare_kernel(plan, count, hbm_taps, hbm_phases, hbm_positions, *refs):
     joined, refs = refs[:count], refs[count:]
-    ky, kz, km, by, bz, table, sheet, together, taps, dtaps, phases, positions, line, sems = refs
+    ky, kz, km, table, sheet, together, taps, phases, positions, line, sems = refs
     ny, half, block = plan.ny, plan.half, plan.block
     wide = 2 * block
-    count = taps.shape[2]
-    pairs = [(hbm_taps, taps), (hbm_dtaps, dtaps), (hbm_phases, phases), (hbm_positions, positions)]
+    pairs = [(hbm_taps, taps), (hbm_phases, phases), (hbm_positions, positions)]
     copies = fetch(pairs, sems)
     for number, piece in enumerate(joined):
         together[number * plan.planes:(number + 1) * plan.planes] = piece[...]
     for copy in copies:
         copy.wait()
 
-    def padded(row):
-        line[...] = jnp.zeros(line.shape, jnp.float32)
-        line[0:1, :count] = row
-        return line[0:1, :]
-
-    def folded(row):
-        spread = padded(row)
-        return sum(spread[:, i:i + ny] for i in range(0, spread.shape[1], ny))
-
-    def keep(ref, matrix, place=()):
-        ref[(0, *place)], ref[(1, *place)] = halves(matrix)
+    padded, folded = tap_rows(ny, line)
 
     cyr = circulant(folded(taps[0, 0:1, :]), ny, half)
     cyi = circulant(folded(taps[0, 1:2, :]), ny, half)
@@ -188,8 +194,6 @@
         km[number] = jnp.concatenate(
             [jnp.concatenate([high, high], axis=1), jnp.concatenate([low, low], axis=1)], axis=0
         )
-    keep(by, circulant(folded(dtaps[0:1, :]), ny, half))
-    keep(bz, band(padded(dtaps[1:2, :])[:, :wide], block, wide))
 
     number = phases.shape[1]
     for part, row in enumerate((jnp.cos(phases[...]), jnp.sin(phases[...]))):
@@ -379,10 +383,14 @@
         step(k, 2 * own - 1 - k)
 
 
-def weight_kernel(plan, hbm_bright, hbm_labels, facing, beyond, weight, bright, labels, sems):
+def weight_kernel(plan, hbm_bright, hbm_labels, hbm_dtaps, facing, beyond, weight, by, bz, bright, labels, dtaps, line, sems):
     half, ny, cz = plan.half, plan.ny, plan.cz
-    first, arriving = fetch([(hbm_bright, bright), (hbm_labels, labels)], sems)
+    first, taps, arriving = fetch([(hbm_bright, bright), (hbm_dtaps, dtaps), (hbm_labels, labels)], sems)
     first.wait()
+    taps.wait()
+    padded, folded = tap_rows(ny, line)
+    keep(by, circulant(folded(dtaps[0:1, :]), ny, half))
+    keep(bz, band(padded(dtaps[1:2, :])[:, :2 * plan.block], plan.block, 2 * plan.block))
     tile = lax.axis_index("tile")
     even = lax.rem(tile, 2) == 0
     first_half = lax.broadcasted_iota(jnp.int32, (ny, 2 * half), 1) < half
@@ -469,28 +477,25 @@
     far_groups = (sources[:1], sources[1:-1], sources[-1:])
     line = -(-max(4 * half, taps) // ny) * ny
     phases = phase_table[None]
-    ky, kz, km, by, bz, table, sheet, together = call(
+    ky, kz, km, table, sheet, together = call(
         functools.partial(prepare_kernel, plan, len(joined)),
         (
             shape((2, 2 * ny, 2 * ny), bf16),
             shape((2, 2, 2 * block, 2 * block), bf16),
             shape((2, 2 * block, 2 * block), bf16),
-            shape((2, ny, ny), bf16),
-            shape((2, block, 2 * block), bf16),
             shape((2 * phases.shape[1], ny), f32),
             shape((1, plan.width), f32),
             shape((len(joined) * plan.planes, ny, plan.cz), classes.dtype),
         ),
-        [HBM] * 4 + [VMEM] * len(joined),
+        [HBM] * 3 + [VMEM] * len(joined),
         [
             pltpu.VMEM(prop_taps.shape, f32),
-            pltpu.VMEM(detect_taps.shape, f32),
             pltpu.VMEM(phases.shape, f32),
             pltpu.SMEM(positions.shape, positions.dtype),
             pltpu.VMEM((8, line), f32),
-            pltpu.SemaphoreType.DMA((4,)),
+            pltpu.SemaphoreType.DMA((3,)),
         ],
-    )(prop_taps, detect_taps, phases, positions, *joined)
+    )(prop_taps, phases, positions, *joined)
     near = sum(near, [])
     crossed += [swap(together, "sect", cores), swap(pieces[-1], "sect", cores)]
 
@@ -540,16 +545,22 @@
         arrived = swap(after(leaving, facing, beyond), "sect", bits)
         other = arrived if other is None else other + arrived
     other = jnp.zeros_like(mine) if other is None else other
-    weight = call(
+    weight, by, bz = call(
         functools.partial(weight_kernel, plan),
-        shape((plan.planes, plan.extent, ny), f32),
-        [HBM] * 2 + [VMEM] * 2,
+        (
+            shape((plan.planes, plan.extent, ny), f32),
+            shape((2, ny, ny), bf16),
+            shape((2, block, 2 * block), bf16),
+        ),
+        [HBM] * 3 + [VMEM] * 2,
         [
             pltpu.SMEM(brightness.shape, f32),
             pltpu.VMEM(labels.shape, labels.dtype),
-            pltpu.SemaphoreType.DMA((2,)),
+            pltpu.VMEM(detect_taps.shape, f32),
+            pltpu.VMEM((8, line), f32),
+            pltpu.SemaphoreType.DMA((3,)),
         ],
-    )(brightness, labels, facing, beyond)
+    )(brightness, labels, detect_taps, facing, beyond)
     return call(
         functools.partial(blur_kernel, plan),
         shape((plan.planes, ny, plan.cz), f32),

time: 41.7 us -> 41.7 us (level)
  transfers between devices with their start and end apart: 16 -> 16, of which waited for: 4 -> 3; matrix products, arithmetic and copies ran while one was open for 0% -> 0% of each run, Pallas kernels for 46% -> 46%
where the time goes in v6:
time: 41.7 us; the launch traced here: 41.6 us
  Pallas kernels  20.4 us (49%)
  starting transfers between devices  15.5 us (37%)
  waiting for transfers between devices  5.54 us (13%)
    pallas_call x5, Pallas kernels, call_with(): pl.pallas_call(kernel, out_shape=outs, in_specs=[pl.BlockSpec(memory_spac...  20.4 us
    ppermute x14, starting transfers between devices, swap(): return lax.ppermute(x, axis, [(i, i ^ bits) for i in range(count)])  12.5 us
    ppermute x14, waiting for transfers between devices, swap(): return lax.ppermute(x, axis, [(i, i ^ bits) for i in range(count)])  5.53 us
    ppermute x1, starting transfers between devices, on_device(): facing = lax.ppermute(late, 'tile', pairs)  1.67 us
    ppermute x1, starting transfers between devices, on_device(): beyond = lax.ppermute(late, 'tile', gaps)  1.33 us
  transfers between devices with their start and end apart: 16, of which 3 were waited for; matrix products, arithmetic and copies ran while one was open for 0% of the time, Pallas kernels for 46%

profile of v6, /device:TPU:0, one launch (start us, length us, event | category | flops | bytes accessed | tf_op | source)
XLA Modules:
  0.0 41.6 jit_solution(2385973244126814411)
XLA Ops:
  0.0 5.0 %collective-permute-start = (s32[2,128,128]{2,1,0:T(8,128)}, s32[2,128,128]{2,1,0:T(8,128)S(1)}, u32[]{:S(2)}, u32[]{:S(2)}) collective-permute-start(s32[2,128,128]{2,1,0:T(8,128)} %mine.1), channel_id=1, source_target_pairs={{0,12},{4,8},{8,4},{12,0},{1,13},{5,9},{9,5},{13,1},{2,14},{6,10},... | collective-permute-start | bytes 393224 | tf_op jit(solution)/shard_map/ppermute | solution.py:61
  5.1 1.5 %collective-permute-start.5 = (s32[2,128,128]{2,1,0:T(8,128)}, s32[2,128,128]{2,1,0:T(8,128)S(1)}, u32[]{:S(2)}, u32[]{:S(2)}) collective-permute-start(s32[2,128,128]{2,1,0:T(8,128)} %mine.1), channel_id=1, source_target_pairs={{0,2},{1,3},{2,0},{3,1},{4,6},{5,7},{6,4},{7,5},{8,10},{9,11},{10,... | collective-permute-start | bytes 393224 | tf_op jit(solution)/shard_map/ppermute | solution.py:61
  6.5 3.1 %collective-permute-done.refs_0_.refs_1_ = s32[2,128,128]{2,1,0:T(8,128)S(1)} collective-permute-done((s32[2,128,128]{2,1,0:T(8,128)}, s32[2,128,128]{2,1,0:T(8,128)S(1)}, u32[]{:S(2)}, u32[]{:S(2)}) %collective-permute-start) | collective-permute-done | bytes 131104 | tf_op jit(solution)/shard_map/ppermute | solution.py:61
  9.6 2.0 %collective-permute-done.2.refs_1_.refs_3_ = s32[2,128,128]{2,1,0:T(8,128)S(1)} collective-permute-done((s32[2,128,128]{2,1,0:T(8,128)}, s32[2,128,128]{2,1,0:T(8,128)S(1)}, u32[]{:S(2)}, u32[]{:S(2)}) %collective-permute-start.2) | collective-permute-done | bytes 131104 | tf_op jit(solution)/shard_map/ppermute | solution.py:61
  11.7 1.7 %collective-permute-start.6 = (s32[2,128,128]{2,1,0:T(8,128)S(1)}, s32[2,128,128]{2,1,0:T(8,128)S(1)}, u32[]{:S(2)}, u32[]{:S(2)}) collective-permute-start(s32[2,128,128]{2,1,0:T(8,128)S(1)} %collective-permute-done.refs_0_.refs_1_), channel_id=1, source_target_pairs={{0,4},{4,0},{8,12},{12,8},{1,5},{5,1},{9,13},{13,9},{2,6},{6,2},{1... | collective-permute-start | bytes 393224 | tf_op jit(solution)/shard_map/ppermute | solution.py:61
  13.4 0.0 collective-permute-done.1.refs_2_
  13.4 1.4 %shard_map.73 = (bf16[2,256,256]{2,1,0:T(8,128)(2,1)S(1)}, bf16[2,2,256,256]{3,2,1,0:T(8,128)(2,1)S(1)}, bf16[2,256,256]{2,1,0:T(8,128)(2,1)S(1)}, f32[16,128]{1...) custom-call(f32[2,2,129]{2,1,0:T(2,128)} %hbm_taps.1, f32[1,8]{1,0:T(1,128)} %bitcast.7, ...), custom_call_target="tpu_custom_call" | custom-call | bytes 1048576 | tf_op jit(solution)/shard_map/pallas_call | solution.py:449
  14.7 1.6 %collective-permute-start.9 = (s32[4,128,128]{2,1,0:T(8,128)S(1)}, s32[4,128,128]{2,1,0:T(8,128)S(1)}, u32[]{:S(2)}, u32[]{:S(2)}) collective-permute-start(s32[4,128,128]{2,1,0:T(8,128)S(1)} %get-tuple-element.35), channel_id=1, source_target_pairs={{0,2},{1,3},{2,0},{3,1},{4,6},{5,7},{6,4},{7,5},{8,10},{9,11},{10,... | collective-permute-start | bytes 786440 | tf_op jit(solution)/shard_map/ppermute | solution.py:61
  16.3 0.0 collective-permute-start.3
  16.3 0.5 %collective-permute-start.4 = (s32[2,128,128]{2,1,0:T(8,128)S(1)}, s32[2,128,128]{2,1,0:T(8,128)S(1)}, u32[]{:S(2)}, u32[]{:S(2)}) collective-permute-start(s32[2,128,128]{2,1,0:T(8,128)S(1)} %collective-permute-done.2.refs_1_.refs_3_), channel_id=1, source_target_pairs={{0,1},{1,0},{2,3},{3,2},{4,5},{5,4},{6,7},{7,6},{8,9},{9,8},{10,11... | collective-permute-start | bytes 393224 | tf_op jit(solution)/shard_map/ppermute | solution.py:61
  16.8 0.0 collective-permute-start.7
  16.8 1.3 %collective-permute-start.11 = (s32[2,128,128]{2,1,0:T(8,128)S(1)}, s32[2,128,128]{2,1,0:T(8,128)S(1)}, u32[]{:S(2)}, u32[]{:S(2)}) collective-permute-start(s32[2,128,128]{2,1,0:T(8,128)S(1)} %collective-permute-done.6.refs_5_), channel_id=1, source_target_pairs={{0,2},{1,3},{2,0},{3,1},{4,6},{5,7},{6,4},{7,5},{8,10},{9,11},{10,... | collective-permute-start | bytes 393224 | tf_op jit(solution)/shard_map/ppermute | solution.py:61
  18.2 0.0 copy-start.1
  18.2 6.5 %shard_map.74 = (f32[4,256,128]{2,1,0:T(8,128)S(1)}, f32[4,512,128]{2,1,0:T(8,128)}, f32[4,512,128]{2,1,0:T(8,128)}) custom-call(s32[2,128,128]{2,1,0:T(8,128)S(1)} %copy-done, bf16[2,256,256]{2,1,0:T(8,128)(2,1)S(1)} %get-tuple-element.25.ky, bf16[2,2,256,256]{3,2,1,0:T(8,128)(2,1)S(1)} %get-tuple-element.26.kz, ...), custom_call_target="tpu_custom_call" | custom-call | flops 1 | bytes 1048576 | tf_op jit(solution)/shard_map/pallas_call | solution.py:449
  24.7 0.3 collective-permute-start.10
  25.0 0.3 collective-permute-start.8
  25.2 0.2 collective-permute-start.12
  25.5 1.7 %collective-permute-start.13 = (s32[2,128,128]{2,1,0:T(8,128)S(1)}, s32[2,128,128]{2,1,0:T(8,128)S(1)}, u32[]{:S(2)}, u32[]{:S(2)}) collective-permute-start(s32[2,128,128]{2,1,0:T(8,128)S(1)} %copy-done.1), channel_id=1, source_target_pairs={{0,4},{4,0},{8,12},{12,8},{1,5},{5,1},{9,13},{13,9},{2,6},{6,2},{1... | collective-permute-start | bytes 393224 | tf_op jit(solution)/shard_map/ppermute | solution.py:526
  27.1 1.3 %collective-permute-start.14 = (s32[2,128,128]{2,1,0:T(8,128)S(1)}, s32[2,128,128]{2,1,0:T(8,128)S(1)}, u32[]{:S(2)}, u32[]{:S(2)}) collective-permute-start(s32[2,128,128]{2,1,0:T(8,128)S(1)} %copy-done.1), channel_id=1, source_target_pairs={{0,12},{4,8},{8,4},{12,0},{1,13},{5,9},{9,5},{13,1},{2,14},{6,10},... | collective-permute-start | bytes 393224 | tf_op jit(solution)/shard_map/ppermute | solution.py:527
  28.5 10.2 %shard_map.75 = f32[4,256,128]{2,1,0:T(8,128)S(1)} custom-call(bf16[2,256,256]{2,1,0:T(8,128)(2,1)S(1)} %get-tuple-element.25.ky, bf16[2,2,256,256]{3,2,1,0:T(8,128)(2,1)S(1)} %get-tuple-element.26.kz, bf16[2,256,256]{2,1,0:T(8,128)(2,1)S(1)} %get-tuple-element.27.km, f32[16,128]{1,0:T(8,128)S(1)} %get-tuple-element.28.table, ...), custom_call_target="tpu_custom_call" | custom-call | flops 6000000000 | bytes 1048576 | tf_op jit(solution)/shard_map/pallas_call | solution.py:449
  38.7 0.1 collective-permute-start.15
  38.8 1.1 %shard_map.76 = (f32[2,256,128]{2,1,0:T(8,128)S(1)}, bf16[2,128,128]{2,1,0:T(8,128)(2,1)S(1)}, bf16[2,128,256]{2,1,0:T(8,128)(2,1)S(1)}) custom-call(f32[16]{0:T(128)} %hbm_bright.1, s32[2,128,128]{2,1,0:T(8,128)} %hbm_labels.1, f32[2,129]{1,0:T(2,128)} %hbm_dtaps.1, s32[2,128,128]{2,1,0:T(8,128)S(1)} %collective-permute-done.13.facing, ...), custom_call_target="tpu_custom_call" | custom-call | bytes 1048576 | tf_op jit(solution)/shard_map/pallas_call | solution.py:449
  39.9 0.4 collective-permute-done.15.other
  40.3 1.2 %shard_map.77 = f32[2,128,128]{2,1,0:T(8,128)} custom-call(f32[2,256,128]{2,1,0:T(8,128)S(1)} %get-tuple-element.44.mine, f32[2,256,128]{2,1,0:T(8,128)S(1)} %collective-permute-done.15.other, f32[2,256,128]{2,1,0:T(8,128)S(1)} %get-tuple-element.40.weight, bf16[2,128,128]{2,1,0:T(8,128)(2,1)S(1)} %get-tuple-element.41.by, ...), custom_call_target="tpu_custom_call" | custom-call | bytes 1048576 | tf_op jit(solution)/shard_map/pallas_call | solution.py:449
  (18 shorter events, 0.1 us)
Async XLA Ops:
  0.0 9.6 %collective-permute-start = (s32[2,128,128]{2,1,0:T(8,128)}, s32[2,128,128]{2,1,0:T(8,128)S(1)}, u32[]{:S(2)}, u32[]{:S(2)}) collective-permute-start(s32[2,128,128]{2,1,0:T(8,128)} %mine.1), channel_id=1, source_target_pairs={{0,12},{4,8},{8,4},{12,0},{1,13},{5,9},{9,5},{13,1},{2,14},{6,10},... | collective-permute-start | bytes 393224 | tf_op jit(solution)/shard_map/ppermute | solution.py:61
  5.0 6.6 %collective-permute-start.2 = (s32[2,128,128]{2,1,0:T(8,128)}, s32[2,128,128]{2,1,0:T(8,128)S(1)}, u32[]{:S(2)}, u32[]{:S(2)}) collective-permute-start(s32[2,128,128]{2,1,0:T(8,128)} %mine.1), channel_id=1, source_target_pairs={{0,4},{4,0},{8,12},{12,8},{1,5},{5,1},{9,13},{13,9},{2,6},{6,2},{1... | collective-permute-start | bytes 393224 | tf_op jit(solution)/shard_map/ppermute | solution.py:61
  5.1 6.6 %collective-permute-start.5 = (s32[2,128,128]{2,1,0:T(8,128)}, s32[2,128,128]{2,1,0:T(8,128)S(1)}, u32[]{:S(2)}, u32[]{:S(2)}) collective-permute-start(s32[2,128,128]{2,1,0:T(8,128)} %mine.1), channel_id=1, source_target_pairs={{0,2},{1,3},{2,0},{3,1},{4,6},{5,7},{6,4},{7,5},{8,10},{9,11},{10,... | collective-permute-start | bytes 393224 | tf_op jit(solution)/shard_map/ppermute | solution.py:61
  9.6 3.7 %collective-permute-start.1 = (s32[2,128,128]{2,1,0:T(8,128)S(1)}, s32[2,128,128]{2,1,0:T(8,128)S(1)}, u32[]{:S(2)}, u32[]{:S(2)}) collective-permute-start(s32[2,128,128]{2,1,0:T(8,128)S(1)} %collective-permute-done.refs_0_.refs_1_), channel_id=1, source_target_pairs={{0,1},{1,0},{2,3},{3,2},{4,5},{5,4},{6,7},{7,6},{8,9},{9,8},{10,11... | collective-permute-start | bytes 393224 | tf_op jit(solution)/shard_map/ppermute | solution.py:61
  11.7 5.1 %collective-permute-start.6 = (s32[2,128,128]{2,1,0:T(8,128)S(1)}, s32[2,128,128]{2,1,0:T(8,128)S(1)}, u32[]{:S(2)}, u32[]{:S(2)}) collective-permute-start(s32[2,128,128]{2,1,0:T(8,128)S(1)} %collective-permute-done.refs_0_.refs_1_), channel_id=1, source_target_pairs={{0,4},{4,0},{8,12},{12,8},{1,5},{5,1},{9,13},{13,9},{2,6},{6,2},{1... | collective-permute-start | bytes 393224 | tf_op jit(solution)/shard_map/ppermute | solution.py:61
  13.4 2.9 %copy-start = (s32[2,128,128]{2,1,0:T(8,128)S(1)}, s32[2,128,128]{2,1,0:T(8,128)}, u32[]{:S(2)}) copy-start(s32[2,128,128]{2,1,0:T(8,128)} %mine.1) | copy-start | bytes 393220
  14.7 9.9 %collective-permute-start.9 = (s32[4,128,128]{2,1,0:T(8,128)S(1)}, s32[4,128,128]{2,1,0:T(8,128)S(1)}, u32[]{:S(2)}, u32[]{:S(2)}) collective-permute-start(s32[4,128,128]{2,1,0:T(8,128)S(1)} %get-tuple-element.35), channel_id=1, source_target_pairs={{0,2},{1,3},{2,0},{3,1},{4,6},{5,7},{6,4},{7,5},{8,10},{9,11},{10,... | collective-permute-start | bytes 786440 | tf_op jit(solution)/shard_map/ppermute | solution.py:61
  16.3 1.9 %collective-permute-start.3 = (s32[2,128,128]{2,1,0:T(8,128)S(1)}, s32[2,128,128]{2,1,0:T(8,128)S(1)}, u32[]{:S(2)}, u32[]{:S(2)}) collective-permute-start(s32[2,128,128]{2,1,0:T(8,128)S(1)} %copy-done), channel_id=1, source_target_pairs={{0,1},{1,0},{2,3},{3,2},{4,5},{5,4},{6,7},{7,6},{8,9},{9,8},{10,11... | collective-permute-start | bytes 393224 | tf_op jit(solution)/shard_map/ppermute | solution.py:61
  16.3 1.9 %collective-permute-start.4 = (s32[2,128,128]{2,1,0:T(8,128)S(1)}, s32[2,128,128]{2,1,0:T(8,128)S(1)}, u32[]{:S(2)}, u32[]{:S(2)}) collective-permute-start(s32[2,128,128]{2,1,0:T(8,128)S(1)} %collective-permute-done.2.refs_1_.refs_3_), channel_id=1, source_target_pairs={{0,1},{1,0},{2,3},{3,2},{4,5},{5,4},{6,7},{7,6},{8,9},{9,8},{10,11... | collective-permute-start | bytes 393224 | tf_op jit(solution)/shard_map/ppermute | solution.py:61
  16.8 1.4 %collective-permute-start.7 = (s32[2,128,128]{2,1,0:T(8,128)S(1)}, s32[2,128,128]{2,1,0:T(8,128)S(1)}, u32[]{:S(2)}, u32[]{:S(2)}) collective-permute-start(s32[2,128,128]{2,1,0:T(8,128)S(1)} %collective-permute-done.6.refs_5_), channel_id=1, source_target_pairs={{0,1},{1,0},{2,3},{3,2},{4,5},{5,4},{6,7},{7,6},{8,9},{9,8},{10,11... | collective-permute-start | bytes 393224 | tf_op jit(solution)/shard_map/ppermute | solution.py:61
  16.8 8.4 %collective-permute-start.11 = (s32[2,128,128]{2,1,0:T(8,128)S(1)}, s32[2,128,128]{2,1,0:T(8,128)S(1)}, u32[]{:S(2)}, u32[]{:S(2)}) collective-permute-start(s32[2,128,128]{2,1,0:T(8,128)S(1)} %collective-permute-done.6.refs_5_), channel_id=1, source_target_pairs={{0,2},{1,3},{2,0},{3,1},{4,6},{5,7},{6,4},{7,5},{8,10},{9,11},{10,... | collective-permute-start | bytes 393224 | tf_op jit(solution)/shard_map/ppermute | solution.py:61
  18.2 7.3 %copy-start.1 = (s32[2,128,128]{2,1,0:T(8,128)S(1)}, s32[2,128,128]{2,1,0:T(8,128)}, u32[]{:S(2)}) copy-start(s32[2,128,128]{2,1,0:T(8,128)} %hbm_labels.1) | copy-start | bytes 393220
  24.7 3.8 %collective-permute-start.10 = (s32[4,128,128]{2,1,0:T(8,128)S(1)}, s32[4,128,128]{2,1,0:T(8,128)S(1)}, u32[]{:S(2)}, u32[]{:S(2)}) collective-permute-start(s32[4,128,128]{2,1,0:T(8,128)S(1)} %collective-permute-done.9.refs_2_), channel_id=1, source_target_pairs={{0,1},{1,0},{2,3},{3,2},{4,5},{5,4},{6,7},{7,6},{8,9},{9,8},{10,11... | collective-permute-start | bytes 786440 | tf_op jit(solution)/shard_map/ppermute | solution.py:61
  25.0 3.5 %collective-permute-start.8 = (s32[2,128,128]{2,1,0:T(8,128)S(1)}, s32[2,128,128]{2,1,0:T(8,128)S(1)}, u32[]{:S(2)}, u32[]{:S(2)}) collective-permute-start(s32[2,128,128]{2,1,0:T(8,128)S(1)} %collective-permute-done.5.refs_0_), channel_id=1, source_target_pairs={{0,1},{1,0},{2,3},{3,2},{4,5},{5,4},{6,7},{7,6},{8,9},{9,8},{10,11... | collective-permute-start | bytes 393224 | tf_op jit(solution)/shard_map/ppermute | solution.py:61
  25.2 3.2 %collective-permute-start.12 = (s32[2,128,128]{2,1,0:T(8,128)S(1)}, s32[2,128,128]{2,1,0:T(8,128)S(1)}, u32[]{:S(2)}, u32[]{:S(2)}) collective-permute-start(s32[2,128,128]{2,1,0:T(8,128)S(1)} %collective-permute-done.11.refs_4_), channel_id=1, source_target_pairs={{0,1},{1,0},{2,3},{3,2},{4,5},{5,4},{6,7},{7,6},{8,9},{9,8},{10,11... | collective-permute-start | bytes 393224 | tf_op jit(solution)/shard_map/ppermute | solution.py:61
  25.5 13.2 %collective-permute-start.13 = (s32[2,128,128]{2,1,0:T(8,128)S(1)}, s32[2,128,128]{2,1,0:T(8,128)S(1)}, u32[]{:S(2)}, u32[]{:S(2)}) collective-permute-start(s32[2,128,128]{2,1,0:T(8,128)S(1)} %copy-done.1), channel_id=1, source_target_pairs={{0,4},{4,0},{8,12},{12,8},{1,5},{5,1},{9,13},{13,9},{2,6},{6,2},{1... | collective-permute-start | bytes 393224 | tf_op jit(solution)/shard_map/ppermute | solution.py:526
  27.1 11.6 %collective-permute-start.14 = (s32[2,128,128]{2,1,0:T(8,128)S(1)}, s32[2,128,128]{2,1,0:T(8,128)S(1)}, u32[]{:S(2)}, u32[]{:S(2)}) collective-permute-start(s32[2,128,128]{2,1,0:T(8,128)S(1)} %copy-done.1), channel_id=1, source_target_pairs={{0,12},{4,8},{8,4},{12,0},{1,13},{5,9},{9,5},{13,1},{2,14},{6,10},... | collective-permute-start | bytes 393224 | tf_op jit(solution)/shard_map/ppermute | solution.py:527
  38.7 1.6 %collective-permute-start.15 = (f32[2,256,128]{2,1,0:T(8,128)S(1)}, f32[2,256,128]{2,1,0:T(8,128)S(1)}, u32[]{:S(2)}, u32[]{:S(2)}) collective-permute-start(f32[2,256,128]{2,1,0:T(8,128)S(1)} %get-tuple-element.39), channel_id=1, source_target_pairs={{0,1},{1,0},{2,3},{3,2},{4,5},{5,4},{6,7},{7,6},{8,9},{9,8},{10,11... | collective-permute-start | bytes 786440 | tf_op jit(solution)/shard_map/ppermute | solution.py:61
